TPU v7x, 128 devices: a whole 4x4x4 slice. The times are simulated.
128 devices in a mesh: leaf: 32 (over y, z, core), panel: 4 (over x).
Axes of the slice: x: 4, y: 4, z: 4, core: 2. Of those that a mesh axis runs over, the one named last changes fastest.
Arguments:
- noise_parts: float32 [131072, 128], P(('leaf', 'panel')), may hold values from -6 to 6
- elimination_row: int32 [131072], P(('leaf', 'panel')), may hold values from 0 to 131071, as said below
- leaf_noise: float32 [524288, 128], P(('leaf', 'panel')), may hold values from -6 to 6
- diag_inverse: float32 [5120, 128, 128], P(('leaf', 'panel')), as said below
- panels: bfloat16 [71680, 128, 128], P(('leaf', 'panel')), may hold values from -0.125 to 0.125
- panel_from: int32 [71680], P(('leaf', 'panel')), may hold values from 0 to 127, as said below
- send_lists: int32 [128, 240], P(('leaf', 'panel')), may hold values from 0 to 1
Outputs:
- sep_solution: float32 [131072, 128], P(('leaf', 'panel'))
- leaf_solution: float32 [524288, 128], P(('leaf', 'panel'))
Inputs may be any that keep to these rules, and one draw needn't show every extreme that they name: `elimination_row`: A permutation of the separator rows in which every device hands exactly 8 rows to every device. `panel_from`: the block of ancestor level l names only positions below 128 / 2^l, and every one of them at least once. `diag_inverse`: each tile is upper triangular with diagonal entries between 0.6 and 1.4.
All inputs are finite; a program needn't handle non-finite values.
Results may differ from a plain program's by a relative error of at most 0.0029.
Values may be sent and summed in bfloat16 or wider, within the bound.
No kernel may reach another device: no remote copies, remote signals or barrier semaphores. Data moves between devices by JAX's collectives and lax.ppermute only.
A program may use at most 128 MiB of HBM per device.

v0:
```python
import jax
import jax.numpy as jnp
from jax import lax
from jax.sharding import PartitionSpec as P

BS = 128
TS = 2
TL = 32
KP = 4
LEVELS = 4


def partner(x, axis, apart):
    return lax.ppermute(x, axis, [(i, i ^ 1 << apart) for i in range(lax.axis_size(axis))])


def per_device(
    noise_parts, elimination_row, leaf_noise, diag_inverse, panels, panel_from, send_lists
):
    highest = lax.Precision.HIGHEST
    owners = lax.axis_size(("leaf", "panel"))
    my_index = lax.axis_index(("leaf", "panel"))
    sep_rows = noise_parts.shape[0]
    rhs_width = noise_parts.shape[1]
    per_owner = sep_rows // owners
    owner_of = elimination_row // sep_rows
    local_slot = elimination_row % sep_rows
    ranking = jnp.argsort(owner_of, stable=True)
    outgoing = noise_parts[ranking].reshape(owners, per_owner, rhs_width)
    places = local_slot[ranking].reshape(owners, per_owner)
    arrived, arrived_at = (
        lax.all_to_all(outgoing, ("leaf", "panel"), split_axis=0, concat_axis=0, tiled=True),
        lax.all_to_all(places, ("leaf", "panel"), split_axis=0, concat_axis=0, tiled=True),
    )
    sep_noise = (
        jnp.zeros_like(noise_parts)
        .at[arrived_at.reshape(-1)]
        .set(arrived.reshape(sep_rows, rhs_width))
    )
    sep_noise = sep_noise.reshape(LEVELS, TS, BS, rhs_width)
    send_row = send_lists[0]
    sep_update = [jnp.zeros((TS, BS, rhs_width), jnp.float32) for tree_level_index in range(LEVELS)]
    leaf_update = jnp.zeros((TL, BS, rhs_width), jnp.float32)
    solved = []
    offset = 0
    send_offset = 0
    for tree_level_index in range(LEVELS):
        right_side = sep_noise[tree_level_index] - sep_update[tree_level_index]
        solution = jnp.einsum(
            "tij,tjr->tir",
            diag_inverse[tree_level_index * TS : (tree_level_index + 1) * TS],
            right_side,
            precision=highest,
            preferred_element_type=jnp.float32,
        )
        solved.append(solution)
        sent_tiles = solution.astype(jnp.bfloat16)
        group = owners >> tree_level_index
        my_rel = my_index % group
        members = jnp.arange(group, dtype=jnp.int32)
        buffer = sent_tiles[send_row[send_offset + jnp.bitwise_xor(members, my_rel)]]
        for bit in range(group.bit_length() - 1):
            shaped = buffer.reshape(group >> bit + 1, 2, 1 << bit, BS, rhs_width)
            arriving = partner(shaped[:, 1], ("leaf", "panel"), bit)
            buffer = jnp.stack([shaped[:, 0], arriving], axis=1).reshape(group, BS, rhs_width)
        received = buffer[jnp.bitwise_xor(members, my_rel)]
        send_offset += group
        desc_tiles = (LEVELS - 1 - tree_level_index) * TS + TL
        entries = KP * desc_tiles
        needed = received[panel_from[offset : offset + entries]]
        products = jnp.einsum(
            "eij,ejr->eir",
            panels[offset : offset + entries],
            needed,
            preferred_element_type=jnp.float32,
        )
        update = products.reshape(desc_tiles, KP, BS, rhs_width).sum(axis=1)
        offset += entries
        for deeper in range(tree_level_index + 1, LEVELS):
            start = (deeper - tree_level_index - 1) * TS
            sep_update[deeper] = sep_update[deeper] + update[start : start + TS]
        leaf_update = leaf_update + update[(LEVELS - 1 - tree_level_index) * TS :]
    leaf_right = leaf_noise.reshape(TL, BS, rhs_width) - leaf_update
    leaf_solved = jnp.einsum(
        "tij,tjr->tir",
        diag_inverse[LEVELS * TS :],
        leaf_right,
        precision=highest,
        preferred_element_type=jnp.float32,
    )
    sep_solution = jnp.stack(solved, axis=0).reshape(sep_rows, rhs_width)
    return (sep_solution, leaf_solved.reshape(TL * BS, rhs_width))


def solution(mesh):
    return jax.shard_map(
        per_device,
        mesh=mesh,
        in_specs=(
            P(("leaf", "panel"), None),
            P(("leaf", "panel")),
            P(("leaf", "panel"), None),
            P(("leaf", "panel"), None, None),
            P(("leaf", "panel"), None, None),
            P(("leaf", "panel")),
            P(("leaf", "panel"), None),
        ),
        out_specs=(P(("leaf", "panel"), None), P(("leaf", "panel"), None)),
        check_vma=False,
    )
```

profile of v0, /device:TPU:1, one launch (start us, length us, event | category | flops | bytes accessed | tf_op | source)
XLA Modules:
  0.0 687.9 jit_solution(3803179433858362684)
XLA Ops:
  1.4 4.4 sort.17
  5.8 4.5 gather_fusion
  11.0 11.5 %all-to-all-start = ((s32[128,1,8]{2,1,0:T(1,128)}), s32[128,1,8]{2,1,0:T(1,128)S(1)}, u32[]{:S(2)}, u32[]{:S(2)}) async-start(s32[128,1,8]{2,1,0:T(1,128)} %bitcast), calls=%async_computation | async-start | bytes 131072 | tf_op jit(solution)/shard_map/all_to_all | solution.py:33
  22.6 4.0 gather_fusion.1
  27.9 4.4 all-to-all-done
  32.3 5.3 all-to-all-start.1
  39.1 12.7 %all-to-all-done.1 = f32[128,8,128]{2,1,0:T(8,128)S(1)} async-done(((f32[128,8,128]{2,1,0:T(8,128)}), f32[128,8,128]{2,1,0:T(8,128)S(1)}, u32[]{:S(2)}, u32[]{:S(2)}) %all-to-all-start.1) | async-done | bytes 524320 | tf_op jit(solution)/shard_map/all_to_all | solution.py:32
  51.8 3.2 scatter_custom_fusion
  55.1 1.8 bitcast_convert_fusion.3
  57.0 3.1 gather_fusion.3
  60.0 2.7 fusion.60
  63.1 46.7 %collective-permute-done = bf16[64,1,128,128]{3,2,0,1:T(8,128)(2,1)S(1)} collective-permute-done((bf16[64,1,128,128]{3,2,0,1:T(8,128)(2,1)S(1)}, bf16[64,1,128,128]{3,2,0,1:T(8,128)(2,1)S(1)}, u32[]{:S(2)}, u32[]{:S(2)}) %collective-permute-start) | collective-permute-done | bytes 2097184 | tf_op jit(solution)/shard_map/ppermute | solution.py:14
  110.4 47.5 %collective-permute-done.1 = bf16[32,2,128,128]{3,2,0,1:T(8,128)(2,1)S(1)} collective-permute-done((bf16[32,2,128,128]{3,2,0,1:T(8,128)(2,1)S(1)}, bf16[32,2,128,128]{3,2,0,1:T(8,128)(2,1)S(1)}, u32[]{:S(2)}, u32[]{:S(2)}) %collective-permute-start.1) | collective-permute-done | bytes 2097184 | tf_op jit(solution)/shard_map/ppermute | solution.py:14
  158.8 2.0 collective-permute-start.2
  160.9 3.8 collective-permute-done.2
  165.7 46.8 %collective-permute-done.3 = bf16[8,8,128,128]{3,2,0,1:T(8,128)(2,1)S(1)} collective-permute-done((bf16[8,8,128,128]{3,2,0,1:T(8,128)(2,1)S(1)}, bf16[8,8,128,128]{3,2,0,1:T(8,128)(2,1)S(1)}, u32[]{:S(2)}, u32[]{:S(2)}) %collective-permute-start.3) | collective-permute-done | bytes 2097184 | tf_op jit(solution)/shard_map/ppermute | solution.py:14
  213.6 47.3 %collective-permute-done.4 = bf16[4,16,128,128]{3,2,0,1:T(8,128)(2,1)S(1)} collective-permute-done((bf16[4,16,128,128]{3,2,0,1:T(8,128)(2,1)S(1)}, bf16[4,16,128,128]{3,2,0,1:T(8,128)(2,1)S(1)}, u32[]{:S(2)}, u32[]{:S(2)}) %collective-permute-start.4) | collective-permute-done | bytes 2097184 | tf_op jit(solution)/shard_map/ppermute | solution.py:14
  262.3 44.7 %collective-permute-done.5 = bf16[2,32,128,128]{3,2,0,1:T(8,128)(2,1)S(1)} collective-permute-done((bf16[2,32,128,128]{3,2,0,1:T(8,128)(2,1)S(1)}, bf16[2,32,128,128]{3,2,0,1:T(8,128)(2,1)S(1)}, u32[]{:S(2)}, u32[]{:S(2)}) %collective-permute-start.5) | collective-permute-done | bytes 2097184 | tf_op jit(solution)/shard_map/ppermute | solution.py:14
  307.4 1.6 slice_bitcast_fusion.1
  311.0 44.1 %collective-permute-done.6 = bf16[1,64,128,128]{3,2,1,0:T(8,128)(2,1)} collective-permute-done((bf16[1,64,128,128]{3,2,1,0:T(8,128)(2,1)}, bf16[1,64,128,128]{3,2,1,0:T(8,128)(2,1)}, u32[]{:S(2)}, u32[]{:S(2)}) %collective-permute-start.6) | collective-permute-done | bytes 2097184 | tf_op jit(solution)/shard_map/ppermute | solution.py:14
  355.1 3.9 pad_maximum_fusion.5
  359.0 5.3 gather_fusion.4
  364.3 9.9 %gather_fusion.5 = bf16[152,128,128]{2,1,0:T(8,128)(2,1)} fusion(bf16[128,128,128]{2,1,0:T(8,128)(2,1)} %gather_fusion.4, s32[1024]{0:T(1024)S(1)} %pad_clamp_fusion.12), kind=kCustom, calls=%fused_computation.5 | custom fusion | bytes 9962080 | tf_op jit(solution)/shard_map/gather | solution.py:70
  374.2 11.4 %fusion = f32[152,128,128]{2,1,0:T(8,128)} fusion(bf16[152,128,128]{2,1,0:T(8,128)(2,1)} %gather_fusion.5, bf16[560,128,128]{2,1,0:T(8,128)(2,1)} %param.11), kind=kOutput, calls=%fused_computation.20 | convolution fusion | flops 637534208 | bytes 19922944 | tf_op jit(solution)/shard_map/eij,ejr->eir/dot_general | solution.py:71
  385.5 5.3 reduce_sum.36
  390.8 2.1 bitcast_convert_fusion.2
  392.9 2.1 gather_fusion.7
  395.0 1.7 fusion.61
  397.1 20.4 %collective-permute-done.7 = bf16[32,1,128,128]{3,2,0,1:T(8,128)(2,1)S(1)} collective-permute-done((bf16[32,1,128,128]{3,2,0,1:T(8,128)(2,1)S(1)}, bf16[32,1,128,128]{3,2,0,1:T(8,128)(2,1)S(1)}, u32[]{:S(2)}, u32[]{:S(2)}) %collective-permute-start.7) | collective-permute-done | bytes 1048608 | tf_op jit(solution)/shard_map/ppermute | solution.py:14
  417.8 19.2 %collective-permute-done.8 = bf16[16,2,128,128]{3,2,0,1:T(8,128)(2,1)S(1)} collective-permute-done((bf16[16,2,128,128]{3,2,0,1:T(8,128)(2,1)S(1)}, bf16[16,2,128,128]{3,2,0,1:T(8,128)(2,1)S(1)}, u32[]{:S(2)}, u32[]{:S(2)}) %collective-permute-start.8) | collective-permute-done | bytes 1048608 | tf_op jit(solution)/shard_map/ppermute | solution.py:14
  437.4 7.9 %collective-permute-start.9 = (bf16[8,4,128,128]{3,2,0,1:T(8,128)(2,1)S(1)}, bf16[8,4,128,128]{3,2,0,1:T(8,128)(2,1)S(1)}, u32[]{:S(2)}, u32[]{:S(2)}) collective-permute-start(bf16[8,4,128,128]{3,2,0,1:T(8,128)(2,1)S(1)} %get-tuple-element.25), channel_id=1, source_target_pairs={{0,4},{1,5},{2,6},{3,7},{4,0},{5,1},{6,2},{7,3},{8,12},{9,13},{10,... | collective-permute-start | bytes 3145736 | tf_op jit(solution)/shard_map/ppermute | solution.py:14
  445.3 2.3 collective-permute-done.9
  448.0 1.8 collective-permute-start.10
  449.7 23.1 %collective-permute-done.10 = bf16[4,8,128,128]{3,2,0,1:T(8,128)(2,1)S(1)} collective-permute-done((bf16[4,8,128,128]{3,2,0,1:T(8,128)(2,1)S(1)}, bf16[4,8,128,128]{3,2,0,1:T(8,128)(2,1)S(1)}, u32[]{:S(2)}, u32[]{:S(2)}) %collective-permute-start.10) | collective-permute-done | bytes 1048608 | tf_op jit(solution)/shard_map/ppermute | solution.py:14
  474.3 24.3 %collective-permute-done.11 = bf16[2,16,128,128]{3,2,0,1:T(8,128)(2,1)} collective-permute-done((bf16[2,16,128,128]{3,2,0,1:T(8,128)(2,1)S(1)}, bf16[2,16,128,128]{3,2,0,1:T(8,128)(2,1)}, u32[]{:S(2)}, u32[]{:S(2)}) %collective-permute-start.11) | collective-permute-done | bytes 1048608 | tf_op jit(solution)/shard_map/ppermute | solution.py:14
  498.6 1.4 pad_maximum_fusion.10
  501.8 21.6 %collective-permute-done.12 = bf16[1,32,128,128]{3,2,1,0:T(8,128)(2,1)} collective-permute-done((bf16[1,32,128,128]{3,2,1,0:T(8,128)(2,1)S(1)}, bf16[1,32,128,128]{3,2,1,0:T(8,128)(2,1)}, u32[]{:S(2)}, u32[]{:S(2)}) %collective-permute-start.12) | collective-permute-done | bytes 1048608 | tf_op jit(solution)/shard_map/ppermute | solution.py:14
  523.4 2.7 pad_maximum_fusion.11
  526.1 2.5 gather_fusion.8
  528.6 7.6 %gather_fusion.9 = bf16[144,128,128]{2,1,0:T(8,128)(2,1)} fusion(bf16[64,128,128]{2,1,0:T(8,128)(2,1)S(1)} %gather_fusion.8, s32[1024]{0:T(1024)S(1)} %pad_clamp_fusion.8), kind=kCustom, calls=%fused_computation.9 | custom fusion | bytes 9437760 | tf_op jit(solution)/shard_map/gather | solution.py:70
  536.3 10.9 %fusion.2 = f32[144,128,128]{2,1,0:T(8,128)} fusion(bf16[144,128,128]{2,1,0:T(8,128)(2,1)} %gather_fusion.9, bf16[560,128,128]{2,1,0:T(8,128)(2,1)} %param.11), kind=kOutput, calls=%fused_computation.22 | convolution fusion | flops 603979776 | bytes 18874368 | tf_op jit(solution)/shard_map/eij,ejr->eir/dot_general | solution.py:71
  547.1 5.0 reduce_sum.37
  552.2 2.3 bitcast_convert_fusion.1
  554.5 1.6 gather_fusion.11
  557.9 10.3 %collective-permute-done.13 = bf16[16,1,128,128]{3,2,0,1:T(8,128)(2,1)S(1)} collective-permute-done((bf16[16,1,128,128]{3,2,0,1:T(8,128)(2,1)S(1)}, bf16[16,1,128,128]{3,2,0,1:T(8,128)(2,1)S(1)}, u32[]{:S(2)}, u32[]{:S(2)}) %collective-permute-start.13) | collective-permute-done | bytes 524320 | tf_op jit(solution)/shard_map/ppermute | solution.py:14
  569.5 10.2 %collective-permute-done.14 = bf16[8,2,128,128]{3,2,0,1:T(8,128)(2,1)S(1)} collective-permute-done((bf16[8,2,128,128]{3,2,0,1:T(8,128)(2,1)S(1)}, bf16[8,2,128,128]{3,2,0,1:T(8,128)(2,1)S(1)}, u32[]{:S(2)}, u32[]{:S(2)}) %collective-permute-start.14) | collective-permute-done | bytes 524320 | tf_op jit(solution)/shard_map/ppermute | solution.py:14
  579.9 4.6 collective-permute-start.15
  584.6 1.5 collective-permute-done.15
  588.5 11.0 %collective-permute-done.16 = bf16[2,8,128,128]{3,2,0,1:T(8,128)(2,1)S(1)} collective-permute-done((bf16[2,8,128,128]{3,2,0,1:T(8,128)(2,1)S(1)}, bf16[2,8,128,128]{3,2,0,1:T(8,128)(2,1)S(1)}, u32[]{:S(2)}, u32[]{:S(2)}) %collective-permute-start.16) | collective-permute-done | bytes 524320 | tf_op jit(solution)/shard_map/ppermute | solution.py:14
  599.7 1.6 collective-permute-start.17
  601.4 12.5 %collective-permute-done.17 = bf16[1,16,128,128]{3,2,1,0:T(8,128)(2,1)S(1)} collective-permute-done((bf16[1,16,128,128]{3,2,1,0:T(8,128)(2,1)S(1)}, bf16[1,16,128,128]{3,2,1,0:T(8,128)(2,1)S(1)}, u32[]{:S(2)}, u32[]{:S(2)}) %collective-permute-start.17) | collective-permute-done | bytes 524320 | tf_op jit(solution)/shard_map/ppermute | solution.py:14
  614.8 7.6 %gather_fusion.13 = bf16[136,128,128]{2,1,0:T(8,128)(2,1)} fusion(bf16[32,128,128]{2,1,0:T(8,128)(2,1)S(1)} %gather_fusion.12, s32[1024]{0:T(1024)S(1)} %pad_clamp_fusion.4), kind=kCustom, calls=%fused_computation.13 | custom fusion | bytes 8913440 | tf_op jit(solution)/shard_map/gather | solution.py:70
  622.3 10.4 %fusion.4 = f32[136,128,128]{2,1,0:T(8,128)} fusion(bf16[136,128,128]{2,1,0:T(8,128)(2,1)} %gather_fusion.13, bf16[560,128,128]{2,1,0:T(8,128)(2,1)} %param.11), kind=kOutput, calls=%fused_computation.24 | convolution fusion | flops 570425344 | bytes 17825792 | tf_op jit(solution)/shard_map/eij,ejr->eir/dot_general | solution.py:71
  632.7 6.2 reduce_sum.38
  638.9 2.1 bitcast_convert_fusion
  642.1 5.4 collective-permute-done.18
  648.7 5.6 collective-permute-done.19
  654.4 4.3 collective-permute-start.20
  660.7 1.6 collective-permute-start.21
  662.3 2.9 copy.105
  666.1 2.5 collective-permute-done.21
  670.2 3.1 gather_fusion.17
  673.3 6.8 bitcast_reduce_fusion
  680.1 7.6 %fusion.14 = f32[32,128,128]{1,2,0:T(8,128)} fusion(f32[32,128,128]{1,2,0:T(8,128)S(1)} %copy-done.8, f32[32,128,128]{1,2,0:T(8,128)S(1)} %bitcast_reduce_fusion, f32[34,128,128]{1,2,0:T(8,128)S(1)} %copy-done.7, f32[36,128,128]{1,2,0:T(8,128)S(1)} %copy-done.6, f32[38,128,128]{1,2,0:T(8,128)S(1)} %copy-done.4, f32[40,128,128]{2,1,0:T(8,128)} %param.10), kind=kOutput, calls=%fused_computation.41 | convolution fusion | flops 807403520 | bytes 14680064 | tf_op jit(solution)/shard_map/tij,tjr->tir/dot_general | solution.py:84
  (132 shorter events, 30.1 us)
Async XLA Ops:
  0.6 21.9 %copy-start = (f32[1024,128]{1,0:T(8,128)S(1)}, f32[1024,128]{1,0:T(8,128)}, u32[]{:S(2)}) copy-start(f32[1024,128]{1,0:T(8,128)} %param.7) | copy-start | bytes 1572868
  11.0 21.3 %all-to-all-start = ((s32[128,1,8]{2,1,0:T(1,128)}), s32[128,1,8]{2,1,0:T(1,128)S(1)}, u32[]{:S(2)}, u32[]{:S(2)}) async-start(s32[128,1,8]{2,1,0:T(1,128)} %bitcast), calls=%async_computation | async-start | bytes 131072 | tf_op jit(solution)/shard_map/all_to_all | solution.py:33
  22.6 4.1 copy-start.2
  32.3 19.5 %all-to-all-start.1 = ((f32[128,8,128]{2,1,0:T(8,128)}), f32[128,8,128]{2,1,0:T(8,128)S(1)}, u32[]{:S(2)}, u32[]{:S(2)}) async-start(f32[128,8,128]{2,1,0:T(8,128)} %bitcast.2), calls=%async_computation.1 | async-start | bytes 1048576 | tf_op jit(solution)/shard_map/all_to_all | solution.py:32
  62.7 47.1 %collective-permute-start = (bf16[64,1,128,128]{3,2,0,1:T(8,128)(2,1)S(1)}, bf16[64,1,128,128]{3,2,0,1:T(8,128)(2,1)S(1)}, u32[]{:S(2)}, u32[]{:S(2)}) collective-permute-start(bf16[64,1,128,128]{3,2,0,1:T(8,128)(2,1)S(1)} %get-tuple-element.17), channel_id=1, source_target_pairs={{0,1},{1,0},{2,3},{3,2},{4,5},{5,4},{6,7},{7,6},{8,9},{9,8},{10,11... | collective-permute-start | bytes 6291464 | tf_op jit(solution)/shard_map/ppermute | solution.py:14
  110.2 47.7 %collective-permute-start.1 = (bf16[32,2,128,128]{3,2,0,1:T(8,128)(2,1)S(1)}, bf16[32,2,128,128]{3,2,0,1:T(8,128)(2,1)S(1)}, u32[]{:S(2)}, u32[]{:S(2)}) collective-permute-start(bf16[32,2,128,128]{3,2,0,1:T(8,128)(2,1)S(1)} %get-tuple-element.15), channel_id=1, source_target_pairs={{0,2},{1,3},{2,0},{3,1},{4,6},{5,7},{6,4},{7,5},{8,10},{9,11},{10,... | collective-permute-start | bytes 6291464 | tf_op jit(solution)/shard_map/ppermute | solution.py:14
  158.8 5.8 collective-permute-start.2
  165.6 46.9 %collective-permute-start.3 = (bf16[8,8,128,128]{3,2,0,1:T(8,128)(2,1)S(1)}, bf16[8,8,128,128]{3,2,0,1:T(8,128)(2,1)S(1)}, u32[]{:S(2)}, u32[]{:S(2)}) collective-permute-start(bf16[8,8,128,128]{3,2,0,1:T(8,128)(2,1)S(1)} %get-tuple-element.11), channel_id=1, source_target_pairs={{0,8},{1,9},{2,10},{3,11},{4,12},{5,13},{6,14},{7,15},{8,0},{9,1},... | collective-permute-start | bytes 6291464 | tf_op jit(solution)/shard_map/ppermute | solution.py:14
  213.5 47.5 %collective-permute-start.4 = (bf16[4,16,128,128]{3,2,0,1:T(8,128)(2,1)S(1)}, bf16[4,16,128,128]{3,2,0,1:T(8,128)(2,1)S(1)}, u32[]{:S(2)}, u32[]{:S(2)}) collective-permute-start(bf16[4,16,128,128]{3,2,0,1:T(8,128)(2,1)S(1)} %get-tuple-element.9), channel_id=1, source_target_pairs={{0,16},{1,17},{2,18},{3,19},{4,20},{5,21},{6,22},{7,23},{8,24},{9,... | collective-permute-start | bytes 6291464 | tf_op jit(solution)/shard_map/ppermute | solution.py:14
  261.9 45.1 %collective-permute-start.5 = (bf16[2,32,128,128]{3,2,0,1:T(8,128)(2,1)S(1)}, bf16[2,32,128,128]{3,2,0,1:T(8,128)(2,1)S(1)}, u32[]{:S(2)}, u32[]{:S(2)}) collective-permute-start(bf16[2,32,128,128]{3,2,0,1:T(8,128)(2,1)S(1)} %get-tuple-element.7), channel_id=1, source_target_pairs={{0,32},{1,33},{2,34},{3,35},{4,36},{5,37},{6,38},{7,39},{8,40},{9,... | collective-permute-start | bytes 6291464 | tf_op jit(solution)/shard_map/ppermute | solution.py:14
  307.4 3.4 copy-start.14
  309.0 46.0 %collective-permute-start.6 = (bf16[1,64,128,128]{3,2,1,0:T(8,128)(2,1)}, bf16[1,64,128,128]{3,2,1,0:T(8,128)(2,1)}, u32[]{:S(2)}, u32[]{:S(2)}) collective-permute-start(bf16[1,64,128,128]{3,2,1,0:T(8,128)(2,1)} %get-tuple-element.5), channel_id=1, source_target_pairs={{0,64},{1,65},{2,66},{3,67},{4,68},{5,69},{6,70},{7,71},{8,72},{9,... | collective-permute-start | bytes 6291464 | tf_op jit(solution)/shard_map/ppermute | solution.py:14
  390.8 4.2 copy-start.3
  396.7 20.8 %collective-permute-start.7 = (bf16[32,1,128,128]{3,2,0,1:T(8,128)(2,1)S(1)}, bf16[32,1,128,128]{3,2,0,1:T(8,128)(2,1)S(1)}, u32[]{:S(2)}, u32[]{:S(2)}) collective-permute-start(bf16[32,1,128,128]{3,2,0,1:T(8,128)(2,1)S(1)} %get-tuple-element.29), channel_id=1, source_target_pairs={{0,1},{1,0},{2,3},{3,2},{4,5},{5,4},{6,7},{7,6},{8,9},{9,8},{10,11... | collective-permute-start | bytes 3145736 | tf_op jit(solution)/shard_map/ppermute | solution.py:14
  417.7 19.3 %collective-permute-start.8 = (bf16[16,2,128,128]{3,2,0,1:T(8,128)(2,1)S(1)}, bf16[16,2,128,128]{3,2,0,1:T(8,128)(2,1)S(1)}, u32[]{:S(2)}, u32[]{:S(2)}) collective-permute-start(bf16[16,2,128,128]{3,2,0,1:T(8,128)(2,1)S(1)} %get-tuple-element.27), channel_id=1, source_target_pairs={{0,2},{1,3},{2,0},{3,1},{4,6},{5,7},{6,4},{7,5},{8,10},{9,11},{10,... | collective-permute-start | bytes 3145736 | tf_op jit(solution)/shard_map/ppermute | solution.py:14
  437.4 10.2 %collective-permute-start.9 = (bf16[8,4,128,128]{3,2,0,1:T(8,128)(2,1)S(1)}, bf16[8,4,128,128]{3,2,0,1:T(8,128)(2,1)S(1)}, u32[]{:S(2)}, u32[]{:S(2)}) collective-permute-start(bf16[8,4,128,128]{3,2,0,1:T(8,128)(2,1)S(1)} %get-tuple-element.25), channel_id=1, source_target_pairs={{0,4},{1,5},{2,6},{3,7},{4,0},{5,1},{6,2},{7,3},{8,12},{9,13},{10,... | collective-permute-start | bytes 3145736 | tf_op jit(solution)/shard_map/ppermute | solution.py:14
  448.0 24.9 %collective-permute-start.10 = (bf16[4,8,128,128]{3,2,0,1:T(8,128)(2,1)S(1)}, bf16[4,8,128,128]{3,2,0,1:T(8,128)(2,1)S(1)}, u32[]{:S(2)}, u32[]{:S(2)}) collective-permute-start(bf16[4,8,128,128]{3,2,0,1:T(8,128)(2,1)S(1)} %get-tuple-element.23), channel_id=1, source_target_pairs={{0,8},{1,9},{2,10},{3,11},{4,12},{5,13},{6,14},{7,15},{8,0},{9,1},... | collective-permute-start | bytes 3145736 | tf_op jit(solution)/shard_map/ppermute | solution.py:14
  473.2 25.4 %collective-permute-start.11 = (bf16[2,16,128,128]{3,2,0,1:T(8,128)(2,1)S(1)}, bf16[2,16,128,128]{3,2,0,1:T(8,128)(2,1)}, u32[]{:S(2)}, u32[]{:S(2)}) collective-permute-start(bf16[2,16,128,128]{3,2,0,1:T(8,128)(2,1)S(1)} %get-tuple-element.21), channel_id=1, source_target_pairs={{0,16},{1,17},{2,18},{3,19},{4,20},{5,21},{6,22},{7,23},{8,24},{9,... | collective-permute-start | bytes 3145736 | tf_op jit(solution)/shard_map/ppermute | solution.py:14
  500.2 23.2 %collective-permute-start.12 = (bf16[1,32,128,128]{3,2,1,0:T(8,128)(2,1)S(1)}, bf16[1,32,128,128]{3,2,1,0:T(8,128)(2,1)}, u32[]{:S(2)}, u32[]{:S(2)}) collective-permute-start(bf16[1,32,128,128]{3,2,1,0:T(8,128)(2,1)S(1)} %get-tuple-element.19), channel_id=1, source_target_pairs={{0,32},{1,33},{2,34},{3,35},{4,36},{5,37},{6,38},{7,39},{8,40},{9,... | collective-permute-start | bytes 3145736 | tf_op jit(solution)/shard_map/ppermute | solution.py:14
  552.1 5.3 copy-start.5
  557.4 10.7 %collective-permute-start.13 = (bf16[16,1,128,128]{3,2,0,1:T(8,128)(2,1)S(1)}, bf16[16,1,128,128]{3,2,0,1:T(8,128)(2,1)S(1)}, u32[]{:S(2)}, u32[]{:S(2)}) collective-permute-start(bf16[16,1,128,128]{3,2,0,1:T(8,128)(2,1)S(1)} %get-tuple-element.39), channel_id=1, source_target_pairs={{0,1},{1,0},{2,3},{3,2},{4,5},{5,4},{6,7},{7,6},{8,9},{9,8},{10,11... | collective-permute-start | bytes 1572872 | tf_op jit(solution)/shard_map/ppermute | solution.py:14
  568.2 11.5 %collective-permute-start.14 = (bf16[8,2,128,128]{3,2,0,1:T(8,128)(2,1)S(1)}, bf16[8,2,128,128]{3,2,0,1:T(8,128)(2,1)S(1)}, u32[]{:S(2)}, u32[]{:S(2)}) collective-permute-start(bf16[8,2,128,128]{3,2,0,1:T(8,128)(2,1)S(1)} %get-tuple-element.37), channel_id=1, source_target_pairs={{0,2},{1,3},{2,0},{3,1},{4,6},{5,7},{6,4},{7,5},{8,10},{9,11},{10,... | collective-permute-start | bytes 1572872 | tf_op jit(solution)/shard_map/ppermute | solution.py:14
  579.9 6.2 collective-permute-start.15
  586.3 13.2 %collective-permute-start.16 = (bf16[2,8,128,128]{3,2,0,1:T(8,128)(2,1)S(1)}, bf16[2,8,128,128]{3,2,0,1:T(8,128)(2,1)S(1)}, u32[]{:S(2)}, u32[]{:S(2)}) collective-permute-start(bf16[2,8,128,128]{3,2,0,1:T(8,128)(2,1)S(1)} %get-tuple-element.33), channel_id=1, source_target_pairs={{0,8},{1,9},{2,10},{3,11},{4,12},{5,13},{6,14},{7,15},{8,0},{9,1},... | collective-permute-start | bytes 1572872 | tf_op jit(solution)/shard_map/ppermute | solution.py:14
  599.7 14.2 %collective-permute-start.17 = (bf16[1,16,128,128]{3,2,1,0:T(8,128)(2,1)S(1)}, bf16[1,16,128,128]{3,2,1,0:T(8,128)(2,1)S(1)}, u32[]{:S(2)}, u32[]{:S(2)}) collective-permute-start(bf16[1,16,128,128]{3,2,1,0:T(8,128)(2,1)S(1)} %get-tuple-element.31), channel_id=1, source_target_pairs={{0,16},{1,17},{2,18},{3,19},{4,20},{5,21},{6,22},{7,23},{8,24},{9,... | collective-permute-start | bytes 1572872 | tf_op jit(solution)/shard_map/ppermute | solution.py:14
  632.7 6.2 copy-start.4
  641.7 5.8 collective-permute-start.18
  647.5 6.8 collective-permute-start.19
  654.4 5.4 collective-permute-start.20
  660.7 4.5 copy-start.10
  660.7 4.5 copy-start.11
  660.7 4.6 copy-start.12
  660.7 4.6 copy-start.13
  660.7 7.9 %collective-permute-start.21 = (bf16[1,8,128,128]{3,2,1,0:T(8,128)(2,1)S(1)}, bf16[1,8,128,128]{3,2,1,0:T(8,128)(2,1)}, u32[]{:S(2)}, u32[]{:S(2)}) collective-permute-start(bf16[1,8,128,128]{3,2,1,0:T(8,128)(2,1)S(1)} %get-tuple-element.41), channel_id=1, source_target_pairs={{0,8},{1,9},{2,10},{3,11},{4,12},{5,13},{6,14},{7,15},{8,0},{9,1},... | collective-permute-start | bytes 786440 | tf_op jit(solution)/shard_map/ppermute | solution.py:14
  662.3 6.3 copy-start.9
  673.3 6.8 copy-start.6
  673.3 6.8 copy-start.7
  673.3 6.8 copy-start.8
  680.1 7.6 %copy-start.1 = (f32[1024,128]{1,0:T(8,128)S(1)}, f32[1024,128]{1,0:T(8,128)}, u32[]{:S(2)}) copy-start(f32[1024,128]{1,0:T(8,128)} %param.7) | copy-start | bytes 1572868
where the time goes:
time: 697 us; the launch traced here: 688 us
  waiting for transfers between devices  469 us (67%)
  local copies, waits for them, and re-layouts  75.9 us (11%)
  matrix products  55.4 us (8%)
  starting transfers between devices  49.8 us (7%)
  other arithmetic  36.5 us (5%)
    ppermute x22, waiting for transfers between devices, partner(): lax.ppermute(x, axis, [(i, i ^ 1 << apart) for i in range(lax.axis_size(a...  452 us
    dot_general x4, matrix products, per_device(): jnp.einsum('eij,ejr->eir', panels[offset:offset + entries], needed, prefe...  39.4 us
    ppermute x22, starting transfers between devices, partner(): lax.ppermute(x, axis, [(i, i ^ 1 << apart) for i in range(lax.axis_size(a...  33 us
    gather x4, local copies, waits for them, and re-layouts, per_device(): needed = received[panel_from[offset:offset + entries]]  28.1 us
    reduce_sum x3, other arithmetic, per_device(): update = products.reshape(desc_tiles, KP, BS, rhs_width).sum(axis=1)  16.5 us
  transfers between devices with their start and end apart: 24, of which 24 were waited for; matrix products, arithmetic and copies ran while one was open for 2% of the time, Pallas kernels for 0%

commit v1 on v0

v1 whole, which is shorter than its diff:
```python
import functools

import jax
import jax.numpy as jnp
from jax import lax
from jax.experimental import pallas as pl
from jax.experimental.pallas import tpu as pltpu
from jax.sharding import PartitionSpec as P

BS = 128
TS = 2
TL = 32
KP = 4
LEVELS = 4
AXES = ("leaf", "panel")
LEAF_STEP = 8
VMEM = pltpu.CompilerParams(vmem_limit_bytes=48 * 1024 * 1024)


def whole():
    return pl.BlockSpec(memory_space=pltpu.VMEM)


def split3(x):
    high = x.astype(jnp.bfloat16)
    rest = x - high.astype(jnp.float32)
    mid = rest.astype(jnp.bfloat16)
    low = (rest - mid.astype(jnp.float32)).astype(jnp.bfloat16)
    return high, mid, low


def place_rows(select, x):
    width = x.shape[1]
    parts = jnp.concatenate(split3(x), axis=1)
    out = jnp.dot(select, parts, preferred_element_type=jnp.float32)
    return out[:, :width] + out[:, width : 2 * width] + out[:, 2 * width :]


def pack_kernel(owner_ref, slot_ref, noise_ref, out_ref, places_ref):
    rows = noise_ref.shape[0]
    per_owner = 8
    owners = rows // per_owner
    owner = owner_ref[...]
    slot = slot_ref[...]
    hot = owner == lax.broadcasted_iota(jnp.int32, (owners, rows), 0)
    hot16 = hot.astype(jnp.float32).astype(jnp.bfloat16)
    before = lax.broadcasted_iota(jnp.int32, (rows, rows), 0) < lax.broadcasted_iota(
        jnp.int32, (rows, rows), 1
    )
    earlier = jnp.dot(
        hot16,
        before.astype(jnp.float32).astype(jnp.bfloat16),
        preferred_element_type=jnp.float32,
    )
    rank = jnp.sum(jnp.where(hot, earlier, 0.0), axis=0, keepdims=True)
    target = owner * per_owner + rank.astype(jnp.int32)
    select = (target == lax.broadcasted_iota(jnp.int32, (rows, rows), 0)).astype(jnp.float32)
    select = select.astype(jnp.bfloat16)
    out_ref[...] = place_rows(select, noise_ref[...])
    digit = lax.broadcasted_iota(jnp.int32, (8, rows), 0)
    digits = jnp.where(digit == 0, slot // 32, jnp.where(digit == 1, slot % 32, 0))
    moved = lax.dot_general(
        digits.astype(jnp.float32).astype(jnp.bfloat16),
        select,
        (((1,), (1,)), ((), ())),
        preferred_element_type=jnp.float32,
    )
    places_ref[...] = (moved[0:1] * 32.0 + moved[1:2]).astype(jnp.int32)


def order_rows(places_ref, arrived_ref, first, count):
    rows = arrived_ref.shape[0]
    select = places_ref[...] == first + lax.broadcasted_iota(jnp.int32, (count, rows), 0)
    return place_rows(select.astype(jnp.float32).astype(jnp.bfloat16), arrived_ref[...])


def solve(diag, right):
    return jnp.dot(
        diag, right, precision=lax.Precision.HIGHEST, preferred_element_type=jnp.float32
    )


def first_kernel(places_ref, arrived_ref, diag_ref, solved_ref, sent_ref):
    right = order_rows(places_ref, arrived_ref, 0, TS * BS)
    for t in range(TS):
        solved = solve(diag_ref[t], right[t * BS : (t + 1) * BS])
        solved_ref[t] = solved
        sent_ref[t] = solved.astype(jnp.bfloat16)


def order_kernel(places_ref, arrived_ref, out_ref):
    for tree_level in range(1, LEVELS):
        right = order_rows(places_ref, arrived_ref, tree_level * TS * BS, TS * BS)
        for t in range(TS):
            out_ref[(tree_level - 1) * TS + t] = right[t * BS : (t + 1) * BS]


def tile_update(from_ref, base, panels_ref, local, received_ref):
    left = jnp.concatenate([panels_ref[local + k] for k in range(KP)], axis=1)
    right = jnp.concatenate([received_ref[from_ref[base + k]] for k in range(KP)], axis=0)
    return jnp.dot(left, right, preferred_element_type=jnp.float32)


def level_kernel(
    offset, from_ref, received_ref, panels_ref, rights_ref, diag_ref, rest_ref, solved_ref, sent_ref
):
    tiles = rights_ref.shape[0]
    for d in range(TS):
        right = rights_ref[d] - tile_update(
            from_ref, offset + KP * d, panels_ref, KP * d, received_ref
        )
        solved = solve(diag_ref[d], right)
        solved_ref[d] = solved
        sent_ref[d] = solved.astype(jnp.bfloat16)
    for d in range(TS, tiles):
        rest_ref[d - TS] = rights_ref[d] - tile_update(
            from_ref, offset + KP * d, panels_ref, KP * d, received_ref
        )


def leaf_kernel(offset, from_ref, received_ref, panels_ref, right_ref, out_ref):
    first = offset + pl.program_id(0) * LEAF_STEP * KP
    for d in range(LEAF_STEP):
        out_ref[d] = right_ref[d] - tile_update(
            from_ref, first + KP * d, panels_ref, KP * d, received_ref
        )


def last_kernel(offset, from_ref, received_ref, panels_ref, right_ref, diag_ref, out_ref):
    first = offset + pl.program_id(0) * LEAF_STEP * KP
    for d in range(LEAF_STEP):
        right = right_ref[d] - tile_update(
            from_ref, first + KP * d, panels_ref, KP * d, received_ref
        )
        out_ref[d] = solve(diag_ref[d], right)


def entries_block(offset, count, grid):
    if grid:
        return pl.BlockSpec(
            (pl.Element(count), pl.Element(BS), pl.Element(BS)),
            lambda i, *_: (offset + i * count, 0, 0),
        )
    return pl.BlockSpec(
        (pl.Element(count), pl.Element(BS), pl.Element(BS)), lambda i, *_: (offset, 0, 0)
    )


def f32(*shape):
    return jax.ShapeDtypeStruct(shape, jnp.float32)


def b16(*shape):
    return jax.ShapeDtypeStruct(shape, jnp.bfloat16)


def per_device(
    noise_parts, elimination_row, leaf_noise, diag_inverse, panels, panel_from, send_lists
):
    owners = lax.axis_size(AXES)
    rows = noise_parts.shape[0]
    rhs = noise_parts.shape[1]
    per_owner = rows // owners
    outgoing, places = pl.pallas_call(
        pack_kernel,
        out_shape=(f32(rows, rhs), jax.ShapeDtypeStruct((1, rows), jnp.int32)),
        in_specs=[whole()] * 3,
        out_specs=(whole(), whole()),
        compiler_params=VMEM,
        name="pack",
    )(
        (elimination_row // rows).reshape(1, rows),
        (elimination_row % rows).reshape(1, rows),
        noise_parts,
    )
    arrived_at = lax.all_to_all(places.reshape(owners, per_owner), AXES, 0, 0, tiled=True)
    arrived = lax.all_to_all(outgoing.reshape(owners, per_owner, rhs), AXES, 0, 0, tiled=True)
    places = arrived_at.reshape(1, rows)
    arrived = arrived.reshape(rows, rhs)

    solved, sent = pl.pallas_call(
        first_kernel,
        grid=(1,),
        out_shape=(f32(TS, BS, rhs), b16(TS, BS, rhs)),
        in_specs=[whole(), whole(), entries_block(0, TS, False)],
        out_specs=(whole(), whole()),
        compiler_params=VMEM,
        name="first",
    )(places, arrived, diag_inverse)
    rights = pl.pallas_call(
        order_kernel,
        out_shape=f32((LEVELS - 1) * TS, BS, rhs),
        in_specs=[whole(), whole()],
        out_specs=whole(),
        compiler_params=VMEM,
        name="order",
    )(places, arrived)
    leaf_right = leaf_noise.reshape(TL, BS, rhs)
    send_row = send_lists[0]
    all_solved = [solved]
    offset = 0
    send_offset = 0
    for tree_level in range(LEVELS):
        group = owners >> tree_level
        groups = [
            list(range(g * group, (g + 1) * group)) for g in range(owners // group)
        ]
        picks = send_row[send_offset : send_offset + group]
        buffer = jnp.where((picks == 0)[:, None, None], sent[0][None], sent[1][None])
        received = lax.all_to_all(
            buffer, AXES, 0, 0, axis_index_groups=groups, tiled=True
        )
        send_offset += group
        sep_tiles = (LEVELS - 1 - tree_level) * TS
        leaf_offset = offset + KP * sep_tiles
        if tree_level < LEVELS - 1:
            first_diag = (tree_level + 1) * TS
            rest_tiles = max(sep_tiles - TS, TS)
            rest, solved, sent = pl.pallas_call(
                functools.partial(level_kernel, offset),
                grid_spec=pltpu.PrefetchScalarGridSpec(
                    num_scalar_prefetch=1,
                    grid=(1,),
                    in_specs=[
                        whole(),
                        entries_block(offset, KP * sep_tiles, False),
                        whole(),
                        entries_block(first_diag, TS, False),
                    ],
                    out_specs=(whole(), whole(), whole()),
                ),
                out_shape=(f32(rest_tiles, BS, rhs), f32(TS, BS, rhs), b16(TS, BS, rhs)),
                compiler_params=VMEM,
                name=f"level{tree_level}",
            )(panel_from, received, panels, rights, diag_inverse)
            rights = rest
            all_solved.append(solved)
        last = tree_level == LEVELS - 1
        in_specs = [
            whole(),
            entries_block(leaf_offset, KP * LEAF_STEP, True),
            entries_block(0, LEAF_STEP, True),
        ]
        operands = [panel_from, received, panels, leaf_right]
        if last:
            in_specs.append(entries_block(LEVELS * TS, LEAF_STEP, True))
            operands.append(diag_inverse)
        leaf_right = pl.pallas_call(
            functools.partial(last_kernel if last else leaf_kernel, leaf_offset),
            grid_spec=pltpu.PrefetchScalarGridSpec(
                num_scalar_prefetch=1,
                grid=(TL // LEAF_STEP,),
                in_specs=in_specs,
                out_specs=pl.BlockSpec((LEAF_STEP, BS, rhs), lambda i, *_: (i, 0, 0)),
            ),
            out_shape=f32(TL, BS, rhs),
            compiler_params=VMEM,
            name=f"leaf{tree_level}",
        )(*operands)
        offset = leaf_offset + KP * TL
    sep_solution = jnp.concatenate(all_solved, axis=0).reshape(rows, rhs)
    return (sep_solution, leaf_right.reshape(TL * BS, rhs))


def solution(mesh):
    return jax.shard_map(
        per_device,
        mesh=mesh,
        in_specs=(
            P(AXES, None),
            P(AXES),
            P(AXES, None),
            P(AXES, None, None),
            P(AXES, None, None),
            P(AXES),
            P(AXES, None),
        ),
        out_specs=(P(AXES, None), P(AXES, None)),
        check_vma=False,
    )
```

time: 697 us -> 215 us (0.31); the launches traced: 688 us -> 214 us
  waiting for transfers between devices: 469 us -> 110 us
  local copies, waits for them, and re-layouts: 75.9 us -> 10.6 us
  matrix products: 55.4 us -> 0 us
  Pallas kernels: 0 us -> 37.6 us
  other arithmetic: 36.5 us -> 9.72 us
  starting transfers between devices: 49.8 us -> 24.3 us
  blocking collectives: 0 us -> 21.2 us
    ppermute x22 -> x0, waiting for transfers between devices: 452 us -> none  [partner(): lax.ppermute(x, axis, [(i, i ^ 1 << apart) for i in range(lax.axis_size(a...]
    all_to_all x2 -> x5, waiting for transfers between devices: 17.1 us -> 110 us  [the longest x4 97.6 us: per_device(): lax.all_to_all(buffer, AXES, 0, 0, axis_index_groups=groups, tiled=True)]
    gather x18 -> x0, local copies, waits for them, and re-layouts: 56.8 us -> none  [the longest x4 28.1 us: per_device(): needed = received[panel_from[offset:offset + entries]]]
    dot_general x9 -> x0, matrix products: 55.4 us -> none  [the longest x4 39.4 us: per_device(): jnp.einsum('eij,ejr->eir', panels[offset:offset + entries], needed, prefe...]
    pallas_call x0 -> x10, Pallas kernels: none -> 37.6 us  [the longest x4 24.4 us: per_device(): pl.pallas_call(functools.partial(last_kernel if last else leaf_kernel, le...]
    ppermute x22 -> x0, starting transfers between devices: 33 us -> none  [partner(): lax.ppermute(x, axis, [(i, i ^ 1 << apart) for i in range(lax.axis_size(a...]
    all_to_all x0 -> x1, blocking collectives: none -> 21.2 us  [per_device(): lax.all_to_all(places.reshape(owners, per_owner), AXES, 0, 0, tiled=True)]
    reduce_sum x3 -> x0, other arithmetic: 16.5 us -> none  [per_device(): update = products.reshape(desc_tiles, KP, BS, rhs_width).sum(axis=1)]
  transfers between devices with their start and end apart: 24 -> 5, of which waited for: 24 -> 4; matrix products, arithmetic and copies ran while one was open for 2% -> 1% of each run, Pallas kernels for 0% -> 8%
where the time goes in v1:
time: 215 us; the launch traced here: 214 us
  waiting for transfers between devices  110 us (51%)
  Pallas kernels  37.6 us (17%)
  starting transfers between devices  24.3 us (11%)
  blocking collectives  21.2 us (10%)
  local copies, waits for them, and re-layouts  10.6 us (5%)
  other arithmetic  9.72 us (5%)
    all_to_all x4, waiting for transfers between devices, per_device(): lax.all_to_all(buffer, AXES, 0, 0, axis_index_groups=groups, tiled=True)  97.6 us
    pallas_call x4, Pallas kernels, per_device(): pl.pallas_call(functools.partial(last_kernel if last else leaf_kernel, le...  24.4 us
    all_to_all x1, blocking collectives, per_device(): lax.all_to_all(places.reshape(owners, per_owner), AXES, 0, 0, tiled=True)  21.2 us
    all_to_all x4, starting transfers between devices, per_device(): lax.all_to_all(buffer, AXES, 0, 0, axis_index_groups=groups, tiled=True)  20.2 us
    all_to_all x1, waiting for transfers between devices, per_device(): lax.all_to_all(outgoing.reshape(owners, per_owner, rhs), AXES, 0, 0, tile...  12.6 us
    unnamed x30, local copies, waits for them, and re-layouts  9.9 us
    pallas_call x3, Pallas kernels, per_device(): pl.pallas_call(functools.partial(level_kernel, offset), grid_spec=pltpu.P...  9.03 us
    select_n x4, other arithmetic, per_device(): jnp.where((picks == 0)[:, None, None], sent[0][None], sent[1][None])  5.91 us
  transfers between devices with their start and end apart: 5, of which 4 were waited for; matrix products, arithmetic and copies ran while one was open for 1% of the time, Pallas kernels for 8%

profile of v1, /device:TPU:1, one launch (start us, length us, event | category | flops | bytes accessed | tf_op | source)
XLA Modules:
  0.0 214.5 jit_solution(4068289338064656148)
XLA Ops:
  0.6 0.7 add_select_fusion
  1.3 0.0 copy-start.6
  1.3 1.0 copy-done.6
  2.4 2.5 %pack.1 = (f32[1024,128]{1,0:T(8,128)}, s32[1,1024]{1,0:T(1,128)S(1)}) custom-call(s32[1,1024]{1,0:T(1,128)S(1)} %bitcast.36, s32[1,1024]{1,0:T(1,128)S(1)} %bitcast.35, f32[1024,128]{1,0:T(8,128)S(1)} %copy-done.6), custom_call_target="tpu_custom_call" | custom-call | tf_op jit(solution)/shard_map/pack/pallas_call | solution.py:164
  4.9 0.5 broadcast.49
  5.4 0.7 reduce.6
  6.0 0.1 all_to_all.21
  6.1 21.2 %all_to_all.34 = s32[128,1,8]{2,1,0:T(1,128)S(1)} all-to-all(s32[128,1,8]{2,1,0:T(1,128)S(1)} %bitcast.39), channel_id=1, replica_groups=mesh['leaf'=32,'panel'=4] {'leaf','panel'}, dimensions={0} | all-to-all | bytes 8192 | tf_op jit(solution)/shard_map/all_to_all | solution.py:176
  27.3 4.1 %all-to-all-start.1 = ((f32[128,8,128]{2,1,0:T(8,128)}), f32[128,8,128]{2,1,0:T(8,128)S(1)}, u32[]{:S(2)}, u32[]{:S(2)}) async-start(f32[128,8,128]{2,1,0:T(8,128)} %bitcast.3), calls=%async_computation.1 | async-start | bytes 1048576 | tf_op jit(solution)/shard_map/all_to_all | solution.py:177
  31.4 0.7 compare_bitcast_fusion.3
  32.0 0.8 reduce.7
  32.9 0.1 reshape.67.places_ref
  33.0 12.6 %all-to-all-done.1 = f32[128,8,128]{2,1,0:T(8,128)S(1)} async-done(((f32[128,8,128]{2,1,0:T(8,128)}), f32[128,8,128]{2,1,0:T(8,128)S(1)}, u32[]{:S(2)}, u32[]{:S(2)}) %all-to-all-start.1) | async-done | bytes 524320 | tf_op jit(solution)/shard_map/all_to_all | solution.py:177
  45.5 0.0 copy-start
  45.5 1.7 copy-done
  47.3 0.7 first.1
  47.9 0.0 copy-start.8
  47.9 0.6 copy-done.8
  48.6 2.4 %broadcast_select_fusion = bf16[128,128,128]{2,1,0:T(8,128)(2,1)} fusion(pred[128]{0:T(512)(128)(4,1)S(1)} %compare_bitcast_fusion.3, bf16[128,128]{1,0:T(8,128)(2,1)S(1)} %get-tuple-element.33, bf16[128,128]{1,0:T(8,128)(2,1)S(1)} %get-tuple-element.32), kind=kLoop, calls=%fused_computation | loop fusion | flops 2097152 | bytes 4259968 | tf_op jit(solution)/shard_map/jit(_where)/select_n | solution.py:209
  50.9 0.0 copy-start.14
  50.9 0.0 copy-start.1
  50.9 5.0 %all-to-all-start.2 = ((bf16[128,128,128]{2,1,0:T(8,128)(2,1)}), bf16[128,128,128]{2,1,0:T(8,128)(2,1)}, u32[]{:S(2)}, u32[]{:S(2)}) async-start(bf16[128,128,128]{2,1,0:T(8,128)(2,1)} %broadcast_select_fusion), calls=%async_computation.2 | async-start | bytes 8388608 | tf_op jit(solution)/shard_map/all_to_all | solution.py:210
  55.9 0.0 copy-done.14
  55.9 1.0 order.1.rights_ref
  57.0 52.2 %all-to-all-done.2.received_ref = bf16[128,128,128]{2,1,0:T(8,128)(2,1)} async-done(((bf16[128,128,128]{2,1,0:T(8,128)(2,1)}), bf16[128,128,128]{2,1,0:T(8,128)(2,1)}, u32[]{:S(2)}, u32[]{:S(2)}) %all-to-all-start.2) | async-done | bytes 4194336 | tf_op jit(solution)/shard_map/all_to_all | solution.py:210
  109.2 0.0 copy-done.1
  109.2 0.0 copy-done.7
  109.2 3.6 %level0.1 = (f32[4,128,128]{2,1,0:T(8,128)S(1)}, f32[2,128,128]{2,1,0:T(8,128)S(1)}, bf16[2,128,128]{2,1,0:T(8,128)(2,1)S(1)}) custom-call(s32[560]{0:T(1024)S(1)} %copy-done.7, bf16[128,128,128]{2,1,0:T(8,128)(2,1)} %all-to-all-done.2.received_ref, bf16[560,128,128]{2,1,0:T(8,128)(2,1)} %panels_ref.13, f32[6,128,128]{2,1,0:T(8,128)S(1)} %order.1.rights_ref, ...), custom_call_target="tpu_custom_call" | custom-call | tf_op jit(solution)/shard_map/level0/pallas_call | solution.py:219
  112.7 0.0 copy-start.10
  112.7 1.5 broadcast_select_fusion.1
  114.3 0.0 copy-done.10
  114.3 5.2 %all-to-all-start.3 = ((bf16[64,128,128]{2,1,0:T(8,128)(2,1)}), bf16[64,128,128]{2,1,0:T(8,128)(2,1)}, u32[]{:S(2)}, u32[]{:S(2)}) async-start(bf16[64,128,128]{2,1,0:T(8,128)(2,1)} %broadcast_select_fusion.1), calls=%async_computation.3 | async-start | bytes 4194304 | tf_op jit(solution)/shard_map/all_to_all | solution.py:210
  119.5 0.1 compare_bitcast_fusion.1
  119.6 29.4 %all-to-all-done.3.received_ref = bf16[64,128,128]{2,1,0:T(8,128)(2,1)} async-done(((bf16[64,128,128]{2,1,0:T(8,128)(2,1)}), bf16[64,128,128]{2,1,0:T(8,128)(2,1)}, u32[]{:S(2)}, u32[]{:S(2)}) %all-to-all-start.3) | async-done | bytes 2097184 | tf_op jit(solution)/shard_map/all_to_all | solution.py:210
  149.0 2.8 %level1.1 = (f32[2,128,128]{2,1,0:T(8,128)S(1)}, f32[2,128,128]{2,1,0:T(8,128)S(1)}, bf16[2,128,128]{2,1,0:T(8,128)(2,1)S(1)}) custom-call(s32[560]{0:T(1024)S(1)} %copy-done.7, bf16[64,128,128]{2,1,0:T(8,128)(2,1)} %all-to-all-done.3.received_ref, bf16[560,128,128]{2,1,0:T(8,128)(2,1)} %panels_ref.13, f32[4,128,128]{2,1,0:T(8,128)S(1)} %get-tuple-element.20.rights_ref, ...), custom_call_target="tpu_custom_call" | custom-call | tf_op jit(solution)/shard_map/level1/pallas_call | solution.py:219
  151.8 1.1 broadcast_select_fusion.2
  152.9 5.3 %all-to-all-start.4 = ((bf16[32,128,128]{2,1,0:T(8,128)(2,1)}), bf16[32,128,128]{2,1,0:T(8,128)(2,1)}, u32[]{:S(2)}, u32[]{:S(2)}) async-start(bf16[32,128,128]{2,1,0:T(8,128)(2,1)} %broadcast_select_fusion.2), calls=%async_computation.4 | async-start | bytes 2097152 | tf_op jit(solution)/shard_map/all_to_all | solution.py:210
  158.2 0.1 compare_bitcast_fusion
  158.3 16.0 %all-to-all-done.4.received_ref = bf16[32,128,128]{2,1,0:T(8,128)(2,1)} async-done(((bf16[32,128,128]{2,1,0:T(8,128)(2,1)}), bf16[32,128,128]{2,1,0:T(8,128)(2,1)}, u32[]{:S(2)}, u32[]{:S(2)}) %all-to-all-start.4) | async-done | bytes 1048608 | tf_op jit(solution)/shard_map/all_to_all | solution.py:210
  174.3 2.7 %level2.1 = (f32[2,128,128]{2,1,0:T(8,128)}, f32[2,128,128]{2,1,0:T(8,128)S(1)}, bf16[2,128,128]{2,1,0:T(8,128)(2,1)S(1)}) custom-call(s32[560]{0:T(1024)S(1)} %copy-done.7, bf16[32,128,128]{2,1,0:T(8,128)(2,1)} %all-to-all-done.4.received_ref, bf16[560,128,128]{2,1,0:T(8,128)(2,1)} %panels_ref.13, f32[2,128,128]{2,1,0:T(8,128)S(1)} %get-tuple-element.23.rights_ref, ...), custom_call_target="tpu_custom_call" | custom-call | tf_op jit(solution)/shard_map/level2/pallas_call | solution.py:219
  177.0 0.0 copy-start.12
  177.0 0.7 copy-done.12
  177.7 0.9 broadcast_select_fusion.3
  178.6 4.7 %all-to-all-start.5 = ((bf16[16,128,128]{2,1,0:T(8,128)(2,1)}), bf16[16,128,128]{2,1,0:T(8,128)(2,1)S(1)}, u32[]{:S(2)}, u32[]{:S(2)}) async-start(bf16[16,128,128]{2,1,0:T(8,128)(2,1)} %broadcast_select_fusion.3), calls=%async_computation.5 | async-start | bytes 1048576 | tf_op jit(solution)/shard_map/all_to_all | solution.py:210
  183.3 0.0 copy-start.5
  183.3 1.6 copy-done.5
  184.9 5.8 %leaf0.1.right_ref = f32[32,128,128]{2,1,0:T(8,128)S(1)} custom-call(s32[560]{0:T(1024)S(1)} %copy-done.7, bf16[128,128,128]{2,1,0:T(8,128)(2,1)} %all-to-all-done.2.received_ref, bf16[560,128,128]{2,1,0:T(8,128)(2,1)} %panels_ref.13, f32[32,128,128]{2,1,0:T(8,128)S(1)} %bitcast.34), custom_call_target="tpu_custom_call" | custom-call | tf_op jit(solution)/shard_map/leaf0/pallas_call | solution.py:248
  190.7 0.0 copy-start.4
  190.7 1.3 copy-done.4
  192.0 5.6 %leaf1.1.right_ref = f32[32,128,128]{2,1,0:T(8,128)S(1)} custom-call(s32[560]{0:T(1024)S(1)} %copy-done.7, bf16[64,128,128]{2,1,0:T(8,128)(2,1)} %all-to-all-done.3.received_ref, bf16[560,128,128]{2,1,0:T(8,128)(2,1)} %panels_ref.13, f32[32,128,128]{2,1,0:T(8,128)} %copy-done.4), custom_call_target="tpu_custom_call" | custom-call | tf_op jit(solution)/shard_map/leaf1/pallas_call | solution.py:248
  197.6 0.0 copy-start.9
  197.6 0.0 copy-start.11
  197.6 0.0 copy-start.13
  197.6 4.8 %leaf2.1.right_ref = f32[32,128,128]{2,1,0:T(8,128)S(1)} custom-call(s32[560]{0:T(1024)S(1)} %copy-done.7, bf16[32,128,128]{2,1,0:T(8,128)(2,1)} %all-to-all-done.4.received_ref, bf16[560,128,128]{2,1,0:T(8,128)(2,1)} %panels_ref.13, f32[32,128,128]{2,1,0:T(8,128)S(1)} %leaf1.1.right_ref), custom_call_target="tpu_custom_call" | custom-call | tf_op jit(solution)/shard_map/leaf2/pallas_call | solution.py:248
  202.4 0.0 copy-start.2
  202.4 1.3 copy-done.2
  203.8 0.0 copy-done.9
  203.8 0.0 copy-done.11
  203.8 0.0 copy-done.13
  203.8 0.8 pad_maximum_fusion
  204.6 0.0 all-to-all-done.5.received_ref
  204.6 0.0 copy-start.3
  204.6 1.6 copy-done.3
  206.2 8.3 %leaf3.1 = f32[32,128,128]{2,1,0:T(8,128)} custom-call(s32[560]{0:T(1024)S(1)} %copy-done.7, bf16[16,128,128]{2,1,0:T(8,128)(2,1)S(1)} %all-to-all-done.5.received_ref, bf16[560,128,128]{2,1,0:T(8,128)(2,1)} %panels_ref.13, f32[32,128,128]{2,1,0:T(8,128)S(1)} %copy-done.3, f32[40,128,128]{2,1,0:T(8,128)S(1)} %copy-done.1), custom_call_target="tpu_custom_call" | custom-call | tf_op jit(solution)/shard_map/leaf3/pallas_call | solution.py:248
  (6 shorter events, 0.0 us)
Async XLA Ops:
  1.3 1.0 copy-start.6
  27.3 18.2 %all-to-all-start.1 = ((f32[128,8,128]{2,1,0:T(8,128)}), f32[128,8,128]{2,1,0:T(8,128)S(1)}, u32[]{:S(2)}, u32[]{:S(2)}) async-start(f32[128,8,128]{2,1,0:T(8,128)} %bitcast.3), calls=%async_computation.1 | async-start | bytes 1048576 | tf_op jit(solution)/shard_map/all_to_all | solution.py:177
  45.5 1.7 copy-start
  47.9 0.6 copy-start.8
  50.9 5.0 %copy-start.14 = (s32[1,240]{1,0:T(1,128)S(1)}, s32[1,240]{1,0:T(1,128)}, u32[]{:S(2)}) copy-start(s32[1,240]{1,0:T(1,128)} %param.13) | copy-start | bytes 2884
  50.9 58.2 %copy-start.1 = (f32[40,128,128]{2,1,0:T(8,128)S(1)}, f32[40,128,128]{2,1,0:T(8,128)}, u32[]{:S(2)}) copy-start(f32[40,128,128]{2,1,0:T(8,128)} %diag_ref.9) | copy-start | bytes 7864324
  50.9 58.2 %copy-start.7 = (s32[560]{0:T(1024)S(1)}, s32[560]{0:T(1024)}, u32[]{:S(2)}) copy-start(s32[560]{0:T(1024)} %from_ref.13) | copy-start | bytes 6724
  50.9 58.2 %all-to-all-start.2 = ((bf16[128,128,128]{2,1,0:T(8,128)(2,1)}), bf16[128,128,128]{2,1,0:T(8,128)(2,1)}, u32[]{:S(2)}, u32[]{:S(2)}) async-start(bf16[128,128,128]{2,1,0:T(8,128)(2,1)} %broadcast_select_fusion), calls=%async_computation.2 | async-start | bytes 8388608 | tf_op jit(solution)/shard_map/all_to_all | solution.py:210
  112.7 1.6 copy-start.10
  114.3 34.7 %all-to-all-start.3 = ((bf16[64,128,128]{2,1,0:T(8,128)(2,1)}), bf16[64,128,128]{2,1,0:T(8,128)(2,1)}, u32[]{:S(2)}, u32[]{:S(2)}) async-start(bf16[64,128,128]{2,1,0:T(8,128)(2,1)} %broadcast_select_fusion.1), calls=%async_computation.3 | async-start | bytes 4194304 | tf_op jit(solution)/shard_map/all_to_all | solution.py:210
  152.9 21.4 %all-to-all-start.4 = ((bf16[32,128,128]{2,1,0:T(8,128)(2,1)}), bf16[32,128,128]{2,1,0:T(8,128)(2,1)}, u32[]{:S(2)}, u32[]{:S(2)}) async-start(bf16[32,128,128]{2,1,0:T(8,128)(2,1)} %broadcast_select_fusion.2), calls=%async_computation.4 | async-start | bytes 2097152 | tf_op jit(solution)/shard_map/all_to_all | solution.py:210
  177.0 0.7 copy-start.12
  178.6 26.0 %all-to-all-start.5 = ((bf16[16,128,128]{2,1,0:T(8,128)(2,1)}), bf16[16,128,128]{2,1,0:T(8,128)(2,1)S(1)}, u32[]{:S(2)}, u32[]{:S(2)}) async-start(bf16[16,128,128]{2,1,0:T(8,128)(2,1)} %broadcast_select_fusion.3), calls=%async_computation.5 | async-start | bytes 1048576 | tf_op jit(solution)/shard_map/all_to_all | solution.py:210
  183.3 1.6 copy-start.5
  190.7 1.3 copy-start.4
  197.6 6.2 %copy-start.9 = (f32[2,128,128]{2,1,0:T(8,128)S(1)}, f32[2,128,128]{2,1,0:T(8,128)}, u32[]{:S(2)}) copy-start(f32[2,128,128]{2,1,0:T(8,128)} %copy-done.8) | copy-start | bytes 393220
  197.6 6.2 %copy-start.11 = (f32[2,128,128]{2,1,0:T(8,128)S(1)}, f32[2,128,128]{2,1,0:T(8,128)}, u32[]{:S(2)}) copy-start(f32[2,128,128]{2,1,0:T(8,128)} %copy-done.10) | copy-start | bytes 393220
  197.6 6.2 %copy-start.13 = (f32[2,128,128]{2,1,0:T(8,128)S(1)}, f32[2,128,128]{2,1,0:T(8,128)}, u32[]{:S(2)}) copy-start(f32[2,128,128]{2,1,0:T(8,128)} %copy-done.12) | copy-start | bytes 393220
  202.4 1.3 copy-start.2
  204.6 1.6 copy-start.3

commit v2 on v1

v2 whole, which is shorter than its diff:
```python
import functools

import jax
import jax.numpy as jnp
from jax import lax
from jax.experimental import pallas as pl
from jax.experimental.pallas import tpu as pltpu
from jax.sharding import PartitionSpec as P

BS = 128
TS = 2
TL = 32
KP = 4
LEVELS = 4
AXES = ("leaf", "panel")
LEAF_STEP = 8
VMEM = pltpu.CompilerParams(vmem_limit_bytes=48 * 1024 * 1024)


def whole():
    return pl.BlockSpec(memory_space=pltpu.VMEM)


def halves(x):
    high = x.astype(jnp.bfloat16)
    return high, (x - high.astype(jnp.float32)).astype(jnp.bfloat16)


def hot(condition):
    return condition.astype(jnp.float32).astype(jnp.bfloat16)


def transposed_dot(a, b):
    return lax.dot_general(a, b, (((1,), (1,)), ((), ())), preferred_element_type=jnp.float32)


def pack_kernel(target_ref, noise_ref, out_ref):
    rows = noise_ref.shape[0]
    owners, per_owner, width = out_ref.shape
    target = target_ref[...]
    owner = target // rows
    slot = target % rows
    mine = owner == lax.broadcasted_iota(jnp.int32, (owners, rows), 0)
    before = lax.broadcasted_iota(jnp.int32, (rows, rows), 0) < lax.broadcasted_iota(
        jnp.int32, (rows, rows), 1
    )
    earlier = jnp.dot(hot(mine), hot(before), preferred_element_type=jnp.float32)
    rank = jnp.sum(jnp.where(mine, earlier, 0.0), axis=0, keepdims=True)
    position = owner * per_owner + rank.astype(jnp.int32)
    select = hot(position == lax.broadcasted_iota(jnp.int32, (rows, rows), 0))
    both = jnp.concatenate(halves(noise_ref[...]), axis=1)
    out = jnp.dot(select, both, preferred_element_type=jnp.float32)
    level_rows = TS * BS
    lane = lax.broadcasted_iota(jnp.int32, (BS, rows), 0)
    place = jnp.where(slot // level_rows == lane, slot % level_rows, -1)
    meta = transposed_dot(select, place.astype(jnp.float32).astype(jnp.bfloat16))
    out = jnp.concatenate([out, meta], axis=1)
    out_ref[...] = out.reshape(owners, per_owner, width).astype(jnp.bfloat16)


def order_rows(arrived_ref, tree_levels):
    owners, per_owner, width = arrived_ref.shape
    rows = owners * per_owner
    rhs = width - BS
    arrived = arrived_ref[...].astype(jnp.float32).reshape(rows, width).astype(jnp.bfloat16)
    unit = hot(
        lax.broadcasted_iota(jnp.int32, (8, BS), 0) == lax.broadcasted_iota(jnp.int32, (8, BS), 1)
    )
    places = transposed_dot(unit, arrived[:, rhs:]).astype(jnp.int32)
    out = []
    for tree_level in tree_levels:
        select = hot(
            places[tree_level : tree_level + 1]
            == lax.broadcasted_iota(jnp.int32, (TS * BS, rows), 0)
        )
        both = jnp.dot(select, arrived[:, :rhs], preferred_element_type=jnp.float32)
        out.append(both[:, : rhs // 2] + both[:, rhs // 2 :])
    return out


def solve(diag, right):
    left = jnp.concatenate(halves(diag), axis=0)
    both = jnp.concatenate(halves(right), axis=1)
    out = jnp.dot(left, both, preferred_element_type=jnp.float32)
    rows, width = diag.shape[0], right.shape[1]
    return (
        out[:rows, :width]
        + (out[:rows, width:] + out[rows:, :width])
        + out[rows:, width:]
    )


def finish(right, diag_ref, t, solved_ref, sent_ref):
    solved = solve(diag_ref[t], right)
    solved_ref[t] = solved
    sent_ref[t] = solved.astype(jnp.bfloat16)


def spread(send_offset, send_ref, sent_ref, buffer_ref):
    for j in range(buffer_ref.shape[0]):
        buffer_ref[j] = sent_ref[send_ref[send_offset + j]]


def first_kernel(send_ref, arrived_ref, diag_ref, solved_ref, buffer_ref, sent_ref):
    [right] = order_rows(arrived_ref, [0])
    for t in range(TS):
        finish(right[t * BS : (t + 1) * BS], diag_ref, t, solved_ref, sent_ref)
    spread(0, send_ref, sent_ref, buffer_ref)


def order_kernel(arrived_ref, out_ref):
    for i, right in enumerate(order_rows(arrived_ref, range(1, LEVELS))):
        for t in range(TS):
            out_ref[i * TS + t] = right[t * BS : (t + 1) * BS]


def tile_update(from_ref, base, panels_ref, local, received_ref):
    left = jnp.concatenate([panels_ref[local + k] for k in range(KP)], axis=1)
    right = jnp.concatenate([received_ref[from_ref[base + k]] for k in range(KP)], axis=0)
    return jnp.dot(left, right, preferred_element_type=jnp.float32)


def level_kernel(
    offset, send_offset, from_ref, send_ref, received_ref, panels_ref, rights_ref, diag_ref,
    rest_ref, solved_ref, buffer_ref, sent_ref,
):
    for d in range(TS):
        right = rights_ref[d] - tile_update(
            from_ref, offset + KP * d, panels_ref, KP * d, received_ref
        )
        finish(right, diag_ref, d, solved_ref, sent_ref)
    spread(send_offset, send_ref, sent_ref, buffer_ref)
    for d in range(TS, rights_ref.shape[0]):
        rest_ref[d - TS] = rights_ref[d] - tile_update(
            from_ref, offset + KP * d, panels_ref, KP * d, received_ref
        )


def leaf_kernel(offset, from_ref, received_ref, panels_ref, right_ref, out_ref):
    first = offset + pl.program_id(0) * LEAF_STEP * KP
    for d in range(LEAF_STEP):
        out_ref[d] = right_ref[d] - tile_update(
            from_ref, first + KP * d, panels_ref, KP * d, received_ref
        )


def last_kernel(offset, from_ref, received_ref, panels_ref, right_ref, diag_ref, out_ref):
    first = offset + pl.program_id(0) * LEAF_STEP * KP
    for d in range(LEAF_STEP):
        right = right_ref[d] - tile_update(
            from_ref, first + KP * d, panels_ref, KP * d, received_ref
        )
        out_ref[d] = solve(diag_ref[d], right)


def entries_block(offset, count, grid):
    if grid:
        return pl.BlockSpec(
            (pl.Element(count), pl.Element(BS), pl.Element(BS)),
            lambda i, *_: (offset + i * count, 0, 0),
        )
    return pl.BlockSpec(
        (pl.Element(count), pl.Element(BS), pl.Element(BS)), lambda i, *_: (offset, 0, 0)
    )


def f32(*shape):
    return jax.ShapeDtypeStruct(shape, jnp.float32)


def b16(*shape):
    return jax.ShapeDtypeStruct(shape, jnp.bfloat16)


def per_device(
    noise_parts, elimination_row, leaf_noise, diag_inverse, panels, panel_from, send_lists
):
    owners = lax.axis_size(AXES)
    rows = noise_parts.shape[0]
    rhs = noise_parts.shape[1]
    per_owner = rows // owners
    outgoing = pl.pallas_call(
        pack_kernel,
        out_shape=b16(owners, per_owner, 2 * rhs + BS),
        in_specs=[whole()] * 2,
        out_specs=whole(),
        compiler_params=VMEM,
        name="pack",
    )(elimination_row.reshape(1, rows), noise_parts)
    arrived = lax.all_to_all(outgoing, AXES, 0, 0, tiled=True)
    send_row = send_lists[0]
    solved, buffer = pl.pallas_call(
        first_kernel,
        grid_spec=pltpu.PrefetchScalarGridSpec(
            num_scalar_prefetch=1,
            grid=(1,),
            in_specs=[whole(), entries_block(0, TS, False)],
            out_specs=(whole(), whole()),
            scratch_shapes=[pltpu.VMEM((TS, BS, rhs), jnp.bfloat16)],
        ),
        out_shape=(f32(TS, BS, rhs), b16(owners, BS, rhs)),
        compiler_params=VMEM,
        name="first",
    )(send_row, arrived, diag_inverse)
    rights = pl.pallas_call(
        order_kernel,
        out_shape=f32((LEVELS - 1) * TS, BS, rhs),
        in_specs=[whole()],
        out_specs=whole(),
        compiler_params=VMEM,
        name="order",
    )(arrived)
    leaf_right = leaf_noise.reshape(TL, BS, rhs)
    all_solved = [solved]
    offset = 0
    send_offset = 0
    for tree_level in range(LEVELS):
        group = owners >> tree_level
        groups = [
            list(range(g * group, (g + 1) * group)) for g in range(owners // group)
        ]
        received = lax.all_to_all(
            buffer, AXES, 0, 0, axis_index_groups=groups, tiled=True
        )
        if tree_level:
            received, leaf_right = lax.optimization_barrier((received, leaf_right))
        send_offset += group
        sep_tiles = (LEVELS - 1 - tree_level) * TS
        leaf_offset = offset + KP * sep_tiles
        if tree_level < LEVELS - 1:
            first_diag = (tree_level + 1) * TS
            rest_tiles = max(sep_tiles - TS, TS)
            rights, solved, buffer = pl.pallas_call(
                functools.partial(level_kernel, offset, send_offset),
                grid_spec=pltpu.PrefetchScalarGridSpec(
                    num_scalar_prefetch=2,
                    grid=(1,),
                    in_specs=[
                        whole(),
                        entries_block(offset, KP * sep_tiles, False),
                        whole(),
                        entries_block(first_diag, TS, False),
                    ],
                    out_specs=(whole(), whole(), whole()),
                    scratch_shapes=[pltpu.VMEM((TS, BS, rhs), jnp.bfloat16)],
                ),
                out_shape=(
                    f32(rest_tiles, BS, rhs),
                    f32(TS, BS, rhs),
                    b16(group // 2, BS, rhs),
                ),
                compiler_params=VMEM,
                name=f"level{tree_level}",
            )(panel_from, send_row, received, panels, rights, diag_inverse)
            all_solved.append(solved)
        last = tree_level == LEVELS - 1
        in_specs = [
            whole(),
            entries_block(leaf_offset, KP * LEAF_STEP, True),
            entries_block(0, LEAF_STEP, True),
        ]
        operands = [panel_from, received, panels, leaf_right]
        if last:
            in_specs.append(entries_block(LEVELS * TS, LEAF_STEP, True))
            operands.append(diag_inverse)
        leaf_right = pl.pallas_call(
            functools.partial(last_kernel if last else leaf_kernel, leaf_offset),
            grid_spec=pltpu.PrefetchScalarGridSpec(
                num_scalar_prefetch=1,
                grid=(TL // LEAF_STEP,),
                in_specs=in_specs,
                out_specs=pl.BlockSpec((LEAF_STEP, BS, rhs), lambda i, *_: (i, 0, 0)),
            ),
            out_shape=f32(TL, BS, rhs),
            compiler_params=VMEM,
            name=f"leaf{tree_level}",
        )(*operands)
        offset = leaf_offset + KP * TL
    sep_solution = jnp.concatenate(all_solved, axis=0).reshape(rows, rhs)
    return (sep_solution, leaf_right.reshape(TL * BS, rhs))


def solution(mesh):
    return jax.shard_map(
        per_device,
        mesh=mesh,
        in_specs=(
            P(AXES, None),
            P(AXES),
            P(AXES, None),
            P(AXES, None, None),
            P(AXES, None, None),
            P(AXES),
            P(AXES, None),
        ),
        out_specs=(P(AXES, None), P(AXES, None)),
        check_vma=False,
    )
```

time: 215 us -> 187 us (0.87)
  waiting for transfers between devices: 110 us -> 82.3 us
  other arithmetic: 9.72 us -> 0.83 us
  blocking collectives: 21.2 us -> 28.2 us
  local copies, waits for them, and re-layouts: 10.6 us -> 16.7 us
  starting transfers between devices: 24.3 us -> 19.3 us
    all_to_all x4, waiting for transfers between devices: 97.6 us -> 82.3 us  [per_device(): lax.all_to_all(buffer, AXES, 0, 0, axis_index_groups=groups, tiled=True)]
    all_to_all x1 -> x0, waiting for transfers between devices: 12.6 us -> none  [per_device(): lax.all_to_all(outgoing.reshape(owners, per_owner, rhs), AXES, 0, 0, tile...]
    all_to_all x1, blocking collectives: 21.2 us -> 28.2 us  [per_device(): arrived = lax.all_to_all(outgoing, AXES, 0, 0, tiled=True)]
    unnamed x30 -> x40, local copies, waits for them, and re-layouts: 9.9 us -> 16.7 us
    select_n x5 -> x0, other arithmetic: 6.61 us -> none  [the longest x4 5.91 us: per_device(): jnp.where((picks == 0)[:, None, None], sent[0][None], sent[1][None])]
    all_to_all x1 -> x0, starting transfers between devices: 4.06 us -> none  [per_device(): lax.all_to_all(outgoing.reshape(owners, per_owner, rhs), AXES, 0, 0, tile...]
    pallas_call x5, Pallas kernels: 12.2 us -> 14.7 us  [the longest x3 9.49 us: per_device(): pl.pallas_call(functools.partial(level_kernel, offset, send_offset), grid...]
    pallas_call x4, Pallas kernels: 24.4 us -> 22.2 us  [per_device(): pl.pallas_call(functools.partial(last_kernel if last else leaf_kernel, le...]
  transfers between devices with their start and end apart: 5 -> 4, of which waited for: 4 -> 4; matrix products, arithmetic and copies ran while one was open for 1% -> 0% of each run, Pallas kernels for 8% -> 9%
where the time goes in v2:
time: 187 us; the launch traced here: 186 us
  waiting for transfers between devices  82.3 us (44%)
  Pallas kernels  37.7 us (20%)
  blocking collectives  28.2 us (15%)
  starting transfers between devices  19.3 us (10%)
  local copies, waits for them, and re-layouts  16.7 us (9%)
    all_to_all x4, waiting for transfers between devices, per_device(): lax.all_to_all(buffer, AXES, 0, 0, axis_index_groups=groups, tiled=True)  82.3 us
    all_to_all x1, blocking collectives, per_device(): arrived = lax.all_to_all(outgoing, AXES, 0, 0, tiled=True)  28.2 us
    pallas_call x4, Pallas kernels, per_device(): pl.pallas_call(functools.partial(last_kernel if last else leaf_kernel, le...  22.2 us
    all_to_all x4, starting transfers between devices, per_device(): lax.all_to_all(buffer, AXES, 0, 0, axis_index_groups=groups, tiled=True)  19.3 us
    unnamed x40, local copies, waits for them, and re-layouts  16.7 us
    pallas_call x3, Pallas kernels, per_device(): pl.pallas_call(functools.partial(level_kernel, offset, send_offset), grid...  9.49 us
  transfers between devices with their start and end apart: 4, of which 4 were waited for; matrix products, arithmetic and copies ran while one was open for 0% of the time, Pallas kernels for 9%

profile of v2, /device:TPU:1, one launch (start us, length us, event | category | flops | bytes accessed | tf_op | source)
XLA Modules:
  0.0 185.9 jit_solution(3121267419931827700)
XLA Ops:
  0.6 0.0 copy-start
  0.6 0.0 copy-start.13
  0.7 1.2 copy-done.13
  1.8 0.0 copy-start.19
  1.8 0.7 copy-done.19
  2.5 0.0 copy-start.18
  2.5 1.7 pack.1
  4.2 28.2 %all_to_all.25.arrived_ref = bf16[128,8,384]{2,1,0:T(8,128)(2,1)S(1)} all-to-all(bf16[128,8,384]{2,1,0:T(8,128)(2,1)S(1)} %pack.1), channel_id=1, replica_groups=mesh['leaf'=32,'panel'=4] {'leaf','panel'}, dimensions={0} | all-to-all | bytes 1572864 | tf_op jit(solution)/shard_map/all_to_all | solution.py:190
  32.5 0.0 copy-done
  32.5 0.0 copy-done.18
  32.5 3.6 %first.1 = (f32[2,128,128]{2,1,0:T(8,128)S(1)}, bf16[128,128,128]{2,1,0:T(8,128)(2,1)}) custom-call(s32[240]{0:T(256)S(1)} %bitcast.6, bf16[128,8,384]{2,1,0:T(8,128)(2,1)S(1)} %all_to_all.25.arrived_ref, f32[40,128,128]{2,1,0:T(8,128)S(1)} %copy-done), custom_call_target="tpu_custom_call" | custom-call | tf_op jit(solution)/shard_map/first/pallas_call | solution.py:192
  36.0 0.0 copy-start.15
  36.0 4.9 %all-to-all-start.1 = ((bf16[128,128,128]{2,1,0:T(8,128)(2,1)}), bf16[128,128,128]{2,1,0:T(8,128)(2,1)}, u32[]{:S(2)}, u32[]{:S(2)}) async-start(bf16[128,128,128]{2,1,0:T(8,128)(2,1)} %get-tuple-element.19), calls=%async_computation.1 | async-start | bytes 8388608 | tf_op jit(solution)/shard_map/all_to_all | solution.py:222
  40.9 0.7 order.1.rights_ref
  41.7 0.0 copy-start.11
  41.7 0.7 copy-done.11
  42.4 51.8 %all-to-all-done.1.received_ref = bf16[128,128,128]{2,1,0:T(8,128)(2,1)} async-done(((bf16[128,128,128]{2,1,0:T(8,128)(2,1)}), bf16[128,128,128]{2,1,0:T(8,128)(2,1)}, u32[]{:S(2)}, u32[]{:S(2)}) %all-to-all-start.1) | async-done | bytes 4194336 | tf_op jit(solution)/shard_map/all_to_all | solution.py:222
  94.2 0.0 copy-done.15
  94.2 0.0 copy-start.12
  94.2 1.0 copy-done.12
  95.2 3.7 %level0.1 = (f32[4,128,128]{2,1,0:T(8,128)S(1)}, f32[2,128,128]{2,1,0:T(8,128)S(1)}, bf16[64,128,128]{2,1,0:T(8,128)(2,1)S(1)}) custom-call(s32[560]{0:T(1024)S(1)} %copy-done.15, s32[240]{0:T(256)S(1)} %bitcast.7, bf16[128,128,128]{2,1,0:T(8,128)(2,1)} %all-to-all-done.1.received_ref, bf16[560,128,128]{2,1,0:T(8,128)(2,1)} %panels_ref.13, ...), custom_call_target="tpu_custom_call" | custom-call | tf_op jit(solution)/shard_map/level0/pallas_call | solution.py:233
  98.9 0.0 copy-start.9
  98.9 1.3 copy-done.9
  100.2 4.4 %all-to-all-start.2 = ((bf16[64,128,128]{2,1,0:T(8,128)(2,1)}), bf16[64,128,128]{2,1,0:T(8,128)(2,1)S(1)}, u32[]{:S(2)}, u32[]{:S(2)}) async-start(bf16[64,128,128]{2,1,0:T(8,128)(2,1)} %copy-done.9), calls=%async_computation.2 | async-start | bytes 4194304 | tf_op jit(solution)/shard_map/all_to_all | solution.py:222
  104.6 0.0 copy-start.10
  104.6 1.6 copy-done.10
  106.2 5.7 %leaf0.1.right_ref = f32[32,128,128]{2,1,0:T(8,128)S(1)} custom-call(s32[560]{0:T(1024)S(1)} %copy-done.15, bf16[128,128,128]{2,1,0:T(8,128)(2,1)} %all-to-all-done.1.received_ref, bf16[560,128,128]{2,1,0:T(8,128)(2,1)} %panels_ref.13, f32[32,128,128]{2,1,0:T(8,128)S(1)} %bitcast.5), custom_call_target="tpu_custom_call" | custom-call | tf_op jit(solution)/shard_map/leaf0/pallas_call | solution.py:266
  112.0 0.0 copy-start.6
  112.0 1.3 copy-done.6
  113.3 20.9 %all-to-all-done.2.received_ref = bf16[64,128,128]{2,1,0:T(8,128)(2,1)S(1)} async-done(((bf16[64,128,128]{2,1,0:T(8,128)(2,1)}), bf16[64,128,128]{2,1,0:T(8,128)(2,1)S(1)}, u32[]{:S(2)}, u32[]{:S(2)}) %all-to-all-start.2) | async-done | bytes 2097184 | tf_op jit(solution)/shard_map/all_to_all | solution.py:222
  134.2 0.0 copy-start.2
  134.2 3.3 %level1.1 = (f32[2,128,128]{2,1,0:T(8,128)S(1)}, f32[2,128,128]{2,1,0:T(8,128)S(1)}, bf16[32,128,128]{2,1,0:T(8,128)(2,1)}) custom-call(s32[560]{0:T(1024)S(1)} %copy-done.15, s32[240]{0:T(256)S(1)} %bitcast.8, bf16[64,128,128]{2,1,0:T(8,128)(2,1)S(1)} %all-to-all-done.2.received_ref, bf16[560,128,128]{2,1,0:T(8,128)(2,1)} %panels_ref.13, ...), custom_call_target="tpu_custom_call" | custom-call | tf_op jit(solution)/shard_map/level1/pallas_call | solution.py:233
  137.5 0.0 copy-done.2
  137.5 5.3 %all-to-all-start.3 = ((bf16[32,128,128]{2,1,0:T(8,128)(2,1)}), bf16[32,128,128]{2,1,0:T(8,128)(2,1)}, u32[]{:S(2)}, u32[]{:S(2)}) async-start(bf16[32,128,128]{2,1,0:T(8,128)(2,1)} %get-tuple-element.25), calls=%async_computation.3 | async-start | bytes 2097152 | tf_op jit(solution)/shard_map/all_to_all | solution.py:222
  142.8 0.0 copy-start.3
  142.8 1.6 copy-done.3
  144.4 0.0 copy-start.1
  144.4 5.0 %leaf1.1.right_ref = f32[32,128,128]{2,1,0:T(8,128)S(1)} custom-call(s32[560]{0:T(1024)S(1)} %copy-done.15, bf16[64,128,128]{2,1,0:T(8,128)(2,1)S(1)} %copy-done.3, bf16[560,128,128]{2,1,0:T(8,128)(2,1)} %panels_ref.13, f32[32,128,128]{2,1,0:T(8,128)} %copy-done.6), custom_call_target="tpu_custom_call" | custom-call | tf_op jit(solution)/shard_map/leaf1/pallas_call | solution.py:266
  149.3 0.0 copy-start.4
  149.4 1.3 copy-done.4
  150.7 8.2 %all-to-all-done.3.received_ref = bf16[32,128,128]{2,1,0:T(8,128)(2,1)} async-done(((bf16[32,128,128]{2,1,0:T(8,128)(2,1)}), bf16[32,128,128]{2,1,0:T(8,128)(2,1)}, u32[]{:S(2)}, u32[]{:S(2)}) %all-to-all-start.3) | async-done | bytes 1048608 | tf_op jit(solution)/shard_map/all_to_all | solution.py:222
  158.9 0.0 copy-done.1
  158.9 2.5 %level2.1 = (f32[2,128,128]{2,1,0:T(8,128)}, f32[2,128,128]{2,1,0:T(8,128)S(1)}, bf16[16,128,128]{2,1,0:T(8,128)(2,1)S(1)}) custom-call(s32[560]{0:T(1024)S(1)} %copy-done.15, s32[240]{0:T(256)S(1)} %bitcast.9, bf16[32,128,128]{2,1,0:T(8,128)(2,1)} %all-to-all-done.3.received_ref, bf16[560,128,128]{2,1,0:T(8,128)(2,1)} %panels_ref.13, ...), custom_call_target="tpu_custom_call" | custom-call | tf_op jit(solution)/shard_map/level2/pallas_call | solution.py:233
  161.4 0.0 copy-start.14
  161.4 0.8 copy-done.14
  162.2 0.0 copy-start.16
  162.2 0.7 copy-done.16
  162.9 4.7 %all-to-all-start.4 = ((bf16[16,128,128]{2,1,0:T(8,128)(2,1)}), bf16[16,128,128]{2,1,0:T(8,128)(2,1)S(1)}, u32[]{:S(2)}, u32[]{:S(2)}) async-start(bf16[16,128,128]{2,1,0:T(8,128)(2,1)} %copy-done.14), calls=%async_computation.4 | async-start | bytes 1048576 | tf_op jit(solution)/shard_map/all_to_all | solution.py:222
  167.6 0.0 copy-start.5
  167.6 1.6 copy-done.5
  169.2 0.0 copy-start.17
  169.2 4.8 %leaf2.1.right_ref = f32[32,128,128]{2,1,0:T(8,128)S(1)} custom-call(s32[560]{0:T(1024)S(1)} %copy-done.15, bf16[32,128,128]{2,1,0:T(8,128)(2,1)} %all-to-all-done.3.received_ref, bf16[560,128,128]{2,1,0:T(8,128)(2,1)} %panels_ref.13, f32[32,128,128]{2,1,0:T(8,128)S(1)} %copy-done.5), custom_call_target="tpu_custom_call" | custom-call | tf_op jit(solution)/shard_map/leaf2/pallas_call | solution.py:266
  173.9 0.0 copy-start.7
  173.9 1.3 copy-done.7
  175.3 0.0 copy-done.17
  175.3 0.8 pad_maximum_fusion
  176.1 1.5 all-to-all-done.4.received_ref
  177.6 0.0 copy-start.8
  177.6 1.6 copy-done.8
  179.2 6.8 %leaf3.1 = f32[32,128,128]{2,1,0:T(8,128)} custom-call(s32[560]{0:T(1024)S(1)} %copy-done.15, bf16[16,128,128]{2,1,0:T(8,128)(2,1)S(1)} %all-to-all-done.4.received_ref, bf16[560,128,128]{2,1,0:T(8,128)(2,1)} %panels_ref.13, f32[32,128,128]{2,1,0:T(8,128)S(1)} %copy-done.8, f32[40,128,128]{2,1,0:T(8,128)S(1)} %copy-done.1), custom_call_target="tpu_custom_call" | custom-call | tf_op jit(solution)/shard_map/leaf3/pallas_call | solution.py:266
Async XLA Ops:
  0.6 31.8 %copy-start = (f32[40,128,128]{2,1,0:T(8,128)S(1)}, f32[40,128,128]{2,1,0:T(8,128)}, u32[]{:S(2)}) copy-start(f32[40,128,128]{2,1,0:T(8,128)} %diag_ref.9) | copy-start | bytes 7864324
  0.6 1.2 copy-start.13
  1.8 0.7 copy-start.19
  2.5 29.9 %copy-start.18 = (s32[1,240]{1,0:T(1,128)S(1)}, s32[1,240]{1,0:T(1,128)}, u32[]{:S(2)}) copy-start(s32[1,240]{1,0:T(1,128)} %param.13) | copy-start | bytes 2884
  36.0 58.2 %copy-start.15 = (s32[560]{0:T(1024)S(1)}, s32[560]{0:T(1024)}, u32[]{:S(2)}) copy-start(s32[560]{0:T(1024)} %from_ref.13) | copy-start | bytes 6724
  36.0 58.2 %all-to-all-start.1 = ((bf16[128,128,128]{2,1,0:T(8,128)(2,1)}), bf16[128,128,128]{2,1,0:T(8,128)(2,1)}, u32[]{:S(2)}, u32[]{:S(2)}) async-start(bf16[128,128,128]{2,1,0:T(8,128)(2,1)} %get-tuple-element.19), calls=%async_computation.1 | async-start | bytes 8388608 | tf_op jit(solution)/shard_map/all_to_all | solution.py:222
  41.7 0.7 copy-start.11
  94.2 1.0 copy-start.12
  98.9 1.3 copy-start.9
  100.2 34.0 %all-to-all-start.2 = ((bf16[64,128,128]{2,1,0:T(8,128)(2,1)}), bf16[64,128,128]{2,1,0:T(8,128)(2,1)S(1)}, u32[]{:S(2)}, u32[]{:S(2)}) async-start(bf16[64,128,128]{2,1,0:T(8,128)(2,1)} %copy-done.9), calls=%async_computation.2 | async-start | bytes 4194304 | tf_op jit(solution)/shard_map/all_to_all | solution.py:222
  104.6 1.6 copy-start.10
  112.0 1.3 copy-start.6
  134.2 3.3 %copy-start.2 = (bf16[64,128,128]{2,1,0:T(8,128)(2,1)}, bf16[64,128,128]{2,1,0:T(8,128)(2,1)S(1)}, u32[]{:S(2)}) copy-start(bf16[64,128,128]{2,1,0:T(8,128)(2,1)S(1)} %all-to-all-done.2.received_ref) | copy-start | bytes 6291460
  137.5 21.4 %all-to-all-start.3 = ((bf16[32,128,128]{2,1,0:T(8,128)(2,1)}), bf16[32,128,128]{2,1,0:T(8,128)(2,1)}, u32[]{:S(2)}, u32[]{:S(2)}) async-start(bf16[32,128,128]{2,1,0:T(8,128)(2,1)} %get-tuple-element.25), calls=%async_computation.3 | async-start | bytes 2097152 | tf_op jit(solution)/shard_map/all_to_all | solution.py:222
  142.8 1.6 copy-start.3
  144.4 14.5 %copy-start.1 = (f32[40,128,128]{2,1,0:T(8,128)S(1)}, f32[40,128,128]{2,1,0:T(8,128)}, u32[]{:S(2)}) copy-start(f32[40,128,128]{2,1,0:T(8,128)} %diag_ref.9) | copy-start | bytes 7864324
  149.3 1.3 copy-start.4
  161.4 0.8 copy-start.14
  162.2 0.7 copy-start.16
  162.9 14.7 %all-to-all-start.4 = ((bf16[16,128,128]{2,1,0:T(8,128)(2,1)}), bf16[16,128,128]{2,1,0:T(8,128)(2,1)S(1)}, u32[]{:S(2)}, u32[]{:S(2)}) async-start(bf16[16,128,128]{2,1,0:T(8,128)(2,1)} %copy-done.14), calls=%async_computation.4 | async-start | bytes 1048576 | tf_op jit(solution)/shard_map/all_to_all | solution.py:222
  167.6 1.6 copy-start.5
  169.2 6.1 %copy-start.17 = (f32[2,128,128]{2,1,0:T(8,128)S(1)}, f32[2,128,128]{2,1,0:T(8,128)}, u32[]{:S(2)}) copy-start(f32[2,128,128]{2,1,0:T(8,128)} %copy-done.16) | copy-start | bytes 393220
  173.9 1.3 copy-start.7
  177.6 1.6 copy-start.8

commit v3 on v2

--- a/solution.py
+++ b/solution.py
@@ -14,7 +14,9 @@
 LEVELS = 4
 AXES = ("leaf", "panel")
 LEAF_STEP = 8
-VMEM = pltpu.CompilerParams(vmem_limit_bytes=48 * 1024 * 1024)
+LAST_STEP = 4
+PIECES = 4
+VMEM = pltpu.CompilerParams(vmem_limit_bytes=20 * 1024 * 1024)
 
 
 def whole():
@@ -96,16 +98,24 @@
     sent_ref[t] = solved.astype(jnp.bfloat16)
 
 
-def spread(send_offset, send_ref, sent_ref, buffer_ref):
-    for j in range(buffer_ref.shape[0]):
-        buffer_ref[j] = sent_ref[send_ref[send_offset + j]]
-
-
-def first_kernel(send_ref, arrived_ref, diag_ref, solved_ref, buffer_ref, sent_ref):
+def spread(send_offset, send_ref, sent_ref, made_ref, buffer_ref, done):
+    count = made_ref.shape[0] // PIECES
+    copies = []
+    for piece in range(PIECES):
+        for j in range(piece * count, (piece + 1) * count):
+            made_ref[j] = sent_ref[send_ref[send_offset + j]]
+        part = pl.ds(piece * count, count)
+        copies.append(pltpu.make_async_copy(made_ref.at[part], buffer_ref.at[part], done.at[piece]))
+        copies[-1].start()
+    return copies
+
+
+def first_kernel(send_ref, arrived_ref, diag_ref, solved_ref, buffer_ref, sent_ref, made_ref, done):
     [right] = order_rows(arrived_ref, [0])
     for t in range(TS):
         finish(right[t * BS : (t + 1) * BS], diag_ref, t, solved_ref, sent_ref)
-    spread(0, send_ref, sent_ref, buffer_ref)
+    for copy in spread(0, send_ref, sent_ref, made_ref, buffer_ref, done):
+        copy.wait()
 
 
 def order_kernel(arrived_ref, out_ref):
@@ -114,54 +124,69 @@
             out_ref[i * TS + t] = right[t * BS : (t + 1) * BS]
 
 
-def tile_update(from_ref, base, panels_ref, local, received_ref):
+def tile_update(panels_ref, local, tile):
     left = jnp.concatenate([panels_ref[local + k] for k in range(KP)], axis=1)
-    right = jnp.concatenate([received_ref[from_ref[base + k]] for k in range(KP)], axis=0)
+    right = jnp.concatenate([tile(k) for k in range(KP)], axis=0)
     return jnp.dot(left, right, preferred_element_type=jnp.float32)
 
 
 def level_kernel(
     offset, send_offset, from_ref, send_ref, received_ref, panels_ref, rights_ref, diag_ref,
-    rest_ref, solved_ref, buffer_ref, sent_ref,
+    rest_ref, solved_ref, buffer_ref, near_ref, sent_ref, made_ref, arrived, done,
 ):
+    tiles = rights_ref.shape[0]
+    fetches = []
+    for e in range(tiles * KP):
+        fetches.append(
+            pltpu.make_async_copy(
+                received_ref.at[from_ref[offset + e]], near_ref.at[e], arrived.at[e]
+            )
+        )
+        fetches[-1].start()
+
+    def right_side(d):
+        for k in range(KP):
+            fetches[KP * d + k].wait()
+        return rights_ref[d] - tile_update(panels_ref, KP * d, lambda k: near_ref[KP * d + k])
+
     for d in range(TS):
-        right = rights_ref[d] - tile_update(
-            from_ref, offset + KP * d, panels_ref, KP * d, received_ref
+        finish(right_side(d), diag_ref, d, solved_ref, sent_ref)
+    copies = spread(send_offset, send_ref, sent_ref, made_ref, buffer_ref, done)
+    for d in range(TS, tiles):
+        rest_ref[d - TS] = right_side(d)
+    for copy in copies:
+        copy.wait()
+
+
+def leaf_update(offset, from_ref, received_ref, panels_ref, right_ref):
+    count = right_ref.shape[0]
+    first = offset + pl.program_id(0) * count * KP
+    for d in range(count):
+        yield right_ref[d] - tile_update(
+            panels_ref, KP * d, lambda k: received_ref[from_ref[first + KP * d + k]]
         )
-        finish(right, diag_ref, d, solved_ref, sent_ref)
-    spread(send_offset, send_ref, sent_ref, buffer_ref)
-    for d in range(TS, rights_ref.shape[0]):
-        rest_ref[d - TS] = rights_ref[d] - tile_update(
-            from_ref, offset + KP * d, panels_ref, KP * d, received_ref
-        )
 
 
 def leaf_kernel(offset, from_ref, received_ref, panels_ref, right_ref, out_ref):
-    first = offset + pl.program_id(0) * LEAF_STEP * KP
-    for d in range(LEAF_STEP):
-        out_ref[d] = right_ref[d] - tile_update(
-            from_ref, first + KP * d, panels_ref, KP * d, received_ref
-        )
+    for d, right in enumerate(leaf_update(offset, from_ref, received_ref, panels_ref, right_ref)):
+        out_ref[d] = right
 
 
 def last_kernel(offset, from_ref, received_ref, panels_ref, right_ref, diag_ref, out_ref):
-    first = offset + pl.program_id(0) * LEAF_STEP * KP
-    for d in range(LEAF_STEP):
-        right = right_ref[d] - tile_update(
-            from_ref, first + KP * d, panels_ref, KP * d, received_ref
-        )
+    rights = list(leaf_update(offset, from_ref, received_ref, panels_ref, right_ref))
+    for d, right in enumerate(rights):
         out_ref[d] = solve(diag_ref[d], right)
 
 
-def entries_block(offset, count, grid):
-    if grid:
-        return pl.BlockSpec(
-            (pl.Element(count), pl.Element(BS), pl.Element(BS)),
-            lambda i, *_: (offset + i * count, 0, 0),
-        )
+def entries_block(offset, count):
     return pl.BlockSpec(
-        (pl.Element(count), pl.Element(BS), pl.Element(BS)), lambda i, *_: (offset, 0, 0)
-    )
+        (pl.Element(count), pl.Element(BS), pl.Element(BS)),
+        lambda i, *_: (offset + i * count, 0, 0),
+    )
+
+
+def streamed(x):
+    return pltpu.with_memory_space_constraint(x, pltpu.HBM)
 
 
 def f32(*shape):
@@ -189,19 +214,27 @@
     )(elimination_row.reshape(1, rows), noise_parts)
     arrived = lax.all_to_all(outgoing, AXES, 0, 0, tiled=True)
     send_row = send_lists[0]
+    stream = streamed(panels)
     solved, buffer = pl.pallas_call(
         first_kernel,
         grid_spec=pltpu.PrefetchScalarGridSpec(
             num_scalar_prefetch=1,
             grid=(1,),
-            in_specs=[whole(), entries_block(0, TS, False)],
-            out_specs=(whole(), whole()),
-            scratch_shapes=[pltpu.VMEM((TS, BS, rhs), jnp.bfloat16)],
+            in_specs=[whole(), whole()],
+            out_specs=(entries_block(0, TS), pl.BlockSpec(memory_space=pltpu.HBM)),
+            scratch_shapes=[
+                pltpu.VMEM((TS, BS, rhs), jnp.bfloat16),
+                pltpu.VMEM((owners, BS, rhs), jnp.bfloat16),
+                pltpu.SemaphoreType.DMA((PIECES,)),
+            ],
         ),
-        out_shape=(f32(TS, BS, rhs), b16(owners, BS, rhs)),
+        out_shape=(
+            pltpu.HBM((TS, BS, rhs), jnp.float32),
+            pltpu.HBM((owners, BS, rhs), jnp.bfloat16),
+        ),
         compiler_params=VMEM,
         name="first",
-    )(send_row, arrived, diag_inverse)
+    )(send_row, arrived, diag_inverse[:TS])
     rights = pl.pallas_call(
         order_kernel,
         out_shape=f32((LEVELS - 1) * TS, BS, rhs),
@@ -229,6 +262,7 @@
         leaf_offset = offset + KP * sep_tiles
         if tree_level < LEVELS - 1:
             first_diag = (tree_level + 1) * TS
+            level_diag = diag_inverse[first_diag : first_diag + TS]
             rest_tiles = max(sep_tiles - TS, TS)
             rights, solved, buffer = pl.pallas_call(
                 functools.partial(level_kernel, offset, send_offset),
@@ -236,42 +270,53 @@
                     num_scalar_prefetch=2,
                     grid=(1,),
                     in_specs=[
+                        pl.BlockSpec(memory_space=pl.ANY),
                         whole(),
-                        entries_block(offset, KP * sep_tiles, False),
                         whole(),
-                        entries_block(first_diag, TS, False),
+                        whole(),
                     ],
-                    out_specs=(whole(), whole(), whole()),
-                    scratch_shapes=[pltpu.VMEM((TS, BS, rhs), jnp.bfloat16)],
+                    out_specs=(
+                        whole(),
+                        entries_block(0, TS),
+                        pl.BlockSpec(memory_space=pltpu.HBM),
+                    ),
+                    scratch_shapes=[
+                        pltpu.VMEM((KP * sep_tiles, BS, rhs), jnp.bfloat16),
+                        pltpu.VMEM((TS, BS, rhs), jnp.bfloat16),
+                        pltpu.VMEM((group // 2, BS, rhs), jnp.bfloat16),
+                        pltpu.SemaphoreType.DMA((KP * sep_tiles,)),
+                        pltpu.SemaphoreType.DMA((PIECES,)),
+                    ],
                 ),
                 out_shape=(
                     f32(rest_tiles, BS, rhs),
-                    f32(TS, BS, rhs),
-                    b16(group // 2, BS, rhs),
+                    pltpu.HBM((TS, BS, rhs), jnp.float32),
+                    pltpu.HBM((group // 2, BS, rhs), jnp.bfloat16),
                 ),
                 compiler_params=VMEM,
                 name=f"level{tree_level}",
-            )(panel_from, send_row, received, panels, rights, diag_inverse)
+            )(panel_from, send_row, received, panels[offset : offset + KP * sep_tiles], rights, level_diag)
             all_solved.append(solved)
         last = tree_level == LEVELS - 1
+        step = LAST_STEP if last else LEAF_STEP
         in_specs = [
             whole(),
-            entries_block(leaf_offset, KP * LEAF_STEP, True),
-            entries_block(0, LEAF_STEP, True),
+            entries_block(leaf_offset, KP * step),
+            entries_block(0, step),
         ]
-        operands = [panel_from, received, panels, leaf_right]
+        operands = [panel_from, received, stream, streamed(leaf_right)]
         if last:
-            in_specs.append(entries_block(LEVELS * TS, LEAF_STEP, True))
-            operands.append(diag_inverse)
+            in_specs.append(entries_block(LEVELS * TS, step))
+            operands.append(streamed(diag_inverse))
         leaf_right = pl.pallas_call(
             functools.partial(last_kernel if last else leaf_kernel, leaf_offset),
             grid_spec=pltpu.PrefetchScalarGridSpec(
                 num_scalar_prefetch=1,
-                grid=(TL // LEAF_STEP,),
+                grid=(TL // step,),
                 in_specs=in_specs,
-                out_specs=pl.BlockSpec((LEAF_STEP, BS, rhs), lambda i, *_: (i, 0, 0)),
+                out_specs=pl.BlockSpec((step, BS, rhs), lambda i, *_: (i, 0, 0)),
             ),
-            out_shape=f32(TL, BS, rhs),
+            out_shape=pltpu.HBM((TL, BS, rhs), jnp.float32),
             compiler_params=VMEM,
             name=f"leaf{tree_level}",
         )(*operands)

time: 187 us -> 189 us (1.011)
  blocking collectives: 28.2 us -> 0 us
  waiting for transfers between devices: 82.3 us -> 101 us
  starting transfers between devices: 19.3 us -> 30.1 us
  Pallas kernels: 37.7 us -> 47.4 us
  local copies, waits for them, and re-layouts: 16.7 us -> 7.68 us
    all_to_all x1 -> x0, blocking collectives: 28.2 us -> none  [per_device(): arrived = lax.all_to_all(outgoing, AXES, 0, 0, tiled=True)]
    all_to_all x0 -> x1, waiting for transfers between devices: none -> 15.8 us  [per_device(): arrived = lax.all_to_all(outgoing, AXES, 0, 0, tiled=True)]
    unnamed x40 -> x20, local copies, waits for them, and re-layouts: 16.7 us -> 3.3 us
    all_to_all x0 -> x1, starting transfers between devices: none -> 11.5 us  [per_device(): arrived = lax.all_to_all(outgoing, AXES, 0, 0, tiled=True)]
    pallas_call x4, Pallas kernels: 22.2 us -> 28.4 us  [per_device(): pl.pallas_call(functools.partial(last_kernel if last else leaf_kernel, le...]
    slice x0 -> x4, local copies, waits for them, and re-layouts: none -> 4.38 us  [the longest x3 3.24 us: per_device(): panels[offset:offset + KP * sep_tiles]]
    all_to_all x4, waiting for transfers between devices: 82.3 us -> 84.8 us  [per_device(): lax.all_to_all(buffer, AXES, 0, 0, axis_index_groups=groups, tiled=True)]
    pallas_call x3, Pallas kernels: 9.49 us -> 11.7 us  [per_device(): pl.pallas_call(functools.partial(level_kernel, offset, send_offset), grid...]
  transfers between devices with their start and end apart: 4 -> 5, of which waited for: 4 -> 5; matrix products, arithmetic and copies ran while one was open for 0% -> 3% of each run, Pallas kernels for 9% -> 11%
where the time goes in v3:
time: 189 us; the launch traced here: 187 us
  waiting for transfers between devices  101 us (53%)
  Pallas kernels  47.4 us (25%)
  starting transfers between devices  30.1 us (16%)
  local copies, waits for them, and re-layouts  7.68 us (4%)
    all_to_all x4, waiting for transfers between devices, per_device(): lax.all_to_all(buffer, AXES, 0, 0, axis_index_groups=groups, tiled=True)  84.8 us
    pallas_call x4, Pallas kernels, per_device(): pl.pallas_call(functools.partial(last_kernel if last else leaf_kernel, le...  28.4 us
    all_to_all x4, starting transfers between devices, per_device(): lax.all_to_all(buffer, AXES, 0, 0, axis_index_groups=groups, tiled=True)  18.6 us
    all_to_all x1, waiting for transfers between devices, per_device(): arrived = lax.all_to_all(outgoing, AXES, 0, 0, tiled=True)  15.8 us
    pallas_call x3, Pallas kernels, per_device(): pl.pallas_call(functools.partial(level_kernel, offset, send_offset), grid...  11.7 us
    all_to_all x1, starting transfers between devices, per_device(): arrived = lax.all_to_all(outgoing, AXES, 0, 0, tiled=True)  11.5 us
    pallas_call x1, Pallas kernels, per_device(): pl.pallas_call(first_kernel, grid_spec=pltpu.PrefetchScalarGridSpec(num_s...  4.02 us
  transfers between devices with their start and end apart: 5, of which 5 were waited for; matrix products, arithmetic and copies ran while one was open for 3% of the time, Pallas kernels for 11%

profile of v3, /device:TPU:1, one launch (start us, length us, event | category | flops | bytes accessed | tf_op | source)
XLA Modules:
  0.0 187.4 jit_solution(15943277479103949154)
XLA Ops:
  0.6 0.0 copy-start.4
  0.6 0.0 copy-start
  0.6 1.0 copy-done
  1.7 0.0 copy-start.5
  1.7 0.7 copy-done.5
  2.4 2.6 %pack.1 = bf16[128,8,384]{2,1,0:T(8,128)(2,1)} custom-call(s32[1,1024]{1,0:T(1,128)S(1)} %bitcast.9, f32[1024,128]{1,0:T(8,128)S(1)} %copy-done), custom_call_target="tpu_custom_call" | custom-call | tf_op jit(solution)/shard_map/pack/pallas_call | solution.py:207
  4.9 11.5 %all-to-all-start = ((bf16[128,8,384]{2,1,0:T(8,128)(2,1)}), bf16[128,8,384]{2,1,0:T(8,128)(2,1)S(1)}, u32[]{:S(2)}, u32[]{:S(2)}) async-start(bf16[128,8,384]{2,1,0:T(8,128)(2,1)} %pack.1), calls=%async_computation | async-start | bytes 1572864 | tf_op jit(solution)/shard_map/all_to_all | solution.py:215
  16.4 1.1 fusion
  17.6 15.8 %all-to-all-done.arrived_ref = bf16[128,8,384]{2,1,0:T(8,128)(2,1)S(1)} async-done(((bf16[128,8,384]{2,1,0:T(8,128)(2,1)}), bf16[128,8,384]{2,1,0:T(8,128)(2,1)S(1)}, u32[]{:S(2)}, u32[]{:S(2)}) %all-to-all-start) | async-done | bytes 786464 | tf_op jit(solution)/shard_map/all_to_all | solution.py:215
  33.4 0.0 copy-done.4
  33.4 4.0 %first.1 = (f32[2,128,128]{2,1,0:T(8,128)}, bf16[128,128,128]{2,1,0:T(8,128)(2,1)}) custom-call(s32[240]{0:T(256)S(1)} %bitcast.5, bf16[128,8,384]{2,1,0:T(8,128)(2,1)S(1)} %all-to-all-done.arrived_ref, f32[2,128,128]{2,1,0:T(8,128)S(1)} %get-tuple-element.37.diag_ref), custom_call_target="tpu_custom_call" | custom-call | tf_op jit(solution)/shard_map/first/pallas_call | solution.py:218
  37.4 4.8 %all-to-all-start.1 = ((bf16[128,128,128]{2,1,0:T(8,128)(2,1)}), bf16[128,128,128]{2,1,0:T(8,128)(2,1)}, u32[]{:S(2)}, u32[]{:S(2)}) async-start(bf16[128,128,128]{2,1,0:T(8,128)(2,1)} %get-tuple-element.19), calls=%async_computation.1 | async-start | bytes 8388608 | tf_op jit(solution)/shard_map/all_to_all | solution.py:255
  42.2 0.0 copy-start.1
  42.3 1.2 slice.22.panels_ref
  43.4 0.7 order.1.rights_ref
  44.2 51.3 %all-to-all-done.1.received_ref = bf16[128,128,128]{2,1,0:T(8,128)(2,1)} async-done(((bf16[128,128,128]{2,1,0:T(8,128)(2,1)}), bf16[128,128,128]{2,1,0:T(8,128)(2,1)}, u32[]{:S(2)}, u32[]{:S(2)}) %all-to-all-start.1) | async-done | bytes 4194336 | tf_op jit(solution)/shard_map/all_to_all | solution.py:255
  95.5 0.0 copy-done.1
  95.5 4.4 %level0.1 = (f32[4,128,128]{2,1,0:T(8,128)S(1)}, f32[2,128,128]{2,1,0:T(8,128)}, bf16[64,128,128]{2,1,0:T(8,128)(2,1)}) custom-call(s32[560]{0:T(1024)S(1)} %copy-done.1, s32[240]{0:T(256)S(1)} %bitcast.6, bf16[128,128,128]{2,1,0:T(8,128)(2,1)} %all-to-all-done.1.received_ref, bf16[24,128,128]{2,1,0:T(8,128)(2,1)S(1)} %slice.22.panels_ref, ...), custom_call_target="tpu_custom_call" | custom-call | tf_op jit(solution)/shard_map/level0/pallas_call | solution.py:267
  99.9 4.4 %all-to-all-start.2 = ((bf16[64,128,128]{2,1,0:T(8,128)(2,1)}), bf16[64,128,128]{2,1,0:T(8,128)(2,1)S(1)}, u32[]{:S(2)}, u32[]{:S(2)}) async-start(bf16[64,128,128]{2,1,0:T(8,128)(2,1)} %get-tuple-element.21), calls=%async_computation.2 | async-start | bytes 4194304 | tf_op jit(solution)/shard_map/all_to_all | solution.py:255
  104.4 1.1 slice.24.panels_ref
  105.4 7.3 %leaf0.1.right_ref = f32[32,128,128]{2,1,0:T(8,128)} custom-call(s32[560]{0:T(1024)S(1)} %copy-done.1, bf16[128,128,128]{2,1,0:T(8,128)(2,1)} %all-to-all-done.1.received_ref, bf16[560,128,128]{2,1,0:T(8,128)(2,1)} %panels_ref.7, f32[32,128,128]{2,1,0:T(8,128)} %bitcast.10), custom_call_target="tpu_custom_call" | custom-call | tf_op jit(solution)/shard_map/leaf0/pallas_call | solution.py:311
  112.7 21.2 %all-to-all-done.2.received_ref = bf16[64,128,128]{2,1,0:T(8,128)(2,1)S(1)} async-done(((bf16[64,128,128]{2,1,0:T(8,128)(2,1)}), bf16[64,128,128]{2,1,0:T(8,128)(2,1)S(1)}, u32[]{:S(2)}, u32[]{:S(2)}) %all-to-all-start.2) | async-done | bytes 2097184 | tf_op jit(solution)/shard_map/all_to_all | solution.py:255
  133.9 3.9 %level1.1 = (f32[2,128,128]{2,1,0:T(8,128)S(1)}, f32[2,128,128]{2,1,0:T(8,128)}, bf16[32,128,128]{2,1,0:T(8,128)(2,1)}) custom-call(s32[560]{0:T(1024)S(1)} %copy-done.1, s32[240]{0:T(256)S(1)} %bitcast.7, bf16[64,128,128]{2,1,0:T(8,128)(2,1)S(1)} %all-to-all-done.2.received_ref, bf16[16,128,128]{2,1,0:T(8,128)(2,1)S(1)} %slice.24.panels_ref, ...), custom_call_target="tpu_custom_call" | custom-call | tf_op jit(solution)/shard_map/level1/pallas_call | solution.py:267
  137.8 0.0 copy-start.2
  137.9 0.6 copy-done.2
  138.5 4.6 %all-to-all-start.3 = ((bf16[32,128,128]{2,1,0:T(8,128)(2,1)}), bf16[32,128,128]{2,1,0:T(8,128)(2,1)S(1)}, u32[]{:S(2)}, u32[]{:S(2)}) async-start(bf16[32,128,128]{2,1,0:T(8,128)(2,1)} %get-tuple-element.25), calls=%async_computation.3 | async-start | bytes 2097152 | tf_op jit(solution)/shard_map/all_to_all | solution.py:255
  143.1 1.0 slice.26.panels_ref
  144.1 5.9 %leaf1.1.right_ref = f32[32,128,128]{2,1,0:T(8,128)} custom-call(s32[560]{0:T(1024)S(1)} %copy-done.1, bf16[64,128,128]{2,1,0:T(8,128)(2,1)S(1)} %all-to-all-done.2.received_ref, bf16[560,128,128]{2,1,0:T(8,128)(2,1)} %panels_ref.7, f32[32,128,128]{2,1,0:T(8,128)} %leaf0.1.right_ref), custom_call_target="tpu_custom_call" | custom-call | tf_op jit(solution)/shard_map/leaf1/pallas_call | solution.py:311
  150.0 9.2 %all-to-all-done.3.received_ref = bf16[32,128,128]{2,1,0:T(8,128)(2,1)S(1)} async-done(((bf16[32,128,128]{2,1,0:T(8,128)(2,1)}), bf16[32,128,128]{2,1,0:T(8,128)(2,1)S(1)}, u32[]{:S(2)}, u32[]{:S(2)}) %all-to-all-start.3) | async-done | bytes 1048608 | tf_op jit(solution)/shard_map/all_to_all | solution.py:255
  159.2 0.0 copy-start.3
  159.2 0.9 copy-done.3
  160.1 3.4 %level2.1 = (f32[2,128,128]{2,1,0:T(8,128)}, f32[2,128,128]{2,1,0:T(8,128)}, bf16[16,128,128]{2,1,0:T(8,128)(2,1)}) custom-call(s32[560]{0:T(1024)S(1)} %copy-done.1, s32[240]{0:T(256)S(1)} %bitcast.8, bf16[32,128,128]{2,1,0:T(8,128)(2,1)S(1)} %all-to-all-done.3.received_ref, bf16[8,128,128]{2,1,0:T(8,128)(2,1)S(1)} %slice.26.panels_ref, ...), custom_call_target="tpu_custom_call" | custom-call | tf_op jit(solution)/shard_map/level2/pallas_call | solution.py:267
  163.5 4.7 %all-to-all-start.4 = ((bf16[16,128,128]{2,1,0:T(8,128)(2,1)}), bf16[16,128,128]{2,1,0:T(8,128)(2,1)S(1)}, u32[]{:S(2)}, u32[]{:S(2)}) async-start(bf16[16,128,128]{2,1,0:T(8,128)(2,1)} %get-tuple-element.30), calls=%async_computation.4 | async-start | bytes 1048576 | tf_op jit(solution)/shard_map/all_to_all | solution.py:255
  168.2 0.0 copy-start.6
  168.2 0.0 copy-start.7
  168.2 0.0 copy-start.8
  168.2 0.0 copy-start.9
  168.2 5.9 %leaf2.1.right_ref = f32[32,128,128]{2,1,0:T(8,128)} custom-call(s32[560]{0:T(1024)S(1)} %copy-done.1, bf16[32,128,128]{2,1,0:T(8,128)(2,1)S(1)} %all-to-all-done.3.received_ref, bf16[560,128,128]{2,1,0:T(8,128)(2,1)} %panels_ref.7, f32[32,128,128]{2,1,0:T(8,128)} %leaf1.1.right_ref), custom_call_target="tpu_custom_call" | custom-call | tf_op jit(solution)/shard_map/leaf2/pallas_call | solution.py:311
  174.2 0.0 copy-done.6
  174.2 0.0 copy-done.7
  174.2 0.0 copy-done.8
  174.2 0.0 copy-done.9
  174.2 0.8 pad_maximum_fusion
  175.0 3.2 %all-to-all-done.4.received_ref = bf16[16,128,128]{2,1,0:T(8,128)(2,1)S(1)} async-done(((bf16[16,128,128]{2,1,0:T(8,128)(2,1)}), bf16[16,128,128]{2,1,0:T(8,128)(2,1)S(1)}, u32[]{:S(2)}, u32[]{:S(2)}) %all-to-all-start.4) | async-done | bytes 524320 | tf_op jit(solution)/shard_map/all_to_all | solution.py:255
  178.2 9.2 %leaf3.1 = f32[32,128,128]{2,1,0:T(8,128)} custom-call(s32[560]{0:T(1024)S(1)} %copy-done.1, bf16[16,128,128]{2,1,0:T(8,128)(2,1)S(1)} %all-to-all-done.4.received_ref, bf16[560,128,128]{2,1,0:T(8,128)(2,1)} %panels_ref.7, f32[32,128,128]{2,1,0:T(8,128)} %leaf2.1.right_ref, f32[40,128,128]{2,1,0:T(8,128)} %diag_ref.1), custom_call_target="tpu_custom_call" | custom-call | tf_op jit(solution)/shard_map/leaf3/pallas_call | solution.py:311
Async XLA Ops:
  0.6 32.8 %copy-start.4 = (s32[1,240]{1,0:T(1,128)S(1)}, s32[1,240]{1,0:T(1,128)}, u32[]{:S(2)}) copy-start(s32[1,240]{1,0:T(1,128)} %param.13) | copy-start | bytes 2884
  0.6 1.0 copy-start
  1.7 0.7 copy-start.5
  4.9 28.4 %all-to-all-start = ((bf16[128,8,384]{2,1,0:T(8,128)(2,1)}), bf16[128,8,384]{2,1,0:T(8,128)(2,1)S(1)}, u32[]{:S(2)}, u32[]{:S(2)}) async-start(bf16[128,8,384]{2,1,0:T(8,128)(2,1)} %pack.1), calls=%async_computation | async-start | bytes 1572864 | tf_op jit(solution)/shard_map/all_to_all | solution.py:215
  37.4 58.1 %all-to-all-start.1 = ((bf16[128,128,128]{2,1,0:T(8,128)(2,1)}), bf16[128,128,128]{2,1,0:T(8,128)(2,1)}, u32[]{:S(2)}, u32[]{:S(2)}) async-start(bf16[128,128,128]{2,1,0:T(8,128)(2,1)} %get-tuple-element.19), calls=%async_computation.1 | async-start | bytes 8388608 | tf_op jit(solution)/shard_map/all_to_all | solution.py:255
  42.2 53.2 %copy-start.1 = (s32[560]{0:T(1024)S(1)}, s32[560]{0:T(1024)}, u32[]{:S(2)}) copy-start(s32[560]{0:T(1024)} %from_ref.13) | copy-start | bytes 6724
  99.9 34.0 %all-to-all-start.2 = ((bf16[64,128,128]{2,1,0:T(8,128)(2,1)}), bf16[64,128,128]{2,1,0:T(8,128)(2,1)S(1)}, u32[]{:S(2)}, u32[]{:S(2)}) async-start(bf16[64,128,128]{2,1,0:T(8,128)(2,1)} %get-tuple-element.21), calls=%async_computation.2 | async-start | bytes 4194304 | tf_op jit(solution)/shard_map/all_to_all | solution.py:255
  137.8 0.6 copy-start.2
  138.5 20.7 %all-to-all-start.3 = ((bf16[32,128,128]{2,1,0:T(8,128)(2,1)}), bf16[32,128,128]{2,1,0:T(8,128)(2,1)S(1)}, u32[]{:S(2)}, u32[]{:S(2)}) async-start(bf16[32,128,128]{2,1,0:T(8,128)(2,1)} %get-tuple-element.25), calls=%async_computation.3 | async-start | bytes 2097152 | tf_op jit(solution)/shard_map/all_to_all | solution.py:255
  159.2 0.9 copy-start.3
  163.5 14.7 %all-to-all-start.4 = ((bf16[16,128,128]{2,1,0:T(8,128)(2,1)}), bf16[16,128,128]{2,1,0:T(8,128)(2,1)S(1)}, u32[]{:S(2)}, u32[]{:S(2)}) async-start(bf16[16,128,128]{2,1,0:T(8,128)(2,1)} %get-tuple-element.30), calls=%async_computation.4 | async-start | bytes 1048576 | tf_op jit(solution)/shard_map/all_to_all | solution.py:255
  168.2 6.0 %copy-start.6 = (f32[2,128,128]{2,1,0:T(8,128)S(1)}, f32[2,128,128]{2,1,0:T(8,128)}, u32[]{:S(2)}) copy-start(f32[2,128,128]{2,1,0:T(8,128)} %get-tuple-element.18) | copy-start | bytes 393220
  168.2 6.0 %copy-start.7 = (f32[2,128,128]{2,1,0:T(8,128)S(1)}, f32[2,128,128]{2,1,0:T(8,128)}, u32[]{:S(2)}) copy-start(f32[2,128,128]{2,1,0:T(8,128)} %get-tuple-element.20) | copy-start | bytes 393220
  168.2 6.0 %copy-start.8 = (f32[2,128,128]{2,1,0:T(8,128)S(1)}, f32[2,128,128]{2,1,0:T(8,128)}, u32[]{:S(2)}) copy-start(f32[2,128,128]{2,1,0:T(8,128)} %get-tuple-element.24) | copy-start | bytes 393220
  168.2 6.0 %copy-start.9 = (f32[2,128,128]{2,1,0:T(8,128)S(1)}, f32[2,128,128]{2,1,0:T(8,128)}, u32[]{:S(2)}) copy-start(f32[2,128,128]{2,1,0:T(8,128)} %get-tuple-element.29) | copy-start | bytes 393220

commit v4 on v2

--- a/solution.py
+++ b/solution.py
@@ -14,7 +14,13 @@
 LEVELS = 4
 AXES = ("leaf", "panel")
 LEAF_STEP = 8
-VMEM = pltpu.CompilerParams(vmem_limit_bytes=48 * 1024 * 1024)
+LAST_STEP = 8
+PIECES = 4
+VMEM = pltpu.CompilerParams(vmem_limit_bytes=16 * 1024 * 1024)
+
+
+def in_hbm():
+    return pl.BlockSpec(memory_space=pltpu.HBM)
 
 
 def whole():
@@ -96,16 +102,13 @@
     sent_ref[t] = solved.astype(jnp.bfloat16)
 
 
-def spread(send_offset, send_ref, sent_ref, buffer_ref):
-    for j in range(buffer_ref.shape[0]):
-        buffer_ref[j] = sent_ref[send_ref[send_offset + j]]
-
-
-def first_kernel(send_ref, arrived_ref, diag_ref, solved_ref, buffer_ref, sent_ref):
+def first_kernel(arrived_ref, diag_hbm, solved_ref, sent_ref, diag_ref, arrived):
+    fetch = pltpu.make_async_copy(diag_hbm.at[pl.ds(0, TS)], diag_ref, arrived)
+    fetch.start()
     [right] = order_rows(arrived_ref, [0])
+    fetch.wait()
     for t in range(TS):
         finish(right[t * BS : (t + 1) * BS], diag_ref, t, solved_ref, sent_ref)
-    spread(0, send_ref, sent_ref, buffer_ref)
 
 
 def order_kernel(arrived_ref, out_ref):
@@ -114,54 +117,113 @@
             out_ref[i * TS + t] = right[t * BS : (t + 1) * BS]
 
 
-def tile_update(from_ref, base, panels_ref, local, received_ref):
+def tile_update(panels_ref, local, tile):
     left = jnp.concatenate([panels_ref[local + k] for k in range(KP)], axis=1)
-    right = jnp.concatenate([received_ref[from_ref[base + k]] for k in range(KP)], axis=0)
+    right = jnp.concatenate([tile(k) for k in range(KP)], axis=0)
     return jnp.dot(left, right, preferred_element_type=jnp.float32)
 
 
+def start(*pairs):
+    copies = [pltpu.make_async_copy(*pair) for pair in pairs]
+    for copy in copies:
+        copy.start()
+    return copies
+
+
 def level_kernel(
-    offset, send_offset, from_ref, send_ref, received_ref, panels_ref, rights_ref, diag_ref,
-    rest_ref, solved_ref, buffer_ref, sent_ref,
+    offset, first_diag, from_hbm, received_ref, panels_hbm, rights_hbm, diag_hbm,
+    rest_ref, solved_ref, sent_ref,
+    from_ref, panels_ref, rights_ref, diag_ref, arrived, near_ref=None, near_arrived=None,
 ):
-    for d in range(TS):
+    tiles = rights_ref.shape[0]
+    copies = start(
+        (from_hbm, from_ref, arrived.at[0]),
+        (panels_hbm.at[pl.ds(offset, KP * tiles)], panels_ref, arrived.at[1]),
+        (rights_hbm, rights_ref, arrived.at[2]),
+        (diag_hbm.at[pl.ds(first_diag, TS)], diag_ref, arrived.at[3]),
+    )
+    if near_ref is not None:
+        count = received_ref.shape[0] // PIECES
+        for piece in range(PIECES):
+            part = pl.ds(piece * count, count)
+            copies += start((received_ref.at[part], near_ref.at[part], near_arrived.at[piece]))
+        received_ref = near_ref
+    for copy in copies:
+        copy.wait()
+    for d in range(tiles):
         right = rights_ref[d] - tile_update(
-            from_ref, offset + KP * d, panels_ref, KP * d, received_ref
-        )
-        finish(right, diag_ref, d, solved_ref, sent_ref)
-    spread(send_offset, send_ref, sent_ref, buffer_ref)
-    for d in range(TS, rights_ref.shape[0]):
-        rest_ref[d - TS] = rights_ref[d] - tile_update(
-            from_ref, offset + KP * d, panels_ref, KP * d, received_ref
-        )
+            panels_ref, KP * d, lambda k: received_ref[from_ref[offset + KP * d + k]]
+        )
+        if d < TS:
+            finish(right, diag_ref, d, solved_ref, sent_ref)
+        else:
+            rest_ref[d - TS] = right
 
 
 def leaf_kernel(offset, from_ref, received_ref, panels_ref, right_ref, out_ref):
     first = offset + pl.program_id(0) * LEAF_STEP * KP
     for d in range(LEAF_STEP):
         out_ref[d] = right_ref[d] - tile_update(
-            from_ref, first + KP * d, panels_ref, KP * d, received_ref
-        )
-
-
-def last_kernel(offset, from_ref, received_ref, panels_ref, right_ref, diag_ref, out_ref):
-    first = offset + pl.program_id(0) * LEAF_STEP * KP
-    for d in range(LEAF_STEP):
-        right = right_ref[d] - tile_update(
-            from_ref, first + KP * d, panels_ref, KP * d, received_ref
-        )
-        out_ref[d] = solve(diag_ref[d], right)
-
-
-def entries_block(offset, count, grid):
-    if grid:
-        return pl.BlockSpec(
-            (pl.Element(count), pl.Element(BS), pl.Element(BS)),
-            lambda i, *_: (offset + i * count, 0, 0),
-        )
+            panels_ref, KP * d, lambda k: received_ref[from_ref[first + KP * d + k]]
+        )
+
+
+def last_kernel(
+    offset, from_hbm, received_ref, panels_hbm, right_hbm, diag_hbm, out_hbm,
+    from_ref, panels_ref, right_ref, diag_ref, out_ref, arrived, left,
+):
+    parts = TL // LAST_STEP
+    [chosen] = start((from_hbm, from_ref, arrived.at[3 * parts]))
+    loads = []
+    for part in range(parts):
+        first = part * LAST_STEP
+        tiles = pl.ds(first, LAST_STEP)
+        entries = pl.ds(KP * first, KP * LAST_STEP)
+        loads.append(
+            start(
+                (
+                    panels_hbm.at[pl.ds(offset + KP * first, KP * LAST_STEP)],
+                    panels_ref.at[entries],
+                    arrived.at[3 * part],
+                ),
+                (right_hbm.at[tiles], right_ref.at[tiles], arrived.at[3 * part + 1]),
+                (
+                    diag_hbm.at[pl.ds(LEVELS * TS + first, LAST_STEP)],
+                    diag_ref.at[tiles],
+                    arrived.at[3 * part + 2],
+                ),
+            )
+        )
+    chosen.wait()
+    stores = []
+    for part in range(parts):
+        for copy in loads[part]:
+            copy.wait()
+        tiles = range(part * LAST_STEP, (part + 1) * LAST_STEP)
+        rights = [
+            right_ref[t]
+            - tile_update(
+                panels_ref, KP * t, lambda k: received_ref[from_ref[offset + KP * t + k]]
+            )
+            for t in tiles
+        ]
+        for t, right in zip(tiles, rights):
+            out_ref[t] = solve(diag_ref[t], right)
+        done = pl.ds(part * LAST_STEP, LAST_STEP)
+        stores += start((out_ref.at[done], out_hbm.at[done], left.at[part]))
+    for copy in stores:
+        copy.wait()
+
+
+def entries_block(offset, count):
     return pl.BlockSpec(
-        (pl.Element(count), pl.Element(BS), pl.Element(BS)), lambda i, *_: (offset, 0, 0)
-    )
+        (pl.Element(count), pl.Element(BS), pl.Element(BS)),
+        lambda i, *_: (offset + i * count, 0, 0),
+    )
+
+
+def streamed(x):
+    return pltpu.with_memory_space_constraint(x, pltpu.HBM)
 
 
 def f32(*shape):
@@ -189,19 +251,18 @@
     )(elimination_row.reshape(1, rows), noise_parts)
     arrived = lax.all_to_all(outgoing, AXES, 0, 0, tiled=True)
     send_row = send_lists[0]
-    solved, buffer = pl.pallas_call(
+    stream = streamed(panels)
+    diag_stream = streamed(diag_inverse)
+    from_stream = streamed(panel_from)
+    solved, sent = pl.pallas_call(
         first_kernel,
-        grid_spec=pltpu.PrefetchScalarGridSpec(
-            num_scalar_prefetch=1,
-            grid=(1,),
-            in_specs=[whole(), entries_block(0, TS, False)],
-            out_specs=(whole(), whole()),
-            scratch_shapes=[pltpu.VMEM((TS, BS, rhs), jnp.bfloat16)],
-        ),
-        out_shape=(f32(TS, BS, rhs), b16(owners, BS, rhs)),
+        out_shape=(f32(TS, BS, rhs), b16(TS, BS, rhs)),
+        in_specs=[whole(), in_hbm()],
+        out_specs=(whole(), whole()),
+        scratch_shapes=[pltpu.VMEM((TS, BS, BS), jnp.float32), pltpu.SemaphoreType.DMA],
         compiler_params=VMEM,
         name="first",
-    )(send_row, arrived, diag_inverse)
+    )(arrived, diag_stream)
     rights = pl.pallas_call(
         order_kernel,
         out_shape=f32((LEVELS - 1) * TS, BS, rhs),
@@ -219,6 +280,8 @@
         groups = [
             list(range(g * group, (g + 1) * group)) for g in range(owners // group)
         ]
+        picks = send_row[send_offset : send_offset + group]
+        buffer = jnp.where((picks == 0)[:, None, None], sent[0][None], sent[1][None])
         received = lax.all_to_all(
             buffer, AXES, 0, 0, axis_index_groups=groups, tiled=True
         )
@@ -230,51 +293,70 @@
         if tree_level < LEVELS - 1:
             first_diag = (tree_level + 1) * TS
             rest_tiles = max(sep_tiles - TS, TS)
-            rights, solved, buffer = pl.pallas_call(
-                functools.partial(level_kernel, offset, send_offset),
+            fetch = tree_level == 0
+            scratch = [
+                pltpu.SMEM(panel_from.shape, jnp.int32),
+                pltpu.VMEM((KP * sep_tiles, BS, BS), jnp.bfloat16),
+                pltpu.VMEM((sep_tiles, BS, rhs), jnp.float32),
+                pltpu.VMEM((TS, BS, BS), jnp.float32),
+                pltpu.SemaphoreType.DMA((4,)),
+            ]
+            if fetch:
+                scratch += [
+                    pltpu.VMEM((group, BS, rhs), jnp.bfloat16),
+                    pltpu.SemaphoreType.DMA((PIECES,)),
+                ]
+            rights, solved, sent = pl.pallas_call(
+                functools.partial(level_kernel, offset, first_diag),
+                in_specs=[in_hbm(), in_hbm() if fetch else whole()] + [in_hbm()] * 3,
+                out_specs=(whole(),) * 3,
+                out_shape=(f32(rest_tiles, BS, rhs), f32(TS, BS, rhs), b16(TS, BS, rhs)),
+                scratch_shapes=scratch,
+                compiler_params=VMEM,
+                name=f"level{tree_level}",
+            )(
+                from_stream,
+                streamed(received) if fetch else received,
+                stream,
+                streamed(rights),
+                diag_stream,
+            )
+            all_solved.append(solved)
+            leaf_right = pl.pallas_call(
+                functools.partial(leaf_kernel, leaf_offset),
                 grid_spec=pltpu.PrefetchScalarGridSpec(
-                    num_scalar_prefetch=2,
-                    grid=(1,),
+                    num_scalar_prefetch=1,
+                    grid=(TL // LEAF_STEP,),
                     in_specs=[
                         whole(),
-                        entries_block(offset, KP * sep_tiles, False),
-                        whole(),
-                        entries_block(first_diag, TS, False),
+                        entries_block(leaf_offset, KP * LEAF_STEP),
+                        entries_block(0, LEAF_STEP),
                     ],
-                    out_specs=(whole(), whole(), whole()),
-                    scratch_shapes=[pltpu.VMEM((TS, BS, rhs), jnp.bfloat16)],
+                    out_specs=entries_block(0, LEAF_STEP),
                 ),
-                out_shape=(
-                    f32(rest_tiles, BS, rhs),
-                    f32(TS, BS, rhs),
-                    b16(group // 2, BS, rhs),
-                ),
+                out_shape=pltpu.HBM((TL, BS, rhs), jnp.float32),
                 compiler_params=VMEM,
-                name=f"level{tree_level}",
-            )(panel_from, send_row, received, panels, rights, diag_inverse)
-            all_solved.append(solved)
-        last = tree_level == LEVELS - 1
-        in_specs = [
-            whole(),
-            entries_block(leaf_offset, KP * LEAF_STEP, True),
-            entries_block(0, LEAF_STEP, True),
-        ]
-        operands = [panel_from, received, panels, leaf_right]
-        if last:
-            in_specs.append(entries_block(LEVELS * TS, LEAF_STEP, True))
-            operands.append(diag_inverse)
-        leaf_right = pl.pallas_call(
-            functools.partial(last_kernel if last else leaf_kernel, leaf_offset),
-            grid_spec=pltpu.PrefetchScalarGridSpec(
-                num_scalar_prefetch=1,
-                grid=(TL // LEAF_STEP,),
-                in_specs=in_specs,
-                out_specs=pl.BlockSpec((LEAF_STEP, BS, rhs), lambda i, *_: (i, 0, 0)),
-            ),
-            out_shape=f32(TL, BS, rhs),
-            compiler_params=VMEM,
-            name=f"leaf{tree_level}",
-        )(*operands)
+                name=f"leaf{tree_level}",
+            )(panel_from, received, stream, streamed(leaf_right))
+        else:
+            parts = TL // LAST_STEP
+            leaf_right = pl.pallas_call(
+                functools.partial(last_kernel, leaf_offset),
+                in_specs=[in_hbm(), whole()] + [in_hbm()] * 3,
+                out_specs=in_hbm(),
+                out_shape=pltpu.HBM((TL, BS, rhs), jnp.float32),
+                scratch_shapes=[
+                    pltpu.SMEM(panel_from.shape, jnp.int32),
+                    pltpu.VMEM((KP * TL, BS, BS), jnp.bfloat16),
+                    pltpu.VMEM((TL, BS, rhs), jnp.float32),
+                    pltpu.VMEM((TL, BS, BS), jnp.float32),
+                    pltpu.VMEM((TL, BS, rhs), jnp.float32),
+                    pltpu.SemaphoreType.DMA((3 * parts + 1,)),
+                    pltpu.SemaphoreType.DMA((parts,)),
+                ],
+                compiler_params=VMEM,
+                name="last",
+            )(from_stream, received, stream, streamed(leaf_right), diag_stream)
         offset = leaf_offset + KP * TL
     sep_solution = jnp.concatenate(all_solved, axis=0).reshape(rows, rhs)
     return (sep_solution, leaf_right.reshape(TL * BS, rhs))

time: 187 us -> 183 us (0.979)
  blocking collectives: 28.2 us -> 0 us
  waiting for transfers between devices: 82.3 us -> 104 us
  local copies, waits for them, and re-layouts: 16.7 us -> 3.85 us
  starting transfers between devices: 19.3 us -> 30.2 us
  other arithmetic: 0.83 us -> 6.95 us
  Pallas kernels: 37.7 us -> 35.8 us
    all_to_all x1 -> x0, blocking collectives: 28.2 us -> none  [per_device(): arrived = lax.all_to_all(outgoing, AXES, 0, 0, tiled=True)]
    all_to_all x0 -> x1, waiting for transfers between devices: none -> 16.9 us  [per_device(): arrived = lax.all_to_all(outgoing, AXES, 0, 0, tiled=True)]
    unnamed x40 -> x18, local copies, waits for them, and re-layouts: 16.7 us -> 3.83 us
    all_to_all x0 -> x1, starting transfers between devices: none -> 11.5 us  [per_device(): arrived = lax.all_to_all(outgoing, AXES, 0, 0, tiled=True)]
    select_n x0 -> x4, other arithmetic: none -> 5.96 us  [per_device(): jnp.where((picks == 0)[:, None, None], sent[0][None], sent[1][None])]
    all_to_all x4, waiting for transfers between devices: 82.3 us -> 87.3 us  [per_device(): lax.all_to_all(buffer, AXES, 0, 0, axis_index_groups=groups, tiled=True)]
    pallas_call x8, Pallas kernels: 35.3 us -> 32.5 us  [the longest x3 19.1 us: per_device(): pl.pallas_call(functools.partial(leaf_kernel, leaf_offset), grid_spec=plt...]
  transfers between devices with their start and end apart: 4 -> 5, of which waited for: 4 -> 5; matrix products, arithmetic and copies ran while one was open for 0% -> 1% of each run, Pallas kernels for 9% -> 11%
where the time goes in v4:
time: 183 us; the launch traced here: 182 us
  waiting for transfers between devices  104 us (57%)
  Pallas kernels  35.8 us (20%)
  starting transfers between devices  30.2 us (17%)
  other arithmetic  6.95 us (4%)
  local copies, waits for them, and re-layouts  3.85 us (2%)
    all_to_all x4, waiting for transfers between devices, per_device(): lax.all_to_all(buffer, AXES, 0, 0, axis_index_groups=groups, tiled=True)  87.3 us
    pallas_call x3, Pallas kernels, per_device(): pl.pallas_call(functools.partial(leaf_kernel, leaf_offset), grid_spec=plt...  19.1 us
    all_to_all x4, starting transfers between devices, per_device(): lax.all_to_all(buffer, AXES, 0, 0, axis_index_groups=groups, tiled=True)  18.7 us
    all_to_all x1, waiting for transfers between devices, per_device(): arrived = lax.all_to_all(outgoing, AXES, 0, 0, tiled=True)  16.9 us
    all_to_all x1, starting transfers between devices, per_device(): arrived = lax.all_to_all(outgoing, AXES, 0, 0, tiled=True)  11.5 us
    pallas_call x3, Pallas kernels, per_device(): pl.pallas_call(functools.partial(level_kernel, offset, first_diag), in_sp...  6.61 us
    select_n x4, other arithmetic, per_device(): jnp.where((picks == 0)[:, None, None], sent[0][None], sent[1][None])  5.96 us
    pallas_call x1, Pallas kernels, per_device(): pl.pallas_call(functools.partial(last_kernel, leaf_offset), in_specs=[in_...  5.4 us
  transfers between devices with their start and end apart: 5, of which 5 were waited for; matrix products, arithmetic and copies ran while one was open for 1% of the time, Pallas kernels for 11%

profile of v4, /device:TPU:1, one launch (start us, length us, event | category | flops | bytes accessed | tf_op | source)
XLA Modules:
  0.0 181.8 jit_solution(12280467282565694399)
XLA Ops:
  0.6 0.0 copy-start.8
  0.6 0.0 copy-start.1
  0.6 1.0 copy-done.1
  1.7 0.0 copy-start.7
  1.7 0.7 copy-done.7
  2.4 2.6 %pack.1 = bf16[128,8,384]{2,1,0:T(8,128)(2,1)} custom-call(s32[1,1024]{1,0:T(1,128)S(1)} %bitcast.28, f32[1024,128]{1,0:T(8,128)S(1)} %copy-done.1), custom_call_target="tpu_custom_call" | custom-call | tf_op jit(solution)/shard_map/pack/pallas_call | solution.py:244
  4.9 11.5 %all-to-all-start = ((bf16[128,8,384]{2,1,0:T(8,128)(2,1)}), bf16[128,8,384]{2,1,0:T(8,128)(2,1)S(1)}, u32[]{:S(2)}, u32[]{:S(2)}) async-start(bf16[128,8,384]{2,1,0:T(8,128)(2,1)} %pack.1), calls=%async_computation | async-start | bytes 1572864 | tf_op jit(solution)/shard_map/all_to_all | solution.py:252
  16.4 0.0 copy-done.8
  16.5 16.9 %all-to-all-done.arrived_ref = bf16[128,8,384]{2,1,0:T(8,128)(2,1)S(1)} async-done(((bf16[128,8,384]{2,1,0:T(8,128)(2,1)}), bf16[128,8,384]{2,1,0:T(8,128)(2,1)S(1)}, u32[]{:S(2)}, u32[]{:S(2)}) %all-to-all-start) | async-done | bytes 786464 | tf_op jit(solution)/shard_map/all_to_all | solution.py:252
  33.4 1.4 first.1
  34.8 2.4 %broadcast_select_fusion = bf16[128,128,128]{2,1,0:T(8,128)(2,1)} fusion(pred[128]{0:T(512)(128)(4,1)S(1)} %compare_bitcast_fusion.3, bf16[128,128]{1,0:T(8,128)(2,1)S(1)} %get-tuple-element.41, bf16[128,128]{1,0:T(8,128)(2,1)S(1)} %get-tuple-element.40), kind=kLoop, calls=%fused_computation | loop fusion | flops 2097152 | bytes 4259968 | tf_op jit(solution)/shard_map/jit(_where)/select_n | solution.py:284
  37.2 4.8 %all-to-all-start.1 = ((bf16[128,128,128]{2,1,0:T(8,128)(2,1)}), bf16[128,128,128]{2,1,0:T(8,128)(2,1)}, u32[]{:S(2)}, u32[]{:S(2)}) async-start(bf16[128,128,128]{2,1,0:T(8,128)(2,1)} %broadcast_select_fusion), calls=%async_computation.1 | async-start | bytes 8388608 | tf_op jit(solution)/shard_map/all_to_all | solution.py:285
  42.0 0.7 order.1.rights_hbm
  42.7 0.0 copy-start
  42.8 0.7 copy-done
  43.5 51.8 %all-to-all-done.1.received_ref = bf16[128,128,128]{2,1,0:T(8,128)(2,1)} async-done(((bf16[128,128,128]{2,1,0:T(8,128)(2,1)}), bf16[128,128,128]{2,1,0:T(8,128)(2,1)}, u32[]{:S(2)}, u32[]{:S(2)}) %all-to-all-start.1) | async-done | bytes 4194336 | tf_op jit(solution)/shard_map/all_to_all | solution.py:285
  95.2 3.2 %level0.1 = (f32[4,128,128]{2,1,0:T(8,128)S(1)}, f32[2,128,128]{2,1,0:T(8,128)S(1)}, bf16[2,128,128]{2,1,0:T(8,128)(2,1)S(1)}) custom-call(s32[560]{0:T(1024)} %from_hbm.7, bf16[128,128,128]{2,1,0:T(8,128)(2,1)} %all-to-all-done.1.received_ref, bf16[560,128,128]{2,1,0:T(8,128)(2,1)} %panels_hbm.7, f32[6,128,128]{2,1,0:T(8,128)} %copy-done, ...), custom_call_target="tpu_custom_call" | custom-call | tf_op jit(solution)/shard_map/level0/pallas_call | solution.py:309
  98.4 0.0 copy-start.2
  98.5 0.7 copy-done.2
  99.2 1.5 broadcast_select_fusion.1
  100.7 0.0 copy-start.3
  100.7 4.6 %all-to-all-start.2 = ((bf16[64,128,128]{2,1,0:T(8,128)(2,1)}), bf16[64,128,128]{2,1,0:T(8,128)(2,1)S(1)}, u32[]{:S(2)}, u32[]{:S(2)}) async-start(bf16[64,128,128]{2,1,0:T(8,128)(2,1)} %broadcast_select_fusion.1), calls=%async_computation.2 | async-start | bytes 4194304 | tf_op jit(solution)/shard_map/all_to_all | solution.py:285
  105.3 0.1 compare_bitcast_fusion.1
  105.3 0.0 copy-done.3
  105.3 7.3 %leaf0.1.right_ref = f32[32,128,128]{2,1,0:T(8,128)} custom-call(s32[560]{0:T(1024)S(1)} %copy-done.3, bf16[128,128,128]{2,1,0:T(8,128)(2,1)} %all-to-all-done.1.received_ref, bf16[560,128,128]{2,1,0:T(8,128)(2,1)} %panels_hbm.7, f32[32,128,128]{2,1,0:T(8,128)} %bitcast.29), custom_call_target="tpu_custom_call" | custom-call | tf_op jit(solution)/shard_map/leaf0/pallas_call | solution.py:325
  112.6 22.2 %all-to-all-done.2.received_ref = bf16[64,128,128]{2,1,0:T(8,128)(2,1)S(1)} async-done(((bf16[64,128,128]{2,1,0:T(8,128)(2,1)}), bf16[64,128,128]{2,1,0:T(8,128)(2,1)S(1)}, u32[]{:S(2)}, u32[]{:S(2)}) %all-to-all-start.2) | async-done | bytes 2097184 | tf_op jit(solution)/shard_map/all_to_all | solution.py:285
  134.8 1.7 level1.1
  136.5 0.0 copy-start.6
  136.5 0.6 copy-done.6
  137.1 0.0 copy-start.4
  137.1 1.2 broadcast_select_fusion.2
  138.3 4.6 %all-to-all-start.3 = ((bf16[32,128,128]{2,1,0:T(8,128)(2,1)}), bf16[32,128,128]{2,1,0:T(8,128)(2,1)S(1)}, u32[]{:S(2)}, u32[]{:S(2)}) async-start(bf16[32,128,128]{2,1,0:T(8,128)(2,1)} %broadcast_select_fusion.2), calls=%async_computation.3 | async-start | bytes 2097152 | tf_op jit(solution)/shard_map/all_to_all | solution.py:285
  142.9 0.1 compare_bitcast_fusion
  143.0 0.0 copy-done.4
  143.0 5.9 %leaf1.1.right_ref = f32[32,128,128]{2,1,0:T(8,128)} custom-call(s32[560]{0:T(1024)S(1)} %copy-done.4, bf16[64,128,128]{2,1,0:T(8,128)(2,1)S(1)} %all-to-all-done.2.received_ref, bf16[560,128,128]{2,1,0:T(8,128)(2,1)} %panels_hbm.7, f32[32,128,128]{2,1,0:T(8,128)} %leaf0.1.right_ref), custom_call_target="tpu_custom_call" | custom-call | tf_op jit(solution)/shard_map/leaf1/pallas_call | solution.py:325
  148.9 10.1 %all-to-all-done.3.received_ref = bf16[32,128,128]{2,1,0:T(8,128)(2,1)S(1)} async-done(((bf16[32,128,128]{2,1,0:T(8,128)(2,1)}), bf16[32,128,128]{2,1,0:T(8,128)(2,1)S(1)}, u32[]{:S(2)}, u32[]{:S(2)}) %all-to-all-start.3) | async-done | bytes 1048608 | tf_op jit(solution)/shard_map/all_to_all | solution.py:285
  159.0 0.0 copy-start.5
  159.0 1.8 level2.1
  160.8 0.9 broadcast_select_fusion.3
  161.7 4.7 %all-to-all-start.4 = ((bf16[16,128,128]{2,1,0:T(8,128)(2,1)}), bf16[16,128,128]{2,1,0:T(8,128)(2,1)S(1)}, u32[]{:S(2)}, u32[]{:S(2)}) async-start(bf16[16,128,128]{2,1,0:T(8,128)(2,1)} %broadcast_select_fusion.3), calls=%async_computation.4 | async-start | bytes 1048576 | tf_op jit(solution)/shard_map/all_to_all | solution.py:285
  166.4 0.0 copy-done.5
  166.4 5.9 %leaf2.1.right_hbm = f32[32,128,128]{2,1,0:T(8,128)} custom-call(s32[560]{0:T(1024)S(1)} %copy-done.5, bf16[32,128,128]{2,1,0:T(8,128)(2,1)S(1)} %all-to-all-done.3.received_ref, bf16[560,128,128]{2,1,0:T(8,128)(2,1)} %panels_hbm.7, f32[32,128,128]{2,1,0:T(8,128)} %leaf1.1.right_ref), custom_call_target="tpu_custom_call" | custom-call | tf_op jit(solution)/shard_map/leaf2/pallas_call | solution.py:325
  172.3 0.8 pad_maximum_fusion
  173.2 3.2 %all-to-all-done.4.received_ref = bf16[16,128,128]{2,1,0:T(8,128)(2,1)S(1)} async-done(((bf16[16,128,128]{2,1,0:T(8,128)(2,1)}), bf16[16,128,128]{2,1,0:T(8,128)(2,1)S(1)}, u32[]{:S(2)}, u32[]{:S(2)}) %all-to-all-start.4) | async-done | bytes 524320 | tf_op jit(solution)/shard_map/all_to_all | solution.py:285
  176.4 5.4 %last.1 = f32[32,128,128]{2,1,0:T(8,128)} custom-call(s32[560]{0:T(1024)} %from_hbm.7, bf16[16,128,128]{2,1,0:T(8,128)(2,1)S(1)} %all-to-all-done.4.received_ref, bf16[560,128,128]{2,1,0:T(8,128)(2,1)} %panels_hbm.7, f32[32,128,128]{2,1,0:T(8,128)} %leaf2.1.right_hbm, f32[40,128,128]{2,1,0:T(8,128)} %diag_hbm.9), custom_call_target="tpu_custom_call" | custom-call | tf_op jit(solution)/shard_map/last/pallas_call | solution.py:343
  (6 shorter events, 0.0 us)
Async XLA Ops:
  0.6 15.8 %copy-start.8 = (s32[1,240]{1,0:T(1,128)S(1)}, s32[1,240]{1,0:T(1,128)}, u32[]{:S(2)}) copy-start(s32[1,240]{1,0:T(1,128)} %param.13) | copy-start | bytes 2884
  0.6 1.0 copy-start.1
  1.7 0.7 copy-start.7
  4.9 28.4 %all-to-all-start = ((bf16[128,8,384]{2,1,0:T(8,128)(2,1)}), bf16[128,8,384]{2,1,0:T(8,128)(2,1)S(1)}, u32[]{:S(2)}, u32[]{:S(2)}) async-start(bf16[128,8,384]{2,1,0:T(8,128)(2,1)} %pack.1), calls=%async_computation | async-start | bytes 1572864 | tf_op jit(solution)/shard_map/all_to_all | solution.py:252
  37.2 58.0 %all-to-all-start.1 = ((bf16[128,128,128]{2,1,0:T(8,128)(2,1)}), bf16[128,128,128]{2,1,0:T(8,128)(2,1)}, u32[]{:S(2)}, u32[]{:S(2)}) async-start(bf16[128,128,128]{2,1,0:T(8,128)(2,1)} %broadcast_select_fusion), calls=%async_computation.1 | async-start | bytes 8388608 | tf_op jit(solution)/shard_map/all_to_all | solution.py:285
  42.7 0.7 copy-start
  98.4 0.7 copy-start.2
  100.7 4.7 %copy-start.3 = (s32[560]{0:T(1024)S(1)}, s32[560]{0:T(1024)}, u32[]{:S(2)}) copy-start(s32[560]{0:T(1024)} %from_hbm.7) | copy-start | bytes 6724
  100.7 34.1 %all-to-all-start.2 = ((bf16[64,128,128]{2,1,0:T(8,128)(2,1)}), bf16[64,128,128]{2,1,0:T(8,128)(2,1)S(1)}, u32[]{:S(2)}, u32[]{:S(2)}) async-start(bf16[64,128,128]{2,1,0:T(8,128)(2,1)} %broadcast_select_fusion.1), calls=%async_computation.2 | async-start | bytes 4194304 | tf_op jit(solution)/shard_map/all_to_all | solution.py:285
  136.5 0.7 copy-start.6
  137.1 5.9 %copy-start.4 = (s32[560]{0:T(1024)S(1)}, s32[560]{0:T(1024)}, u32[]{:S(2)}) copy-start(s32[560]{0:T(1024)} %from_hbm.7) | copy-start | bytes 6724
  138.3 20.7 %all-to-all-start.3 = ((bf16[32,128,128]{2,1,0:T(8,128)(2,1)}), bf16[32,128,128]{2,1,0:T(8,128)(2,1)S(1)}, u32[]{:S(2)}, u32[]{:S(2)}) async-start(bf16[32,128,128]{2,1,0:T(8,128)(2,1)} %broadcast_select_fusion.2), calls=%async_computation.3 | async-start | bytes 2097152 | tf_op jit(solution)/shard_map/all_to_all | solution.py:285
  159.0 7.4 %copy-start.5 = (s32[560]{0:T(1024)S(1)}, s32[560]{0:T(1024)}, u32[]{:S(2)}) copy-start(s32[560]{0:T(1024)} %from_hbm.7) | copy-start | bytes 6724
  161.7 14.7 %all-to-all-start.4 = ((bf16[16,128,128]{2,1,0:T(8,128)(2,1)}), bf16[16,128,128]{2,1,0:T(8,128)(2,1)S(1)}, u32[]{:S(2)}, u32[]{:S(2)}) async-start(bf16[16,128,128]{2,1,0:T(8,128)(2,1)} %broadcast_select_fusion.3), calls=%async_computation.4 | async-start | bytes 1048576 | tf_op jit(solution)/shard_map/all_to_all | solution.py:285

commit v5 on v4

--- a/solution.py
+++ b/solution.py
@@ -15,7 +15,9 @@
 AXES = ("leaf", "panel")
 LEAF_STEP = 8
 LAST_STEP = 8
-PIECES = 4
+SIDE = 4
+CUTS = (0, 48, 96, 128)
+ORDERS = ("xzy", "zyx", "yxz")
 VMEM = pltpu.CompilerParams(vmem_limit_bytes=16 * 1024 * 1024)
 
 
@@ -40,7 +42,7 @@
     return lax.dot_general(a, b, (((1,), (1,)), ((), ())), preferred_element_type=jnp.float32)
 
 
-def pack_kernel(target_ref, noise_ref, out_ref):
+def pack_kernel(target_ref, send_ref, noise_ref, out_ref):
     rows = noise_ref.shape[0]
     owners, per_owner, width = out_ref.shape
     target = target_ref[...]
@@ -59,29 +61,39 @@
     level_rows = TS * BS
     lane = lax.broadcasted_iota(jnp.int32, (BS, rows), 0)
     place = jnp.where(slot // level_rows == lane, slot % level_rows, -1)
-    meta = transposed_dot(select, place.astype(jnp.float32).astype(jnp.bfloat16))
+    row = lax.broadcasted_iota(jnp.int32, (BS, owners), 0)
+    picks = send_ref[:, :owners]
+    theirs = (owner ^ SIDE) == lax.broadcasted_iota(jnp.int32, (owners, rows), 0)
+    picked = jnp.dot(
+        hot((picks > 0) & (row == LEVELS)), hot(mine), preferred_element_type=jnp.float32
+    ) + jnp.dot(
+        hot((picks > 0) & (row == LEVELS + 1)), hot(theirs), preferred_element_type=jnp.float32
+    )
+    place = jnp.where(lane < LEVELS, place.astype(jnp.float32), picked)
+    meta = transposed_dot(select, place.astype(jnp.bfloat16))
     out = jnp.concatenate([out, meta], axis=1)
     out_ref[...] = out.reshape(owners, per_owner, width).astype(jnp.bfloat16)
 
 
-def order_rows(arrived_ref, tree_levels):
+def arrived_parts(arrived_ref):
     owners, per_owner, width = arrived_ref.shape
     rows = owners * per_owner
-    rhs = width - BS
     arrived = arrived_ref[...].astype(jnp.float32).reshape(rows, width).astype(jnp.bfloat16)
     unit = hot(
         lax.broadcasted_iota(jnp.int32, (8, BS), 0) == lax.broadcasted_iota(jnp.int32, (8, BS), 1)
     )
-    places = transposed_dot(unit, arrived[:, rhs:]).astype(jnp.int32)
-    out = []
-    for tree_level in tree_levels:
-        select = hot(
-            places[tree_level : tree_level + 1]
-            == lax.broadcasted_iota(jnp.int32, (TS * BS, rows), 0)
-        )
-        both = jnp.dot(select, arrived[:, :rhs], preferred_element_type=jnp.float32)
-        out.append(both[:, : rhs // 2] + both[:, rhs // 2 :])
-    return out
+    places = transposed_dot(unit, arrived[:, width - BS :]).astype(jnp.int32)
+    return arrived[:, : width - BS], places
+
+
+def order_rows(arrived, places, tree_level):
+    rows, width = arrived.shape
+    select = hot(
+        places[tree_level : tree_level + 1]
+        == lax.broadcasted_iota(jnp.int32, (TS * BS, rows), 0)
+    )
+    both = jnp.dot(select, arrived, preferred_element_type=jnp.float32)
+    return both[:, : width // 2] + both[:, width // 2 :]
 
 
 def solve(diag, right):
@@ -105,16 +117,96 @@
 def first_kernel(arrived_ref, diag_hbm, solved_ref, sent_ref, diag_ref, arrived):
     fetch = pltpu.make_async_copy(diag_hbm.at[pl.ds(0, TS)], diag_ref, arrived)
     fetch.start()
-    [right] = order_rows(arrived_ref, [0])
+    right = order_rows(*arrived_parts(arrived_ref), 0)
     fetch.wait()
     for t in range(TS):
         finish(right[t * BS : (t + 1) * BS], diag_ref, t, solved_ref, sent_ref)
 
 
-def order_kernel(arrived_ref, out_ref):
-    for i, right in enumerate(order_rows(arrived_ref, range(1, LEVELS))):
+def order_kernel(arrived_ref, out_ref, picks_ref):
+    arrived, places = arrived_parts(arrived_ref)
+    for i in range(LEVELS - 1):
+        right = order_rows(arrived, places, i + 1)
         for t in range(TS):
             out_ref[i * TS + t] = right[t * BS : (t + 1) * BS]
+    picks_ref[...] = places[LEVELS : LEVELS + 2]
+
+
+def step_pairs(axis, second):
+    pairs = []
+    for device in range(2 * SIDE**3):
+        at = {
+            "x": device % SIDE,
+            "c": device // SIDE % 2,
+            "z": device // (2 * SIDE) % SIDE,
+            "y": device // (2 * SIDE * SIDE),
+        }
+        up = (at[axis] + at["c"] + second) % 2 == 0
+        at[axis] = (at[axis] + (1 if up else -1)) % SIDE
+        pairs.append((device, ((at["y"] * SIDE + at["z"]) * 2 + at["c"]) * SIDE + at["x"]))
+    return pairs
+
+
+def gather_core(sent):
+    parts = [sent[:, a:b] for a, b in zip(CUTS, CUTS[1:])]
+    for step in range(2 * len(ORDERS[0])):
+        arriving = [
+            lax.ppermute(part, AXES, step_pairs(order[step // 2], step % 2))
+            for part, order in zip(parts, ORDERS)
+        ]
+        parts = [jnp.concatenate(both, axis=0) for both in zip(parts, arriving)]
+    return parts
+
+
+def swap_core(x):
+    return lax.ppermute(x, AXES, [(i, i ^ SIDE) for i in range(2 * SIDE**3)])
+
+
+def same_core(position, at_ref):
+    return (position // SIDE) % 2 == at_ref[3]
+
+
+def take(parts, at_ref, position, pick):
+    core = at_ref[3]
+
+    def place(axis, there):
+        here = at_ref["xyz".index(axis)]
+        away = there - here
+        away = jnp.where((here + core) % 2 == 0, away, -away) & (SIDE - 1)
+        return away ^ (away >> 1)
+
+    there = {
+        "x": position % SIDE,
+        "z": position // (2 * SIDE) % SIDE,
+        "y": position // (2 * SIDE * SIDE),
+    }
+    spots = {axis: place(axis, there[axis]) for axis in there}
+    for part, order in zip(parts, ORDERS):
+        at = 0
+        for axis in reversed(order):
+            at = at * SIDE + spots[axis]
+        yield part[at * TS + pick]
+
+
+def near_kernel(at_ref, picks_ref, mine_ref, theirs_ref, a_ref, b_ref, c_ref, own_ref, other_ref):
+    for which, (from_ref, out_ref) in enumerate(((mine_ref, own_ref), (theirs_ref, other_ref))):
+        for e in range(out_ref.shape[0]):
+            position = from_ref[e]
+            blocks = take((a_ref, b_ref, c_ref), at_ref, position, picks_ref[which, position * 8])
+            for first, block in zip(CUTS, blocks):
+                out_ref[e, first : first + block.shape[0]] = block
+
+
+def spread_kernel(at_ref, picks_ref, a_ref, b_ref, c_ref, own_ref, other_ref):
+    def body(i, carry):
+        position = i // SIDE * (2 * SIDE) + at_ref[3] * SIDE + i % SIDE
+        for which, out_ref in enumerate((own_ref, other_ref)):
+            blocks = take((a_ref, b_ref, c_ref), at_ref, position, picks_ref[which, position * 8])
+            for first, block in zip(CUTS, blocks):
+                out_ref[i, first : first + block.shape[0]] = block
+        return carry
+
+    lax.fori_loop(0, own_ref.shape[0], body, 0)
 
 
 def tile_update(panels_ref, local, tile):
@@ -130,34 +222,68 @@
     return copies
 
 
-def level_kernel(
-    offset, first_diag, from_hbm, received_ref, panels_hbm, rights_hbm, diag_hbm,
-    rest_ref, solved_ref, sent_ref,
-    from_ref, panels_ref, rights_ref, diag_ref, arrived, near_ref=None, near_arrived=None,
-):
-    tiles = rights_ref.shape[0]
+def load_level(offset, first_diag, sources, targets, arrived):
+    from_hbm, panels_hbm, rights_hbm, diag_hbm = sources
+    from_ref, panels_ref, rights_ref, diag_ref = targets
     copies = start(
         (from_hbm, from_ref, arrived.at[0]),
-        (panels_hbm.at[pl.ds(offset, KP * tiles)], panels_ref, arrived.at[1]),
+        (panels_hbm.at[pl.ds(offset, panels_ref.shape[0])], panels_ref, arrived.at[1]),
         (rights_hbm, rights_ref, arrived.at[2]),
         (diag_hbm.at[pl.ds(first_diag, TS)], diag_ref, arrived.at[3]),
     )
-    if near_ref is not None:
-        count = received_ref.shape[0] // PIECES
-        for piece in range(PIECES):
-            part = pl.ds(piece * count, count)
-            copies += start((received_ref.at[part], near_ref.at[part], near_arrived.at[piece]))
-        received_ref = near_ref
     for copy in copies:
         copy.wait()
-    for d in range(tiles):
-        right = rights_ref[d] - tile_update(
-            panels_ref, KP * d, lambda k: received_ref[from_ref[offset + KP * d + k]]
-        )
+
+
+def run_level(tile, panels_ref, rights_ref, diag_ref, rest_ref, solved_ref, sent_ref):
+    for d in range(rights_ref.shape[0]):
+        right = rights_ref[d] - tile_update(panels_ref, KP * d, lambda k: tile(KP * d + k))
         if d < TS:
             finish(right, diag_ref, d, solved_ref, sent_ref)
         else:
             rest_ref[d - TS] = right
+
+
+def level_kernel(
+    offset, first_diag, from_hbm, panels_hbm, rights_hbm, diag_hbm, received_ref,
+    rest_ref, solved_ref, sent_ref, from_ref, panels_ref, rights_ref, diag_ref, arrived,
+):
+    load_level(
+        offset, first_diag, (from_hbm, panels_hbm, rights_hbm, diag_hbm),
+        (from_ref, panels_ref, rights_ref, diag_ref), arrived,
+    )
+    run_level(
+        lambda e: received_ref[from_ref[offset + e]],
+        panels_ref, rights_ref, diag_ref, rest_ref, solved_ref, sent_ref,
+    )
+
+
+def top_kernel(
+    from_hbm, panels_hbm, rights_hbm, diag_hbm, at_ref, own_ref, other_ref,
+    rest_ref, solved_ref, sent_ref, from_ref, panels_ref, rights_ref, diag_ref, arrived,
+):
+    load_level(
+        0, TS, (from_hbm, panels_hbm, rights_hbm, diag_hbm),
+        (from_ref, panels_ref, rights_ref, diag_ref), arrived,
+    )
+    run_level(
+        lambda e: jnp.where(same_core(from_ref[e], at_ref), own_ref[e], other_ref[e]),
+        panels_ref, rights_ref, diag_ref, rest_ref, solved_ref, sent_ref,
+    )
+
+
+def top_leaf_kernel(offset, from_ref, at_ref, own_ref, other_ref, panels_ref, right_ref, out_ref):
+    first = offset + pl.program_id(0) * LEAF_STEP * KP
+
+    def tile(entry):
+        position = from_ref[entry]
+        slot = position // (2 * SIDE) * SIDE + position % SIDE
+        return jnp.where(same_core(position, at_ref), own_ref[slot], other_ref[slot])
+
+    for d in range(LEAF_STEP):
+        out_ref[d] = right_ref[d] - tile_update(
+            panels_ref, KP * d, lambda k: tile(first + KP * d + k)
+        )
 
 
 def leaf_kernel(offset, from_ref, received_ref, panels_ref, right_ref, out_ref):
@@ -234,6 +360,23 @@
     return jax.ShapeDtypeStruct(shape, jnp.bfloat16)
 
 
+def leaf_pass(kernel, offset, scalars, received, stream, leaf_right):
+    tiles, rows, rhs = leaf_right.shape
+    return pl.pallas_call(
+        kernel,
+        grid_spec=pltpu.PrefetchScalarGridSpec(
+            num_scalar_prefetch=len(scalars),
+            grid=(tiles // LEAF_STEP,),
+            in_specs=[whole()] * len(received)
+            + [entries_block(offset, KP * LEAF_STEP), entries_block(0, LEAF_STEP)],
+            out_specs=entries_block(0, LEAF_STEP),
+        ),
+        out_shape=pltpu.HBM((tiles, rows, rhs), jnp.float32),
+        compiler_params=VMEM,
+        name="leaf",
+    )(*scalars, *received, stream, streamed(leaf_right))
+
+
 def per_device(
     noise_parts, elimination_row, leaf_noise, diag_inverse, panels, panel_from, send_lists
 ):
@@ -244,11 +387,11 @@
     outgoing = pl.pallas_call(
         pack_kernel,
         out_shape=b16(owners, per_owner, 2 * rhs + BS),
-        in_specs=[whole()] * 2,
+        in_specs=[whole()] * 3,
         out_specs=whole(),
         compiler_params=VMEM,
         name="pack",
-    )(elimination_row.reshape(1, rows), noise_parts)
+    )(elimination_row.reshape(1, rows), send_lists, noise_parts)
     arrived = lax.all_to_all(outgoing, AXES, 0, 0, tiled=True)
     send_row = send_lists[0]
     stream = streamed(panels)
@@ -263,14 +406,33 @@
         compiler_params=VMEM,
         name="first",
     )(arrived, diag_stream)
-    rights = pl.pallas_call(
+    rights, picks = pl.pallas_call(
         order_kernel,
-        out_shape=f32((LEVELS - 1) * TS, BS, rhs),
+        out_shape=(
+            f32((LEVELS - 1) * TS, BS, rhs),
+            jax.ShapeDtypeStruct((2, rows), jnp.int32),
+        ),
         in_specs=[whole()],
-        out_specs=whole(),
+        out_specs=(whole(), whole()),
         compiler_params=VMEM,
         name="order",
     )(arrived)
+    in_smem = pl.BlockSpec(memory_space=pltpu.SMEM)
+    leaf = lax.axis_index("leaf")
+    at = jnp.stack([lax.axis_index("panel"), leaf // (2 * SIDE), leaf // 2 % SIDE, leaf % 2])
+    near = KP * TS * (LEVELS - 1)
+    mine = panel_from[:near]
+    theirs = swap_core(mine)
+    gathered = gather_core(sent)
+    own, other = pl.pallas_call(
+        near_kernel,
+        out_shape=(b16(near, BS, rhs), b16(near, BS, rhs)),
+        in_specs=[in_smem] * 4 + [whole()] * 3,
+        out_specs=(whole(), whole()),
+        compiler_params=VMEM,
+        name="near",
+    )(at, picks, mine, theirs, *gathered)
+    other = swap_core(other)
     leaf_right = leaf_noise.reshape(TL, BS, rhs)
     all_solved = [solved]
     offset = 0
@@ -280,64 +442,78 @@
         groups = [
             list(range(g * group, (g + 1) * group)) for g in range(owners // group)
         ]
-        picks = send_row[send_offset : send_offset + group]
-        buffer = jnp.where((picks == 0)[:, None, None], sent[0][None], sent[1][None])
-        received = lax.all_to_all(
-            buffer, AXES, 0, 0, axis_index_groups=groups, tiled=True
-        )
         if tree_level:
+            chosen = send_row[send_offset : send_offset + group]
+            buffer = jnp.where((chosen == 0)[:, None, None], sent[0][None], sent[1][None])
+            if tree_level == 1:
+                gathered, buffer = lax.optimization_barrier((gathered, buffer))
+                own_all, other_all = pl.pallas_call(
+                    spread_kernel,
+                    out_shape=(b16(owners // 2, BS, rhs), b16(owners // 2, BS, rhs)),
+                    in_specs=[in_smem] * 2 + [whole()] * 3,
+                    out_specs=(whole(), whole()),
+                    compiler_params=VMEM,
+                    name="spread",
+                )(at, picks, *gathered)
+                other_all = swap_core(other_all)
+            received = lax.all_to_all(
+                buffer, AXES, 0, 0, axis_index_groups=groups, tiled=True
+            )
+        if tree_level == 2:
+            leaf_right = leaf_pass(
+                functools.partial(top_leaf_kernel, KP * TS * (LEVELS - 1)),
+                KP * TS * (LEVELS - 1),
+                (panel_from, at),
+                (own_all, other_all),
+                stream,
+                leaf_right,
+            )
+            leaf_right = leaf_pass(*waiting, leaf_right)
+        if tree_level == 3:
+            leaf_right = leaf_pass(*waiting, leaf_right)
+        if tree_level >= 2:
             received, leaf_right = lax.optimization_barrier((received, leaf_right))
         send_offset += group
         sep_tiles = (LEVELS - 1 - tree_level) * TS
         leaf_offset = offset + KP * sep_tiles
         if tree_level < LEVELS - 1:
-            first_diag = (tree_level + 1) * TS
-            rest_tiles = max(sep_tiles - TS, TS)
-            fetch = tree_level == 0
-            scratch = [
-                pltpu.SMEM(panel_from.shape, jnp.int32),
-                pltpu.VMEM((KP * sep_tiles, BS, BS), jnp.bfloat16),
-                pltpu.VMEM((sep_tiles, BS, rhs), jnp.float32),
-                pltpu.VMEM((TS, BS, BS), jnp.float32),
-                pltpu.SemaphoreType.DMA((4,)),
-            ]
-            if fetch:
-                scratch += [
-                    pltpu.VMEM((group, BS, rhs), jnp.bfloat16),
-                    pltpu.SemaphoreType.DMA((PIECES,)),
-                ]
+            operands = [from_stream, stream, streamed(rights), diag_stream]
+            in_specs = [in_hbm()] * 4
+            if tree_level:
+                kernel = functools.partial(level_kernel, offset, (tree_level + 1) * TS)
+                operands.append(received)
+                in_specs.append(whole())
+                waiting = (
+                    functools.partial(leaf_kernel, leaf_offset),
+                    leaf_offset,
+                    (panel_from,),
+                    (received,),
+                    stream,
+                )
+            else:
+                kernel = top_kernel
+                operands += [at, own, other]
+                in_specs += [in_smem, whole(), whole()]
             rights, solved, sent = pl.pallas_call(
-                functools.partial(level_kernel, offset, first_diag),
-                in_specs=[in_hbm(), in_hbm() if fetch else whole()] + [in_hbm()] * 3,
+                kernel,
+                in_specs=in_specs,
                 out_specs=(whole(),) * 3,
-                out_shape=(f32(rest_tiles, BS, rhs), f32(TS, BS, rhs), b16(TS, BS, rhs)),
-                scratch_shapes=scratch,
+                out_shape=(
+                    f32(max(sep_tiles - TS, TS), BS, rhs),
+                    f32(TS, BS, rhs),
+                    b16(TS, BS, rhs),
+                ),
+                scratch_shapes=[
+                    pltpu.SMEM(panel_from.shape, jnp.int32),
+                    pltpu.VMEM((KP * sep_tiles, BS, BS), jnp.bfloat16),
+                    pltpu.VMEM((sep_tiles, BS, rhs), jnp.float32),
+                    pltpu.VMEM((TS, BS, BS), jnp.float32),
+                    pltpu.SemaphoreType.DMA((4,)),
+                ],
                 compiler_params=VMEM,
                 name=f"level{tree_level}",
-            )(
-                from_stream,
-                streamed(received) if fetch else received,
-                stream,
-                streamed(rights),
-                diag_stream,
-            )
+            )(*operands)
             all_solved.append(solved)
-            leaf_right = pl.pallas_call(
-                functools.partial(leaf_kernel, leaf_offset),
-                grid_spec=pltpu.PrefetchScalarGridSpec(
-                    num_scalar_prefetch=1,
-                    grid=(TL // LEAF_STEP,),
-                    in_specs=[
-                        whole(),
-                        entries_block(leaf_offset, KP * LEAF_STEP),
-                        entries_block(0, LEAF_STEP),
-                    ],
-                    out_specs=entries_block(0, LEAF_STEP),
-                ),
-                out_shape=pltpu.HBM((TL, BS, rhs), jnp.float32),
-                compiler_params=VMEM,
-                name=f"leaf{tree_level}",
-            )(panel_from, received, stream, streamed(leaf_right))
         else:
             parts = TL // LAST_STEP
             leaf_right = pl.pallas_call(

time: 183 us -> 183 us (level)
  waiting for transfers between devices: 104 us -> 36.3 us
  blocking collectives: 0 us -> 28.2 us
  local copies, waits for them, and re-layouts: 3.85 us -> 26.9 us
  starting transfers between devices: 30.2 us -> 42.5 us
  Pallas kernels: 35.8 us -> 41.7 us
  other arithmetic: 6.95 us -> 4.76 us
    all_to_all x4 -> x3, waiting for transfers between devices: 87.3 us -> 24 us  [per_device(): lax.all_to_all(buffer, AXES, 0, 0, axis_index_groups=groups, tiled=True)]
    all_to_all x0 -> x1, blocking collectives: none -> 28.2 us  [per_device(): arrived = lax.all_to_all(outgoing, AXES, 0, 0, tiled=True)]
    ppermute x0 -> x21, starting transfers between devices: none -> 25.8 us  [the longest x3 14.6 us: swap_core(): return lax.ppermute(x, AXES, [(i, i ^ SIDE) for i in range(2 * SIDE ** 3)])]
    all_to_all x1 -> x0, waiting for transfers between devices: 16.9 us -> none  [per_device(): arrived = lax.all_to_all(outgoing, AXES, 0, 0, tiled=True)]
    unnamed x18 -> x56, local copies, waits for them, and re-layouts: 3.83 us -> 19.4 us
    ppermute x0 -> x21, waiting for transfers between devices: none -> 12.2 us  [the longest x18 10.3 us: gather_core(): lax.ppermute(part, AXES, step_pairs(order[step // 2], step % 2))]
    all_to_all x1 -> x0, starting transfers between devices: 11.5 us -> none  [per_device(): arrived = lax.all_to_all(outgoing, AXES, 0, 0, tiled=True)]
    concatenate x0 -> x6, local copies, waits for them, and re-layouts: none -> 6.75 us  [gather_core(): parts = [jnp.concatenate(both, axis=0) for both in zip(parts, arriving)]]
  transfers between devices with their start and end apart: 5 -> 24, of which waited for: 5 -> 13; matrix products, arithmetic and copies ran while one was open for 1% -> 10% of each run, Pallas kernels for 11% -> 15%
where the time goes in v5:
time: 183 us; the launch traced here: 182 us
  starting transfers between devices  42.5 us (23%)
  Pallas kernels  41.7 us (23%)
  waiting for transfers between devices  36.3 us (20%)
  blocking collectives  28.2 us (15%)
  local copies, waits for them, and re-layouts  26.9 us (15%)
  other arithmetic  4.76 us (3%)
    all_to_all x1, blocking collectives, per_device(): arrived = lax.all_to_all(outgoing, AXES, 0, 0, tiled=True)  28.2 us
    all_to_all x3, waiting for transfers between devices, per_device(): lax.all_to_all(buffer, AXES, 0, 0, axis_index_groups=groups, tiled=True)  24 us
    unnamed x56, local copies, waits for them, and re-layouts  19.4 us
    pallas_call x3, Pallas kernels, leaf_pass(): pl.pallas_call(kernel, grid_spec=pltpu.PrefetchScalarGridSpec(num_scalar_...  19.1 us
    all_to_all x3, starting transfers between devices, per_device(): lax.all_to_all(buffer, AXES, 0, 0, axis_index_groups=groups, tiled=True)  16.8 us
    ppermute x3, starting transfers between devices, swap_core(): return lax.ppermute(x, AXES, [(i, i ^ SIDE) for i in range(2 * SIDE ** 3)])  14.6 us
    ppermute x18, starting transfers between devices, gather_core(): lax.ppermute(part, AXES, step_pairs(order[step // 2], step % 2))  11.2 us
    ppermute x18, waiting for transfers between devices, gather_core(): lax.ppermute(part, AXES, step_pairs(order[step // 2], step % 2))  10.3 us
  transfers between devices with their start and end apart: 24, of which 13 were waited for; matrix products, arithmetic and copies ran while one was open for 10% of the time, Pallas kernels for 15%

profile of v5, /device:TPU:1, one launch (start us, length us, event | category | flops | bytes accessed | tf_op | source)
XLA Modules:
  0.0 181.6 jit_solution(3289826695168978612)
XLA Ops:
  0.6 1.0 copy-done.8
  1.7 0.7 copy-done.16
  2.4 0.7 copy-done.17
  3.0 1.8 pack.1
  4.8 28.2 %all_to_all.20.arrived_ref = bf16[128,8,384]{2,1,0:T(8,128)(2,1)S(1)} all-to-all(bf16[128,8,384]{2,1,0:T(8,128)(2,1)S(1)} %pack.1), channel_id=1, replica_groups=mesh['leaf'=32,'panel'=4] {'leaf','panel'}, dimensions={0} | all-to-all | bytes 1572864 | tf_op jit(solution)/shard_map/all_to_all | solution.py:395
  33.1 1.4 first.1
  35.1 0.8 collective-permute-start.13
  36.0 0.7 constant_dynamic-update-slice_fusion.28
  36.7 0.7 collective-permute-start.1
  37.4 1.5 collective-permute-done.13
  39.6 0.9 collective-permute-done.7
  42.7 1.1 collective-permute-done.8
  43.8 1.6 collective-permute-start.9
  45.4 2.0 %collective-permute-start.3 = (bf16[8,48,128]{2,1,0:T(8,128)(2,1)S(1)}, bf16[8,48,128]{2,1,0:T(8,128)(2,1)S(1)}, u32[]{:S(2)}, u32[]{:S(2)}) collective-permute-start(bf16[8,48,128]{2,1,0:T(8,128)(2,1)S(1)} %pad_maximum_fusion.4), channel_id=1, source_target_pairs={{0,8},{1,9},{2,10},{3,11},{4,28},{5,29},{6,30},{7,31},{8,0},{9,1},... | collective-permute-start | bytes 294920 | tf_op jit(solution)/shard_map/ppermute | solution.py:154
  48.1 0.6 constant_dynamic-update-slice_fusion.8
  48.7 0.9 collective-permute-start.16
  50.4 0.7 constant_dynamic-update-slice_fusion.25
  51.1 0.7 constant_dynamic-update-slice_fusion.7
  51.8 2.8 %collective-permute-done.10 = bf16[16,48,128]{2,1,0:T(8,128)(2,1)S(1)} collective-permute-done((bf16[16,48,128]{2,1,0:T(8,128)(2,1)S(1)}, bf16[16,48,128]{2,1,0:T(8,128)(2,1)S(1)}, u32[]{:S(2)}, u32[]{:S(2)}) %collective-permute-start.10) | collective-permute-done | bytes 196640 | tf_op jit(solution)/shard_map/ppermute | solution.py:154
  54.6 0.8 constant_dynamic-update-slice_fusion.24
  55.3 1.8 %collective-permute-start.11 = (bf16[32,48,128]{2,1,0:T(8,128)(2,1)S(1)}, bf16[32,48,128]{2,1,0:T(8,128)(2,1)S(1)}, u32[]{:S(2)}, u32[]{:S(2)}) collective-permute-start(bf16[32,48,128]{2,1,0:T(8,128)(2,1)S(1)} %get-tuple-element.58), channel_id=1, source_target_pairs={{0,1},{1,0},{2,3},{3,2},{4,7},{5,6},{6,5},{7,4},{8,9},{9,8},{10,11... | collective-permute-start | bytes 1179656 | tf_op jit(solution)/shard_map/ppermute | solution.py:154
  57.2 0.8 constant_dynamic-update-slice_fusion.6
  57.9 0.8 collective-permute-start.5
  59.4 0.7 constant_dynamic-update-slice_fusion.43
  60.0 0.7 constant_dynamic-update-slice_fusion.42
  60.8 1.2 collective-permute-start.17
  62.0 1.2 collective-permute-done.11
  63.2 0.9 constant_dynamic-update-slice_fusion.23
  64.0 1.7 collective-permute-done.5
  65.8 0.8 constant_dynamic-update-slice_fusion.5
  67.2 0.8 constant_dynamic-update-slice_fusion.41
  68.0 0.7 slice.42.mine_ref
  68.7 7.3 %collective-permute-start = (s32[24]{0:T(128)S(1)}, s32[24]{0:T(128)}, u32[]{:S(2)}, u32[]{:S(2)}) collective-permute-start(s32[24]{0:T(128)S(1)} %slice.42.mine_ref), channel_id=1, source_target_pairs={{0,4},{1,5},{2,6},{3,7},{4,0},{5,1},{6,2},{7,3},{8,12},{9,13},{10,... | collective-permute-start | bytes 296 | tf_op jit(solution)/shard_map/ppermute | solution.py:162
  76.0 0.7 order.1
  76.8 1.3 constant_dynamic-update-slice_fusion.47.c_ref
  78.0 1.2 constant_dynamic-update-slice_fusion.29.b_ref
  79.3 1.8 constant_dynamic-update-slice_fusion.11.a_ref
  81.2 2.3 %near.1 = (bf16[24,128,128]{2,1,0:T(8,128)(2,1)S(1)}, bf16[24,128,128]{2,1,0:T(8,128)(2,1)S(1)}) custom-call(s32[4]{0:T(128)S(1)} %pad_add_fusion.at_ref, s32[2,1024]{1,0:T(2,128)S(1)} %get-tuple-element.28.picks_ref, s32[24]{0:T(128)S(1)} %copy-done.20, s32[24]{0:T(128)} %collective-permute-done.theirs_ref, ...), custom_call_target="tpu_custom_call" | custom-call | tf_op jit(solution)/shard_map/near/pallas_call | solution.py:427
  83.5 6.8 %collective-permute-start.19 = (bf16[24,128,128]{2,1,0:T(8,128)(2,1)S(1)}, bf16[24,128,128]{2,1,0:T(8,128)(2,1)S(1)}, u32[]{:S(2)}, u32[]{:S(2)}) collective-permute-start(bf16[24,128,128]{2,1,0:T(8,128)(2,1)S(1)} %get-tuple-element.31), channel_id=1, source_target_pairs={{0,4},{1,5},{2,6},{3,7},{4,0},{5,1},{6,2},{7,3},{8,12},{9,13},{10,... | collective-permute-start | bytes 2359304 | tf_op jit(solution)/shard_map/ppermute | solution.py:162
  90.3 1.9 %collective-permute-done.19.other_ref = bf16[24,128,128]{2,1,0:T(8,128)(2,1)S(1)} collective-permute-done((bf16[24,128,128]{2,1,0:T(8,128)(2,1)S(1)}, bf16[24,128,128]{2,1,0:T(8,128)(2,1)S(1)}, u32[]{:S(2)}, u32[]{:S(2)}) %collective-permute-start.19) | collective-permute-done | bytes 786464 | tf_op jit(solution)/shard_map/ppermute | solution.py:162
  92.2 2.4 %level0.1 = (f32[4,128,128]{2,1,0:T(8,128)S(1)}, f32[2,128,128]{2,1,0:T(8,128)S(1)}, bf16[2,128,128]{2,1,0:T(8,128)(2,1)S(1)}) custom-call(s32[560]{0:T(1024)} %from_hbm.7, bf16[560,128,128]{2,1,0:T(8,128)(2,1)} %panels_hbm.7, f32[6,128,128]{2,1,0:T(8,128)} %copy-done.9, f32[40,128,128]{2,1,0:T(8,128)} %diag_hbm.9, s32[4]{0:T(128)S(1)} %pad_add_fusion.at_ref, ...), custom_call_target="tpu_custom_call" | custom-call | tf_op jit(solution)/shard_map/level0/pallas_call | solution.py:497
  94.7 0.7 copy-done.10
  95.4 0.7 copy-done.14
  96.0 1.5 broadcast_select_fusion
  97.6 7.4 %all-to-all-start.1 = ((bf16[64,128,128]{2,1,0:T(8,128)(2,1)}), bf16[64,128,128]{2,1,0:T(8,128)(2,1)S(1)}, u32[]{:S(2)}, u32[]{:S(2)}) async-start(bf16[64,128,128]{2,1,0:T(8,128)(2,1)} %broadcast_select_fusion), calls=%async_computation.1 | async-start | bytes 4194304 | tf_op jit(solution)/shard_map/all_to_all | solution.py:459
  105.0 1.4 copy-done.1
  106.4 1.4 copy-done.5
  107.8 5.2 %spread.1 = (bf16[64,128,128]{2,1,0:T(8,128)(2,1)S(1)}, bf16[64,128,128]{2,1,0:T(8,128)(2,1)}) custom-call(s32[4]{0:T(128)S(1)} %pad_add_fusion.at_ref, s32[2,1024]{1,0:T(2,128)S(1)} %get-tuple-element.28.picks_ref, bf16[128,48,128]{2,1,0:T(8,128)(2,1)S(1)} %copy-done.1, bf16[128,48,128]{2,1,0:T(8,128)(2,1)S(1)} %copy-done.5, ...), custom_call_target="tpu_custom_call" | custom-call | tf_op jit(solution)/shard_map/spread/pallas_call | solution.py:450
  113.0 1.3 copy-done.6
  114.9 19.6 %all-to-all-done.1.received_ref = bf16[64,128,128]{2,1,0:T(8,128)(2,1)S(1)} async-done(((bf16[64,128,128]{2,1,0:T(8,128)(2,1)}), bf16[64,128,128]{2,1,0:T(8,128)(2,1)S(1)}, u32[]{:S(2)}, u32[]{:S(2)}) %all-to-all-start.1) | async-done | bytes 2097184 | tf_op jit(solution)/shard_map/all_to_all | solution.py:459
  134.5 1.7 level1.1
  136.8 1.2 broadcast_select_fusion.1
  138.0 4.6 %all-to-all-start.2 = ((bf16[32,128,128]{2,1,0:T(8,128)(2,1)}), bf16[32,128,128]{2,1,0:T(8,128)(2,1)S(1)}, u32[]{:S(2)}, u32[]{:S(2)}) async-start(bf16[32,128,128]{2,1,0:T(8,128)(2,1)} %broadcast_select_fusion.1), calls=%async_computation.2 | async-start | bytes 2097152 | tf_op jit(solution)/shard_map/all_to_all | solution.py:459
  142.7 1.6 copy-done.7
  144.3 7.3 %leaf.3.right_ref = f32[32,128,128]{2,1,0:T(8,128)} custom-call(s32[560]{0:T(1024)S(1)} %copy-done.11, s32[4]{0:T(128)S(1)} %pad_add_fusion.at_ref, bf16[64,128,128]{2,1,0:T(8,128)(2,1)S(1)} %copy-done.7, bf16[64,128,128]{2,1,0:T(8,128)(2,1)} %collective-permute-done.20.other_ref, bf16[560,128,128]{2,1,0:T(8,128)(2,1)} %panels_hbm.7, f32[32,128,128]{2,1,0:T(8,128)} %bitcast.27), custom_call_target="tpu_custom_call" | custom-call | tf_op jit(solution)/shard_map/leaf/pallas_call | solution.py:365
  151.6 5.9 %leaf.4.right_ref = f32[32,128,128]{2,1,0:T(8,128)} custom-call(s32[560]{0:T(1024)S(1)} %copy-done.11, bf16[64,128,128]{2,1,0:T(8,128)(2,1)S(1)} %all-to-all-done.1.received_ref, bf16[560,128,128]{2,1,0:T(8,128)(2,1)} %panels_hbm.7, f32[32,128,128]{2,1,0:T(8,128)} %leaf.3.right_ref), custom_call_target="tpu_custom_call" | custom-call | tf_op jit(solution)/shard_map/leaf/pallas_call | solution.py:365
  157.5 1.2 all-to-all-done.2.received_ref
  158.7 1.7 level2.1
  160.5 0.9 broadcast_select_fusion.2
  161.4 4.7 %all-to-all-start.3 = ((bf16[16,128,128]{2,1,0:T(8,128)(2,1)}), bf16[16,128,128]{2,1,0:T(8,128)(2,1)S(1)}, u32[]{:S(2)}, u32[]{:S(2)}) async-start(bf16[16,128,128]{2,1,0:T(8,128)(2,1)} %broadcast_select_fusion.2), calls=%async_computation.3 | async-start | bytes 1048576 | tf_op jit(solution)/shard_map/all_to_all | solution.py:459
  166.1 5.9 %leaf.5.right_hbm = f32[32,128,128]{2,1,0:T(8,128)} custom-call(s32[560]{0:T(1024)S(1)} %copy-done.12, bf16[32,128,128]{2,1,0:T(8,128)(2,1)S(1)} %all-to-all-done.2.received_ref, bf16[560,128,128]{2,1,0:T(8,128)(2,1)} %panels_hbm.7, f32[32,128,128]{2,1,0:T(8,128)} %leaf.4.right_ref), custom_call_target="tpu_custom_call" | custom-call | tf_op jit(solution)/shard_map/leaf/pallas_call | solution.py:365
  172.0 0.8 pad_maximum_fusion
  172.8 3.2 %all-to-all-done.3.received_ref = bf16[16,128,128]{2,1,0:T(8,128)(2,1)S(1)} async-done(((bf16[16,128,128]{2,1,0:T(8,128)(2,1)}), bf16[16,128,128]{2,1,0:T(8,128)(2,1)S(1)}, u32[]{:S(2)}, u32[]{:S(2)}) %all-to-all-start.3) | async-done | bytes 524320 | tf_op jit(solution)/shard_map/all_to_all | solution.py:459
  176.1 5.3 %last.1 = f32[32,128,128]{2,1,0:T(8,128)} custom-call(s32[560]{0:T(1024)} %from_hbm.7, bf16[16,128,128]{2,1,0:T(8,128)(2,1)S(1)} %all-to-all-done.3.received_ref, bf16[560,128,128]{2,1,0:T(8,128)(2,1)} %panels_hbm.7, f32[32,128,128]{2,1,0:T(8,128)} %leaf.5.right_hbm, f32[40,128,128]{2,1,0:T(8,128)} %diag_hbm.9), custom_call_target="tpu_custom_call" | custom-call | tf_op jit(solution)/shard_map/last/pallas_call | solution.py:519
  (80 shorter events, 7.6 us)
Async XLA Ops:
  0.6 1.0 copy-start.8
  1.7 0.7 copy-start.16
  2.4 0.7 copy-start.17
  35.1 3.8 %collective-permute-start.13 = (bf16[2,32,128]{2,1,0:T(8,128)(2,1)S(1)}, bf16[2,32,128]{2,1,0:T(8,128)(2,1)S(1)}, u32[]{:S(2)}, u32[]{:S(2)}) collective-permute-start(bf16[2,32,128]{2,1,0:T(8,128)(2,1)S(1)} %get-tuple-element.83), channel_id=1, source_target_pairs={{0,32},{1,33},{2,34},{3,35},{4,100},{5,101},{6,102},{7,103},{8,40}... | collective-permute-start | bytes 49160 | tf_op jit(solution)/shard_map/ppermute | solution.py:154
  36.6 3.9 %collective-permute-start.7 = (bf16[2,48,128]{2,1,0:T(8,128)(2,1)S(1)}, bf16[2,48,128]{2,1,0:T(8,128)(2,1)S(1)}, u32[]{:S(2)}, u32[]{:S(2)}) collective-permute-start(bf16[2,48,128]{2,1,0:T(8,128)(2,1)S(1)} %get-tuple-element.90), channel_id=1, source_target_pairs={{0,8},{1,9},{2,10},{3,11},{4,28},{5,29},{6,30},{7,31},{8,0},{9,1},... | collective-permute-start | bytes 73736 | tf_op jit(solution)/shard_map/ppermute | solution.py:154
  36.7 3.9 %collective-permute-start.1 = (bf16[2,48,128]{2,1,0:T(8,128)(2,1)S(1)}, bf16[2,48,128]{2,1,0:T(8,128)(2,1)S(1)}, u32[]{:S(2)}, u32[]{:S(2)}) collective-permute-start(bf16[2,48,128]{2,1,0:T(8,128)(2,1)S(1)} %get-tuple-element.91), channel_id=1, source_target_pairs={{0,1},{1,0},{2,3},{3,2},{4,7},{5,6},{6,5},{7,4},{8,9},{9,8},{10,11... | collective-permute-start | bytes 73736 | tf_op jit(solution)/shard_map/ppermute | solution.py:154
  39.0 3.2 %collective-permute-start.14 = (bf16[4,32,128]{2,1,0:T(8,128)(2,1)S(1)}, bf16[4,32,128]{2,1,0:T(8,128)(2,1)S(1)}, u32[]{:S(2)}, u32[]{:S(2)}) collective-permute-start(bf16[4,32,128]{2,1,0:T(8,128)(2,1)S(1)} %pad_maximum_fusion.9), channel_id=1, source_target_pairs={{0,96},{1,97},{2,98},{3,99},{4,36},{5,37},{6,38},{7,39},{8,104},{9... | collective-permute-start | bytes 98312 | tf_op jit(solution)/shard_map/ppermute | solution.py:154
  40.5 3.2 %collective-permute-start.8 = (bf16[4,48,128]{2,1,0:T(8,128)(2,1)S(1)}, bf16[4,48,128]{2,1,0:T(8,128)(2,1)S(1)}, u32[]{:S(2)}, u32[]{:S(2)}) collective-permute-start(bf16[4,48,128]{2,1,0:T(8,128)(2,1)S(1)} %pad_maximum_fusion.8), channel_id=1, source_target_pairs={{0,24},{1,25},{2,26},{3,27},{4,12},{5,13},{6,14},{7,15},{8,16},{9,... | collective-permute-start | bytes 147464 | tf_op jit(solution)/shard_map/ppermute | solution.py:154
  40.6 4.8 %collective-permute-start.2 = (bf16[4,48,128]{2,1,0:T(8,128)(2,1)S(1)}, bf16[4,48,128]{2,1,0:T(8,128)(2,1)S(1)}, u32[]{:S(2)}, u32[]{:S(2)}) collective-permute-start(bf16[4,48,128]{2,1,0:T(8,128)(2,1)S(1)} %pad_maximum_fusion.7), channel_id=1, source_target_pairs={{0,3},{1,2},{2,1},{3,0},{4,5},{5,4},{6,7},{7,6},{8,11},{9,10},{10,... | collective-permute-start | bytes 147464 | tf_op jit(solution)/shard_map/ppermute | solution.py:154
  42.2 6.5 %collective-permute-start.15 = (bf16[8,32,128]{2,1,0:T(8,128)(2,1)S(1)}, bf16[8,32,128]{2,1,0:T(8,128)(2,1)S(1)}, u32[]{:S(2)}, u32[]{:S(2)}) collective-permute-start(bf16[8,32,128]{2,1,0:T(8,128)(2,1)S(1)} %pad_maximum_fusion.6), channel_id=1, source_target_pairs={{0,1},{1,0},{2,3},{3,2},{4,7},{5,6},{6,5},{7,4},{8,9},{9,8},{10,11... | collective-permute-start | bytes 196616 | tf_op jit(solution)/shard_map/ppermute | solution.py:154
  43.8 5.9 %collective-permute-start.9 = (bf16[8,48,128]{2,1,0:T(8,128)(2,1)S(1)}, bf16[8,48,128]{2,1,0:T(8,128)(2,1)S(1)}, u32[]{:S(2)}, u32[]{:S(2)}) collective-permute-start(bf16[8,48,128]{2,1,0:T(8,128)(2,1)S(1)} %pad_maximum_fusion.5), channel_id=1, source_target_pairs={{0,32},{1,33},{2,34},{3,35},{4,100},{5,101},{6,102},{7,103},{8,40}... | collective-permute-start | bytes 294920 | tf_op jit(solution)/shard_map/ppermute | solution.py:154
  45.4 4.8 %collective-permute-start.3 = (bf16[8,48,128]{2,1,0:T(8,128)(2,1)S(1)}, bf16[8,48,128]{2,1,0:T(8,128)(2,1)S(1)}, u32[]{:S(2)}, u32[]{:S(2)}) collective-permute-start(bf16[8,48,128]{2,1,0:T(8,128)(2,1)S(1)} %pad_maximum_fusion.4), channel_id=1, source_target_pairs={{0,8},{1,9},{2,10},{3,11},{4,28},{5,29},{6,30},{7,31},{8,0},{9,1},... | collective-permute-start | bytes 294920 | tf_op jit(solution)/shard_map/ppermute | solution.py:154
  48.7 11.3 %collective-permute-start.16 = (bf16[16,32,128]{2,1,0:T(8,128)(2,1)S(1)}, bf16[16,32,128]{2,1,0:T(8,128)(2,1)S(1)}, u32[]{:S(2)}, u32[]{:S(2)}) collective-permute-start(bf16[16,32,128]{2,1,0:T(8,128)(2,1)S(1)} %pad_maximum_fusion.3), channel_id=1, source_target_pairs={{0,3},{1,2},{2,1},{3,0},{4,5},{5,4},{6,7},{7,6},{8,11},{9,10},{10,... | collective-permute-start | bytes 393224 | tf_op jit(solution)/shard_map/ppermute | solution.py:154
  49.7 4.9 %collective-permute-start.10 = (bf16[16,48,128]{2,1,0:T(8,128)(2,1)S(1)}, bf16[16,48,128]{2,1,0:T(8,128)(2,1)S(1)}, u32[]{:S(2)}, u32[]{:S(2)}) collective-permute-start(bf16[16,48,128]{2,1,0:T(8,128)(2,1)S(1)} %pad_maximum_fusion.2), channel_id=1, source_target_pairs={{0,96},{1,97},{2,98},{3,99},{4,36},{5,37},{6,38},{7,39},{8,104},{9... | collective-permute-start | bytes 589832 | tf_op jit(solution)/shard_map/ppermute | solution.py:154
  50.2 6.9 %collective-permute-start.4 = (bf16[16,48,128]{2,1,0:T(8,128)(2,1)S(1)}, bf16[16,48,128]{2,1,0:T(8,128)(2,1)S(1)}, u32[]{:S(2)}, u32[]{:S(2)}) collective-permute-start(bf16[16,48,128]{2,1,0:T(8,128)(2,1)S(1)} %pad_maximum_fusion.1), channel_id=1, source_target_pairs={{0,24},{1,25},{2,26},{3,27},{4,12},{5,13},{6,14},{7,15},{8,16},{9,... | collective-permute-start | bytes 589832 | tf_op jit(solution)/shard_map/ppermute | solution.py:154
  55.3 7.8 %collective-permute-start.11 = (bf16[32,48,128]{2,1,0:T(8,128)(2,1)S(1)}, bf16[32,48,128]{2,1,0:T(8,128)(2,1)S(1)}, u32[]{:S(2)}, u32[]{:S(2)}) collective-permute-start(bf16[32,48,128]{2,1,0:T(8,128)(2,1)S(1)} %get-tuple-element.58), channel_id=1, source_target_pairs={{0,1},{1,0},{2,3},{3,2},{4,7},{5,6},{6,5},{7,4},{8,9},{9,8},{10,11... | collective-permute-start | bytes 1179656 | tf_op jit(solution)/shard_map/ppermute | solution.py:154
  57.9 7.8 %collective-permute-start.5 = (bf16[32,48,128]{2,1,0:T(8,128)(2,1)S(1)}, bf16[32,48,128]{2,1,0:T(8,128)(2,1)S(1)}, u32[]{:S(2)}, u32[]{:S(2)}) collective-permute-start(bf16[32,48,128]{2,1,0:T(8,128)(2,1)S(1)} %get-tuple-element.61), channel_id=1, source_target_pairs={{0,32},{1,33},{2,34},{3,35},{4,100},{5,101},{6,102},{7,103},{8,40}... | collective-permute-start | bytes 1179656 | tf_op jit(solution)/shard_map/ppermute | solution.py:154
  60.8 6.4 %collective-permute-start.17 = (bf16[32,32,128]{2,1,0:T(8,128)(2,1)S(1)}, bf16[32,32,128]{2,1,0:T(8,128)(2,1)S(1)}, u32[]{:S(2)}, u32[]{:S(2)}) collective-permute-start(bf16[32,32,128]{2,1,0:T(8,128)(2,1)S(1)} %get-tuple-element.64), channel_id=1, source_target_pairs={{0,8},{1,9},{2,10},{3,11},{4,28},{5,29},{6,30},{7,31},{8,0},{9,1},... | collective-permute-start | bytes 786440 | tf_op jit(solution)/shard_map/ppermute | solution.py:154
  64.0 2.6 %copy-start.2 = (bf16[128,48,128]{2,1,0:T(8,128)(2,1)}, bf16[128,48,128]{2,1,0:T(8,128)(2,1)S(1)}, u32[]{:S(2)}) copy-start(bf16[128,48,128]{2,1,0:T(8,128)(2,1)S(1)} %get-tuple-element.51) | copy-start | bytes 4718596
  64.0 14.0 %collective-permute-start.12 = (bf16[64,48,128]{2,1,0:T(8,128)(2,1)}, bf16[64,48,128]{2,1,0:T(8,128)(2,1)}, u32[]{:S(2)}, u32[]{:S(2)}) collective-permute-start(bf16[64,48,128]{2,1,0:T(8,128)(2,1)} %get-tuple-element.50), channel_id=1, source_target_pairs={{0,3},{1,2},{2,1},{3,0},{4,5},{5,4},{6,7},{7,6},{8,11},{9,10},{10,... | collective-permute-start | bytes 2359304 | tf_op jit(solution)/shard_map/ppermute | solution.py:154
  66.6 12.7 %collective-permute-start.6 = (bf16[64,48,128]{2,1,0:T(8,128)(2,1)}, bf16[64,48,128]{2,1,0:T(8,128)(2,1)}, u32[]{:S(2)}, u32[]{:S(2)}) collective-permute-start(bf16[64,48,128]{2,1,0:T(8,128)(2,1)} %get-tuple-element.52), channel_id=1, source_target_pairs={{0,96},{1,97},{2,98},{3,99},{4,36},{5,37},{6,38},{7,39},{8,104},{9... | collective-permute-start | bytes 2359304 | tf_op jit(solution)/shard_map/ppermute | solution.py:154
  68.0 8.8 %collective-permute-start.18 = (bf16[64,32,128]{2,1,0:T(8,128)(2,1)}, bf16[64,32,128]{2,1,0:T(8,128)(2,1)}, u32[]{:S(2)}, u32[]{:S(2)}) collective-permute-start(bf16[64,32,128]{2,1,0:T(8,128)(2,1)} %get-tuple-element.54), channel_id=1, source_target_pairs={{0,24},{1,25},{2,26},{3,27},{4,12},{5,13},{6,14},{7,15},{8,16},{9,... | collective-permute-start | bytes 1572872 | tf_op jit(solution)/shard_map/ppermute | solution.py:154
  68.7 10.6 %copy-start.19 = (s32[24]{0:T(128)}, s32[24]{0:T(128)S(1)}, u32[]{:S(2)}) copy-start(s32[24]{0:T(128)S(1)} %slice.42.mine_ref) | copy-start | bytes 292
  68.7 12.5 %collective-permute-start = (s32[24]{0:T(128)S(1)}, s32[24]{0:T(128)}, u32[]{:S(2)}, u32[]{:S(2)}) collective-permute-start(s32[24]{0:T(128)S(1)} %slice.42.mine_ref), channel_id=1, source_target_pairs={{0,4},{1,5},{2,6},{3,7},{4,0},{5,1},{6,2},{7,3},{8,12},{9,13},{10,... | collective-permute-start | bytes 296 | tf_op jit(solution)/shard_map/ppermute | solution.py:162
  75.9 2.1 %copy-start.3 = (bf16[128,48,128]{2,1,0:T(8,128)(2,1)S(1)}, bf16[128,48,128]{2,1,0:T(8,128)(2,1)}, u32[]{:S(2)}) copy-start(bf16[128,48,128]{2,1,0:T(8,128)(2,1)} %copy-done.2) | copy-start | bytes 4718596
  76.7 4.4 %copy-start.9 = (f32[6,128,128]{2,1,0:T(8,128)}, f32[6,128,128]{2,1,0:T(8,128)S(1)}, u32[]{:S(2)}) copy-start(f32[6,128,128]{2,1,0:T(8,128)S(1)} %get-tuple-element.27.rights_hbm) | copy-start | bytes 1179652
  79.3 15.4 %copy-start.4 = (bf16[128,48,128]{2,1,0:T(8,128)(2,1)}, bf16[128,48,128]{2,1,0:T(8,128)(2,1)S(1)}, u32[]{:S(2)}) copy-start(bf16[128,48,128]{2,1,0:T(8,128)(2,1)S(1)} %constant_dynamic-update-slice_fusion.29.b_ref) | copy-start | bytes 4718596
  79.3 1.8 %copy-start.20 = (s32[24]{0:T(128)S(1)}, s32[24]{0:T(128)}, u32[]{:S(2)}) copy-start(s32[24]{0:T(128)} %copy-done.19) | copy-start | bytes 292
  81.1 2.3 %copy-start = (bf16[128,48,128]{2,1,0:T(8,128)(2,1)}, bf16[128,48,128]{2,1,0:T(8,128)(2,1)S(1)}, u32[]{:S(2)}) copy-start(bf16[128,48,128]{2,1,0:T(8,128)(2,1)S(1)} %constant_dynamic-update-slice_fusion.11.a_ref) | copy-start | bytes 4718596
  81.2 9.1 %copy-start.18 = (s32[1,240]{1,0:T(1,128)S(1)}, s32[1,240]{1,0:T(1,128)}, u32[]{:S(2)}) copy-start(s32[1,240]{1,0:T(1,128)} %send_ref.1) | copy-start | bytes 2884
  83.5 8.7 %collective-permute-start.19 = (bf16[24,128,128]{2,1,0:T(8,128)(2,1)S(1)}, bf16[24,128,128]{2,1,0:T(8,128)(2,1)S(1)}, u32[]{:S(2)}, u32[]{:S(2)}) collective-permute-start(bf16[24,128,128]{2,1,0:T(8,128)(2,1)S(1)} %get-tuple-element.31), channel_id=1, source_target_pairs={{0,4},{1,5},{2,6},{3,7},{4,0},{5,1},{6,2},{7,3},{8,12},{9,13},{10,... | collective-permute-start | bytes 2359304 | tf_op jit(solution)/shard_map/ppermute | solution.py:162
  94.7 0.7 copy-start.10
  95.4 0.7 copy-start.14
  97.6 36.9 %all-to-all-start.1 = ((bf16[64,128,128]{2,1,0:T(8,128)(2,1)}), bf16[64,128,128]{2,1,0:T(8,128)(2,1)S(1)}, u32[]{:S(2)}, u32[]{:S(2)}) async-start(bf16[64,128,128]{2,1,0:T(8,128)(2,1)} %broadcast_select_fusion), calls=%async_computation.1 | async-start | bytes 4194304 | tf_op jit(solution)/shard_map/all_to_all | solution.py:459
  105.0 1.4 copy-start.1
  106.4 1.4 copy-start.5
  113.0 1.3 copy-start.6
  114.3 28.4 %collective-permute-start.20 = (bf16[64,128,128]{2,1,0:T(8,128)(2,1)}, bf16[64,128,128]{2,1,0:T(8,128)(2,1)}, u32[]{:S(2)}, u32[]{:S(2)}) collective-permute-start(bf16[64,128,128]{2,1,0:T(8,128)(2,1)} %get-tuple-element.43), channel_id=1, source_target_pairs={{0,4},{1,5},{2,6},{3,7},{4,0},{5,1},{6,2},{7,3},{8,12},{9,13},{10,... | collective-permute-start | bytes 6291464 | tf_op jit(solution)/shard_map/ppermute | solution.py:162
  136.1 0.7 copy-start.13
  136.8 5.9 %copy-start.11 = (s32[560]{0:T(1024)S(1)}, s32[560]{0:T(1024)}, u32[]{:S(2)}) copy-start(s32[560]{0:T(1024)} %from_hbm.7) | copy-start | bytes 6724
  138.0 20.7 %all-to-all-start.2 = ((bf16[32,128,128]{2,1,0:T(8,128)(2,1)}), bf16[32,128,128]{2,1,0:T(8,128)(2,1)S(1)}, u32[]{:S(2)}, u32[]{:S(2)}) async-start(bf16[32,128,128]{2,1,0:T(8,128)(2,1)} %broadcast_select_fusion.1), calls=%async_computation.2 | async-start | bytes 2097152 | tf_op jit(solution)/shard_map/all_to_all | solution.py:459
  142.7 1.6 copy-start.7
  160.4 5.6 %copy-start.12 = (s32[560]{0:T(1024)S(1)}, s32[560]{0:T(1024)}, u32[]{:S(2)}) copy-start(s32[560]{0:T(1024)} %from_hbm.7) | copy-start | bytes 6724
  161.4 14.7 %all-to-all-start.3 = ((bf16[16,128,128]{2,1,0:T(8,128)(2,1)}), bf16[16,128,128]{2,1,0:T(8,128)(2,1)S(1)}, u32[]{:S(2)}, u32[]{:S(2)}) async-start(bf16[16,128,128]{2,1,0:T(8,128)(2,1)} %broadcast_select_fusion.2), calls=%async_computation.3 | async-start | bytes 1048576 | tf_op jit(solution)/shard_map/all_to_all | solution.py:459
  166.1 5.9 %copy-start.15 = (f32[2,128,128]{2,1,0:T(8,128)S(1)}, f32[2,128,128]{2,1,0:T(8,128)}, u32[]{:S(2)}) copy-start(f32[2,128,128]{2,1,0:T(8,128)} %copy-done.14) | copy-start | bytes 393220

commit v6 on v5

--- a/solution.py
+++ b/solution.py
@@ -147,15 +147,24 @@
     return pairs
 
 
-def gather_core(sent):
+def gather_core(sent, early):
+    sent, early = lax.optimization_barrier((sent, early))
     parts = [sent[:, a:b] for a, b in zip(CUTS, CUTS[1:])]
-    for step in range(2 * len(ORDERS[0])):
+    steps = 2 * len(ORDERS[0])
+    for step in range(steps):
         arriving = [
             lax.ppermute(part, AXES, step_pairs(order[step // 2], step % 2))
             for part, order in zip(parts, ORDERS)
         ]
-        parts = [jnp.concatenate(both, axis=0) for both in zip(parts, arriving)]
-    return parts
+        if step == 0:
+            early = swap_core(early)
+            early, arriving[2] = lax.optimization_barrier((early, arriving[2]))
+        if step < steps - 1:
+            parts = [
+                lax.optimization_barrier(jnp.concatenate(both, axis=0))
+                for both in zip(parts, arriving)
+            ]
+    return [x for both in zip(parts, arriving) for x in both], early
 
 
 def swap_core(x):
@@ -181,27 +190,31 @@
         "y": position // (2 * SIDE * SIDE),
     }
     spots = {axis: place(axis, there[axis]) for axis in there}
-    for part, order in zip(parts, ORDERS):
+    for held, came, order in zip(parts[::2], parts[1::2], ORDERS):
         at = 0
         for axis in reversed(order):
             at = at * SIDE + spots[axis]
-        yield part[at * TS + pick]
-
-
-def near_kernel(at_ref, picks_ref, mine_ref, theirs_ref, a_ref, b_ref, c_ref, own_ref, other_ref):
-    for which, (from_ref, out_ref) in enumerate(((mine_ref, own_ref), (theirs_ref, other_ref))):
-        for e in range(out_ref.shape[0]):
-            position = from_ref[e]
-            blocks = take((a_ref, b_ref, c_ref), at_ref, position, picks_ref[which, position * 8])
-            for first, block in zip(CUTS, blocks):
-                out_ref[e, first : first + block.shape[0]] = block
-
-
-def spread_kernel(at_ref, picks_ref, a_ref, b_ref, c_ref, own_ref, other_ref):
+        at = at * TS + pick
+        half = held.shape[0]
+        yield jnp.where(at < half, held[at & (half - 1)], came[at & (half - 1)])
+
+
+def near_kernel(which, at_ref, picks_ref, from_ref, *refs):
+    *parts, out_ref = refs
+    for e in range(out_ref.shape[0]):
+        position = from_ref[e]
+        blocks = take(parts, at_ref, position, picks_ref[which, position * 8])
+        for first, block in zip(CUTS, blocks):
+            out_ref[e, first : first + block.shape[0]] = block
+
+
+def spread_kernel(at_ref, picks_ref, *refs):
+    *parts, own_ref, other_ref = refs
+
     def body(i, carry):
         position = i // SIDE * (2 * SIDE) + at_ref[3] * SIDE + i % SIDE
         for which, out_ref in enumerate((own_ref, other_ref)):
-            blocks = take((a_ref, b_ref, c_ref), at_ref, position, picks_ref[which, position * 8])
+            blocks = take(parts, at_ref, position, picks_ref[which, position * 8])
             for first, block in zip(CUTS, blocks):
                 out_ref[i, first : first + block.shape[0]] = block
         return carry
@@ -422,17 +435,19 @@
     at = jnp.stack([lax.axis_index("panel"), leaf // (2 * SIDE), leaf // 2 % SIDE, leaf % 2])
     near = KP * TS * (LEVELS - 1)
     mine = panel_from[:near]
-    theirs = swap_core(mine)
-    gathered = gather_core(sent)
-    own, other = pl.pallas_call(
-        near_kernel,
-        out_shape=(b16(near, BS, rhs), b16(near, BS, rhs)),
-        in_specs=[in_smem] * 4 + [whole()] * 3,
-        out_specs=(whole(), whole()),
-        compiler_params=VMEM,
-        name="near",
-    )(at, picks, mine, theirs, *gathered)
-    other = swap_core(other)
+    gathered, theirs = gather_core(sent, mine)
+    near_tiles = [
+        pl.pallas_call(
+            functools.partial(near_kernel, which),
+            out_shape=b16(near, BS, rhs),
+            in_specs=[in_smem] * 3 + [whole()] * 6,
+            out_specs=whole(),
+            compiler_params=VMEM,
+            name=f"near{which}",
+        )(at, picks, wanted, *gathered)
+        for which, wanted in enumerate((mine, theirs))
+    ]
+    own, other = near_tiles[0], swap_core(near_tiles[1])
     leaf_right = leaf_noise.reshape(TL, BS, rhs)
     all_solved = [solved]
     offset = 0
@@ -450,7 +465,7 @@
                 own_all, other_all = pl.pallas_call(
                     spread_kernel,
                     out_shape=(b16(owners // 2, BS, rhs), b16(owners // 2, BS, rhs)),
-                    in_specs=[in_smem] * 2 + [whole()] * 3,
+                    in_specs=[in_smem] * 2 + [whole()] * 6,
                     out_specs=(whole(), whole()),
                     compiler_params=VMEM,
                     name="spread",

time: 183 us -> 179 us (0.978)
  waiting for transfers between devices: 36.3 us -> 66.9 us
  blocking collectives: 28.2 us -> 0 us
  local copies, waits for them, and re-layouts: 26.9 us -> 10.3 us
  starting transfers between devices: 42.5 us -> 47.9 us
  Pallas kernels: 41.7 us -> 46.6 us
    all_to_all x1 -> x0, blocking collectives: 28.2 us -> none  [per_device(): arrived = lax.all_to_all(outgoing, AXES, 0, 0, tiled=True)]
    ppermute x18, waiting for transfers between devices: 10.3 us -> 27.8 us  [gather_core(): lax.ppermute(part, AXES, step_pairs(order[step // 2], step % 2))]
    all_to_all x0 -> x1, waiting for transfers between devices: none -> 16.3 us  [per_device(): arrived = lax.all_to_all(outgoing, AXES, 0, 0, tiled=True)]
    all_to_all x0 -> x1, starting transfers between devices: none -> 11.5 us  [per_device(): arrived = lax.all_to_all(outgoing, AXES, 0, 0, tiled=True)]
    unnamed x56 -> x42, local copies, waits for them, and re-layouts: 19.4 us -> 9.58 us
    concatenate x6 -> x0, local copies, waits for them, and re-layouts: 6.75 us -> none  [gather_core(): parts = [jnp.concatenate(both, axis=0) for both in zip(parts, arriving)]]
    ppermute x3, starting transfers between devices: 14.6 us -> 8.65 us  [swap_core(): return lax.ppermute(x, AXES, [(i, i ^ SIDE) for i in range(2 * SIDE ** 3)])]
    pallas_call x1 -> x2, Pallas kernels: 2.27 us -> 4.5 us  [per_device(): pl.pallas_call(functools.partial(near_kernel, which), out_shape=b16(near,...]
  transfers between devices with their start and end apart: 24 -> 25, of which waited for: 13 -> 15; matrix products, arithmetic and copies ran while one was open for 10% -> 2% of each run, Pallas kernels for 15% -> 17%
where the time goes in v6:
time: 179 us; the launch traced here: 178 us
  waiting for transfers between devices  66.9 us (37%)
  starting transfers between devices  47.9 us (27%)
  Pallas kernels  46.6 us (26%)
  local copies, waits for them, and re-layouts  10.3 us (6%)
  other arithmetic  4.99 us (3%)
    ppermute x18, waiting for transfers between devices, gather_core(): lax.ppermute(part, AXES, step_pairs(order[step // 2], step % 2))  27.8 us
    all_to_all x3, waiting for transfers between devices, per_device(): lax.all_to_all(buffer, AXES, 0, 0, axis_index_groups=groups, tiled=True)  22.9 us
    pallas_call x3, Pallas kernels, leaf_pass(): pl.pallas_call(kernel, grid_spec=pltpu.PrefetchScalarGridSpec(num_scalar_...  19.1 us
    all_to_all x1, waiting for transfers between devices, per_device(): arrived = lax.all_to_all(outgoing, AXES, 0, 0, tiled=True)  16.3 us
    all_to_all x3, starting transfers between devices, per_device(): lax.all_to_all(buffer, AXES, 0, 0, axis_index_groups=groups, tiled=True)  14.9 us
    ppermute x18, starting transfers between devices, gather_core(): lax.ppermute(part, AXES, step_pairs(order[step // 2], step % 2))  12.8 us
    all_to_all x1, starting transfers between devices, per_device(): arrived = lax.all_to_all(outgoing, AXES, 0, 0, tiled=True)  11.5 us
    unnamed x42, local copies, waits for them, and re-layouts  9.58 us
  transfers between devices with their start and end apart: 25, of which 15 were waited for; matrix products, arithmetic and copies ran while one was open for 2% of the time, Pallas kernels for 17%

profile of v6, /device:TPU:1, one launch (start us, length us, event | category | flops | bytes accessed | tf_op | source)
XLA Modules:
  0.0 177.8 jit_solution(5808155791345393378)
XLA Ops:
  0.6 1.0 copy-done.6
  1.7 0.7 copy-done.14
  2.4 0.7 copy-done.15
  3.0 2.7 %pack.1 = bf16[128,8,384]{2,1,0:T(8,128)(2,1)} custom-call(s32[1,1024]{1,0:T(1,128)S(1)} %bitcast.26, s32[1,240]{1,0:T(1,128)S(1)} %copy-done.15, f32[1024,128]{1,0:T(8,128)S(1)} %copy-done.6), custom_call_target="tpu_custom_call" | custom-call | tf_op jit(solution)/shard_map/pack/pallas_call | solution.py:400
  5.7 11.5 %all-to-all-start = ((bf16[128,8,384]{2,1,0:T(8,128)(2,1)}), bf16[128,8,384]{2,1,0:T(8,128)(2,1)S(1)}, u32[]{:S(2)}, u32[]{:S(2)}) async-start(bf16[128,8,384]{2,1,0:T(8,128)(2,1)} %pack.1), calls=%async_computation | async-start | bytes 1572864 | tf_op jit(solution)/shard_map/all_to_all | solution.py:408
  17.2 0.7 slice.42.from_ref
  17.9 16.3 %all-to-all-done.arrived_ref = bf16[128,8,384]{2,1,0:T(8,128)(2,1)S(1)} async-done(((bf16[128,8,384]{2,1,0:T(8,128)(2,1)}), bf16[128,8,384]{2,1,0:T(8,128)(2,1)S(1)}, u32[]{:S(2)}, u32[]{:S(2)}) %all-to-all-start) | async-done | bytes 786464 | tf_op jit(solution)/shard_map/all_to_all | solution.py:408
  34.2 1.4 first.1
  35.6 0.9 collective-permute-start.13
  36.6 0.3 collective-permute-start.6
  36.8 1.1 collective-permute-start
  37.9 1.6 collective-permute-done.13
  39.5 1.0 collective-permute-done.6
  40.5 0.2 collective-permute-done
  40.7 0.2 collective-permute-start.1
  40.9 2.5 %collective-permute-done.7 = bf16[4,48,128]{2,1,0:T(8,128)(2,1)S(1)} collective-permute-done((bf16[4,48,128]{2,1,0:T(8,128)(2,1)S(1)}, bf16[4,48,128]{2,1,0:T(8,128)(2,1)S(1)}, u32[]{:S(2)}, u32[]{:S(2)}) %collective-permute-start.7) | collective-permute-done | bytes 49184 | tf_op jit(solution)/shard_map/ppermute | solution.py:156
  43.5 1.9 %collective-permute-start.8 = (bf16[8,48,128]{2,1,0:T(8,128)(2,1)S(1)}, bf16[8,48,128]{2,1,0:T(8,128)(2,1)S(1)}, u32[]{:S(2)}, u32[]{:S(2)}) collective-permute-start(bf16[8,48,128]{2,1,0:T(8,128)(2,1)S(1)} %pad_maximum_fusion.11), channel_id=1, source_target_pairs={{0,32},{1,33},{2,34},{3,35},{4,100},{5,101},{6,102},{7,103},{8,40}... | collective-permute-start | bytes 294920 | tf_op jit(solution)/shard_map/ppermute | solution.py:156
  45.4 0.8 collective-permute-start.2
  46.2 2.0 %collective-permute-done.8 = bf16[8,48,128]{2,1,0:T(8,128)(2,1)S(1)} collective-permute-done((bf16[8,48,128]{2,1,0:T(8,128)(2,1)S(1)}, bf16[8,48,128]{2,1,0:T(8,128)(2,1)S(1)}, u32[]{:S(2)}, u32[]{:S(2)}) %collective-permute-start.8) | collective-permute-done | bytes 98336 | tf_op jit(solution)/shard_map/ppermute | solution.py:156
  48.3 1.8 %collective-permute-done.2 = bf16[8,48,128]{2,1,0:T(8,128)(2,1)S(1)} collective-permute-done((bf16[8,48,128]{2,1,0:T(8,128)(2,1)S(1)}, bf16[8,48,128]{2,1,0:T(8,128)(2,1)S(1)}, u32[]{:S(2)}, u32[]{:S(2)}) %collective-permute-start.2) | collective-permute-done | bytes 98336 | tf_op jit(solution)/shard_map/ppermute | solution.py:156
  50.2 0.1 collective-permute-start.3
  50.3 1.1 collective-permute-start.15
  51.4 1.4 collective-permute-done.9
  52.9 1.4 collective-permute-start.10
  54.2 0.6 collective-permute-done.3
  54.8 1.1 collective-permute-start.4
  56.0 0.2 collective-permute-start.16
  56.1 3.7 %collective-permute-done.16 = bf16[16,32,128]{2,1,0:T(8,128)(2,1)S(1)} collective-permute-done((bf16[16,32,128]{2,1,0:T(8,128)(2,1)S(1)}, bf16[16,32,128]{2,1,0:T(8,128)(2,1)S(1)}, u32[]{:S(2)}, u32[]{:S(2)}) %collective-permute-start.16) | collective-permute-done | bytes 131104 | tf_op jit(solution)/shard_map/ppermute | solution.py:156
  59.9 3.5 %collective-permute-start.17 = (bf16[32,32,128]{2,1,0:T(8,128)(2,1)S(1)}, bf16[32,32,128]{2,1,0:T(8,128)(2,1)S(1)}, u32[]{:S(2)}, u32[]{:S(2)}) collective-permute-start(bf16[32,32,128]{2,1,0:T(8,128)(2,1)S(1)} %pad_maximum_fusion.6), channel_id=1, source_target_pairs={{0,8},{1,9},{2,10},{3,11},{4,28},{5,29},{6,30},{7,31},{8,0},{9,1},... | collective-permute-start | bytes 786440 | tf_op jit(solution)/shard_map/ppermute | solution.py:156
  63.5 0.1 collective-permute-start.11
  63.7 0.1 collective-permute-start.5
  63.8 3.4 %collective-permute-done.17 = bf16[32,32,128]{2,1,0:T(8,128)(2,1)S(1)} collective-permute-done((bf16[32,32,128]{2,1,0:T(8,128)(2,1)S(1)}, bf16[32,32,128]{2,1,0:T(8,128)(2,1)S(1)}, u32[]{:S(2)}, u32[]{:S(2)}) %collective-permute-start.17) | collective-permute-done | bytes 262176 | tf_op jit(solution)/shard_map/ppermute | solution.py:156
  67.2 0.1 collective-permute-start.18
  67.4 0.7 order.1
  68.1 0.7 copy-done.7
  68.9 9.5 %collective-permute-done.18.refs_5_ = bf16[64,32,128]{2,1,0:T(8,128)(2,1)S(1)} collective-permute-done((bf16[64,32,128]{2,1,0:T(8,128)(2,1)S(1)}, bf16[64,32,128]{2,1,0:T(8,128)(2,1)S(1)}, u32[]{:S(2)}, u32[]{:S(2)}) %collective-permute-start.18) | collective-permute-done | bytes 524320 | tf_op jit(solution)/shard_map/ppermute | solution.py:156
  78.4 0.6 copy-done.20
  79.1 2.3 %near1.1 = bf16[24,128,128]{2,1,0:T(8,128)(2,1)S(1)} custom-call(s32[4]{0:T(128)S(1)} %pad_add_fusion.at_ref, s32[2,1024]{1,0:T(2,128)S(1)} %get-tuple-element.33.picks_ref, s32[24]{0:T(128)S(1)} %copy-done.20, bf16[64,48,128]{2,1,0:T(8,128)(2,1)S(1)} %pad_maximum_fusion.refs_0_, bf16[64,48,128]{2,1,0:T(8,128)(2,1)} %collective-permute-done.5.refs_1_, ...), custom_call_target="tpu_custom_call" | custom-call | tf_op jit(solution)/shard_map/near1/pallas_call | solution.py:440
  81.3 8.1 %collective-permute-start.19 = (bf16[24,128,128]{2,1,0:T(8,128)(2,1)S(1)}, bf16[24,128,128]{2,1,0:T(8,128)(2,1)S(1)}, u32[]{:S(2)}, u32[]{:S(2)}) collective-permute-start(bf16[24,128,128]{2,1,0:T(8,128)(2,1)S(1)} %near1.1), channel_id=1, source_target_pairs={{0,4},{1,5},{2,6},{3,7},{4,0},{5,1},{6,2},{7,3},{8,12},{9,13},{10,... | collective-permute-start | bytes 2359304 | tf_op jit(solution)/shard_map/ppermute | solution.py:171
  89.5 2.2 %near0.1.own_ref = bf16[24,128,128]{2,1,0:T(8,128)(2,1)S(1)} custom-call(s32[4]{0:T(128)S(1)} %pad_add_fusion.at_ref, s32[2,1024]{1,0:T(2,128)S(1)} %get-tuple-element.33.picks_ref, s32[24]{0:T(128)S(1)} %copy-done.18, bf16[64,48,128]{2,1,0:T(8,128)(2,1)S(1)} %pad_maximum_fusion.refs_0_, bf16[64,48,128]{2,1,0:T(8,128)(2,1)} %collective-permute-done.5.refs_1_, ...), custom_call_target="tpu_custom_call" | custom-call | tf_op jit(solution)/shard_map/near0/pallas_call | solution.py:440
  91.8 2.4 %level0.1 = (f32[4,128,128]{2,1,0:T(8,128)S(1)}, f32[2,128,128]{2,1,0:T(8,128)S(1)}, bf16[2,128,128]{2,1,0:T(8,128)(2,1)S(1)}) custom-call(s32[560]{0:T(1024)} %from_hbm.7, bf16[560,128,128]{2,1,0:T(8,128)(2,1)} %panels_hbm.7, f32[6,128,128]{2,1,0:T(8,128)} %copy-done.7, f32[40,128,128]{2,1,0:T(8,128)} %diag_hbm.9, s32[4]{0:T(128)S(1)} %pad_add_fusion.at_ref, ...), custom_call_target="tpu_custom_call" | custom-call | tf_op jit(solution)/shard_map/level0/pallas_call | solution.py:512
  94.2 1.5 broadcast_select_fusion
  95.8 5.6 %all-to-all-start.1 = ((bf16[64,128,128]{2,1,0:T(8,128)(2,1)}), bf16[64,128,128]{2,1,0:T(8,128)(2,1)S(1)}, u32[]{:S(2)}, u32[]{:S(2)}) async-start(bf16[64,128,128]{2,1,0:T(8,128)(2,1)} %broadcast_select_fusion), calls=%async_computation.1 | async-start | bytes 4194304 | tf_op jit(solution)/shard_map/all_to_all | solution.py:474
  101.3 1.1 copy-done.1
  102.5 1.0 copy-done.3
  103.5 6.9 %spread.1 = (bf16[64,128,128]{2,1,0:T(8,128)(2,1)S(1)}, bf16[64,128,128]{2,1,0:T(8,128)(2,1)}) custom-call(s32[4]{0:T(128)S(1)} %pad_add_fusion.at_ref, s32[2,1024]{1,0:T(2,128)S(1)} %get-tuple-element.33.picks_ref, bf16[64,48,128]{2,1,0:T(8,128)(2,1)S(1)} %copy-done.1, bf16[64,48,128]{2,1,0:T(8,128)(2,1)} %collective-permute-done.5.refs_1_, ...), custom_call_target="tpu_custom_call" | custom-call | tf_op jit(solution)/shard_map/spread/pallas_call | solution.py:465
  110.4 1.4 copy-done.4
  111.8 0.5 collective-permute-start.20
  112.3 18.5 %all-to-all-done.1.received_ref = bf16[64,128,128]{2,1,0:T(8,128)(2,1)S(1)} async-done(((bf16[64,128,128]{2,1,0:T(8,128)(2,1)}), bf16[64,128,128]{2,1,0:T(8,128)(2,1)S(1)}, u32[]{:S(2)}, u32[]{:S(2)}) %all-to-all-start.1) | async-done | bytes 2097184 | tf_op jit(solution)/shard_map/all_to_all | solution.py:474
  130.8 1.7 level1.1
  132.5 0.6 copy-done.11
  133.1 1.1 broadcast_select_fusion.1
  134.2 4.6 %all-to-all-start.2 = ((bf16[32,128,128]{2,1,0:T(8,128)(2,1)}), bf16[32,128,128]{2,1,0:T(8,128)(2,1)S(1)}, u32[]{:S(2)}, u32[]{:S(2)}) async-start(bf16[32,128,128]{2,1,0:T(8,128)(2,1)} %broadcast_select_fusion.1), calls=%async_computation.2 | async-start | bytes 2097152 | tf_op jit(solution)/shard_map/all_to_all | solution.py:474
  139.0 1.6 copy-done.5
  140.5 7.3 %leaf.3.right_ref = f32[32,128,128]{2,1,0:T(8,128)} custom-call(s32[560]{0:T(1024)S(1)} %copy-done.9, s32[4]{0:T(128)S(1)} %pad_add_fusion.at_ref, bf16[64,128,128]{2,1,0:T(8,128)(2,1)S(1)} %copy-done.5, bf16[64,128,128]{2,1,0:T(8,128)(2,1)} %collective-permute-done.20.other_ref, bf16[560,128,128]{2,1,0:T(8,128)(2,1)} %panels_hbm.7, f32[32,128,128]{2,1,0:T(8,128)} %bitcast.27), custom_call_target="tpu_custom_call" | custom-call | tf_op jit(solution)/shard_map/leaf/pallas_call | solution.py:378
  147.8 5.9 %leaf.4.right_ref = f32[32,128,128]{2,1,0:T(8,128)} custom-call(s32[560]{0:T(1024)S(1)} %copy-done.9, bf16[64,128,128]{2,1,0:T(8,128)(2,1)S(1)} %all-to-all-done.1.received_ref, bf16[560,128,128]{2,1,0:T(8,128)(2,1)} %panels_hbm.7, f32[32,128,128]{2,1,0:T(8,128)} %leaf.3.right_ref), custom_call_target="tpu_custom_call" | custom-call | tf_op jit(solution)/shard_map/leaf/pallas_call | solution.py:378
  153.8 1.2 all-to-all-done.2.received_ref
  154.9 1.8 level2.1
  156.7 0.9 broadcast_select_fusion.2
  157.6 4.7 %all-to-all-start.3 = ((bf16[16,128,128]{2,1,0:T(8,128)(2,1)}), bf16[16,128,128]{2,1,0:T(8,128)(2,1)S(1)}, u32[]{:S(2)}, u32[]{:S(2)}) async-start(bf16[16,128,128]{2,1,0:T(8,128)(2,1)} %broadcast_select_fusion.2), calls=%async_computation.3 | async-start | bytes 1048576 | tf_op jit(solution)/shard_map/all_to_all | solution.py:474
  162.3 5.9 %leaf.5.right_hbm = f32[32,128,128]{2,1,0:T(8,128)} custom-call(s32[560]{0:T(1024)S(1)} %copy-done.10, bf16[32,128,128]{2,1,0:T(8,128)(2,1)S(1)} %all-to-all-done.2.received_ref, bf16[560,128,128]{2,1,0:T(8,128)(2,1)} %panels_hbm.7, f32[32,128,128]{2,1,0:T(8,128)} %leaf.4.right_ref), custom_call_target="tpu_custom_call" | custom-call | tf_op jit(solution)/shard_map/leaf/pallas_call | solution.py:378
  168.3 0.8 pad_maximum_fusion.3
  169.1 3.2 %all-to-all-done.3.received_ref = bf16[16,128,128]{2,1,0:T(8,128)(2,1)S(1)} async-done(((bf16[16,128,128]{2,1,0:T(8,128)(2,1)}), bf16[16,128,128]{2,1,0:T(8,128)(2,1)S(1)}, u32[]{:S(2)}, u32[]{:S(2)}) %all-to-all-start.3) | async-done | bytes 524320 | tf_op jit(solution)/shard_map/all_to_all | solution.py:474
  172.3 5.3 %last.1 = f32[32,128,128]{2,1,0:T(8,128)} custom-call(s32[560]{0:T(1024)} %from_hbm.7, bf16[16,128,128]{2,1,0:T(8,128)(2,1)S(1)} %all-to-all-done.3.received_ref, bf16[560,128,128]{2,1,0:T(8,128)(2,1)} %panels_hbm.7, f32[32,128,128]{2,1,0:T(8,128)} %leaf.5.right_hbm, f32[40,128,128]{2,1,0:T(8,128)} %diag_hbm.9), custom_call_target="tpu_custom_call" | custom-call | tf_op jit(solution)/shard_map/last/pallas_call | solution.py:534
  (70 shorter events, 0.9 us)
Async XLA Ops:
  0.6 1.0 copy-start.6
  1.7 0.7 copy-start.14
  2.4 0.7 copy-start.15
  5.7 28.4 %all-to-all-start = ((bf16[128,8,384]{2,1,0:T(8,128)(2,1)}), bf16[128,8,384]{2,1,0:T(8,128)(2,1)S(1)}, u32[]{:S(2)}, u32[]{:S(2)}) async-start(bf16[128,8,384]{2,1,0:T(8,128)(2,1)} %pack.1), calls=%async_computation | async-start | bytes 1572864 | tf_op jit(solution)/shard_map/all_to_all | solution.py:408
  17.9 27.5 %copy-start.17 = (s32[24]{0:T(128)}, s32[24]{0:T(128)S(1)}, u32[]{:S(2)}) copy-start(s32[24]{0:T(128)S(1)} %slice.42.from_ref) | copy-start | bytes 292
  35.6 3.9 %collective-permute-start.13 = (bf16[2,32,128]{2,1,0:T(8,128)(2,1)S(1)}, bf16[2,32,128]{2,1,0:T(8,128)(2,1)S(1)}, u32[]{:S(2)}, u32[]{:S(2)}) collective-permute-start(bf16[2,32,128]{2,1,0:T(8,128)(2,1)S(1)} %slice.45), channel_id=1, source_target_pairs={{0,32},{1,33},{2,34},{3,35},{4,100},{5,101},{6,102},{7,103},{8,40}... | collective-permute-start | bytes 49160 | tf_op jit(solution)/shard_map/ppermute | solution.py:156
  36.5 1.4 collective-permute-start.12
  36.6 3.9 %collective-permute-start.6 = (bf16[2,48,128]{2,1,0:T(8,128)(2,1)S(1)}, bf16[2,48,128]{2,1,0:T(8,128)(2,1)S(1)}, u32[]{:S(2)}, u32[]{:S(2)}) collective-permute-start(bf16[2,48,128]{2,1,0:T(8,128)(2,1)S(1)} %get-tuple-element.66), channel_id=1, source_target_pairs={{0,8},{1,9},{2,10},{3,11},{4,28},{5,29},{6,30},{7,31},{8,0},{9,1},... | collective-permute-start | bytes 73736 | tf_op jit(solution)/shard_map/ppermute | solution.py:156
  36.8 3.9 %collective-permute-start = (bf16[2,48,128]{2,1,0:T(8,128)(2,1)S(1)}, bf16[2,48,128]{2,1,0:T(8,128)(2,1)S(1)}, u32[]{:S(2)}, u32[]{:S(2)}) collective-permute-start(bf16[2,48,128]{2,1,0:T(8,128)(2,1)S(1)} %get-tuple-element.67), channel_id=1, source_target_pairs={{0,1},{1,0},{2,3},{3,2},{4,7},{5,6},{6,5},{7,4},{8,9},{9,8},{10,11... | collective-permute-start | bytes 73736 | tf_op jit(solution)/shard_map/ppermute | solution.py:156
  37.9 25.5 %copy-start.19 = (s32[24]{0:T(128)}, s32[24]{0:T(128)S(1)}, u32[]{:S(2)}) copy-start(s32[24]{0:T(128)S(1)} %collective-permute-done.12.from_ref) | copy-start | bytes 292
  39.5 10.8 %collective-permute-start.14 = (bf16[4,32,128]{2,1,0:T(8,128)(2,1)S(1)}, bf16[4,32,128]{2,1,0:T(8,128)(2,1)S(1)}, u32[]{:S(2)}, u32[]{:S(2)}) collective-permute-start(bf16[4,32,128]{2,1,0:T(8,128)(2,1)S(1)} %pad_maximum_fusion.15), channel_id=1, source_target_pairs={{0,96},{1,97},{2,98},{3,99},{4,36},{5,37},{6,38},{7,39},{8,104},{9... | collective-permute-start | bytes 98312 | tf_op jit(solution)/shard_map/ppermute | solution.py:156
  40.5 2.9 %collective-permute-start.7 = (bf16[4,48,128]{2,1,0:T(8,128)(2,1)S(1)}, bf16[4,48,128]{2,1,0:T(8,128)(2,1)S(1)}, u32[]{:S(2)}, u32[]{:S(2)}) collective-permute-start(bf16[4,48,128]{2,1,0:T(8,128)(2,1)S(1)} %pad_maximum_fusion.14), channel_id=1, source_target_pairs={{0,24},{1,25},{2,26},{3,27},{4,12},{5,13},{6,14},{7,15},{8,16},{9,... | collective-permute-start | bytes 147464 | tf_op jit(solution)/shard_map/ppermute | solution.py:156
  40.7 4.7 %collective-permute-start.1 = (bf16[4,48,128]{2,1,0:T(8,128)(2,1)S(1)}, bf16[4,48,128]{2,1,0:T(8,128)(2,1)S(1)}, u32[]{:S(2)}, u32[]{:S(2)}) collective-permute-start(bf16[4,48,128]{2,1,0:T(8,128)(2,1)S(1)} %pad_maximum_fusion.13), channel_id=1, source_target_pairs={{0,3},{1,2},{2,1},{3,0},{4,5},{5,4},{6,7},{7,6},{8,11},{9,10},{10,... | collective-permute-start | bytes 147464 | tf_op jit(solution)/shard_map/ppermute | solution.py:156
  43.5 4.8 %collective-permute-start.8 = (bf16[8,48,128]{2,1,0:T(8,128)(2,1)S(1)}, bf16[8,48,128]{2,1,0:T(8,128)(2,1)S(1)}, u32[]{:S(2)}, u32[]{:S(2)}) collective-permute-start(bf16[8,48,128]{2,1,0:T(8,128)(2,1)S(1)} %pad_maximum_fusion.11), channel_id=1, source_target_pairs={{0,32},{1,33},{2,34},{3,35},{4,100},{5,101},{6,102},{7,103},{8,40}... | collective-permute-start | bytes 294920 | tf_op jit(solution)/shard_map/ppermute | solution.py:156
  45.4 4.8 %collective-permute-start.2 = (bf16[8,48,128]{2,1,0:T(8,128)(2,1)S(1)}, bf16[8,48,128]{2,1,0:T(8,128)(2,1)S(1)}, u32[]{:S(2)}, u32[]{:S(2)}) collective-permute-start(bf16[8,48,128]{2,1,0:T(8,128)(2,1)S(1)} %pad_maximum_fusion.10), channel_id=1, source_target_pairs={{0,8},{1,9},{2,10},{3,11},{4,28},{5,29},{6,30},{7,31},{8,0},{9,1},... | collective-permute-start | bytes 294920 | tf_op jit(solution)/shard_map/ppermute | solution.py:156
  48.2 4.6 %collective-permute-start.9 = (bf16[16,48,128]{2,1,0:T(8,128)(2,1)S(1)}, bf16[16,48,128]{2,1,0:T(8,128)(2,1)S(1)}, u32[]{:S(2)}, u32[]{:S(2)}) collective-permute-start(bf16[16,48,128]{2,1,0:T(8,128)(2,1)S(1)} %pad_maximum_fusion.8), channel_id=1, source_target_pairs={{0,96},{1,97},{2,98},{3,99},{4,36},{5,37},{6,38},{7,39},{8,104},{9... | collective-permute-start | bytes 589832 | tf_op jit(solution)/shard_map/ppermute | solution.py:156
  50.2 4.6 %collective-permute-start.3 = (bf16[16,48,128]{2,1,0:T(8,128)(2,1)S(1)}, bf16[16,48,128]{2,1,0:T(8,128)(2,1)S(1)}, u32[]{:S(2)}, u32[]{:S(2)}) collective-permute-start(bf16[16,48,128]{2,1,0:T(8,128)(2,1)S(1)} %pad_maximum_fusion.7), channel_id=1, source_target_pairs={{0,24},{1,25},{2,26},{3,27},{4,12},{5,13},{6,14},{7,15},{8,16},{9,... | collective-permute-start | bytes 589832 | tf_op jit(solution)/shard_map/ppermute | solution.py:156
  50.3 5.6 %collective-permute-start.15 = (bf16[8,32,128]{2,1,0:T(8,128)(2,1)S(1)}, bf16[8,32,128]{2,1,0:T(8,128)(2,1)S(1)}, u32[]{:S(2)}, u32[]{:S(2)}) collective-permute-start(bf16[8,32,128]{2,1,0:T(8,128)(2,1)S(1)} %pad_maximum_fusion.12), channel_id=1, source_target_pairs={{0,1},{1,0},{2,3},{3,2},{4,7},{5,6},{6,5},{7,4},{8,9},{9,8},{10,11... | collective-permute-start | bytes 196616 | tf_op jit(solution)/shard_map/ppermute | solution.py:156
  52.9 10.5 %collective-permute-start.10 = (bf16[32,48,128]{2,1,0:T(8,128)(2,1)S(1)}, bf16[32,48,128]{2,1,0:T(8,128)(2,1)S(1)}, u32[]{:S(2)}, u32[]{:S(2)}) collective-permute-start(bf16[32,48,128]{2,1,0:T(8,128)(2,1)S(1)} %pad_maximum_fusion.5), channel_id=1, source_target_pairs={{0,1},{1,0},{2,3},{3,2},{4,7},{5,6},{6,5},{7,4},{8,9},{9,8},{10,11... | collective-permute-start | bytes 1179656 | tf_op jit(solution)/shard_map/ppermute | solution.py:156
  54.8 8.7 %collective-permute-start.4 = (bf16[32,48,128]{2,1,0:T(8,128)(2,1)S(1)}, bf16[32,48,128]{2,1,0:T(8,128)(2,1)S(1)}, u32[]{:S(2)}, u32[]{:S(2)}) collective-permute-start(bf16[32,48,128]{2,1,0:T(8,128)(2,1)S(1)} %pad_maximum_fusion.4), channel_id=1, source_target_pairs={{0,32},{1,33},{2,34},{3,35},{4,100},{5,101},{6,102},{7,103},{8,40}... | collective-permute-start | bytes 1179656 | tf_op jit(solution)/shard_map/ppermute | solution.py:156
  56.0 3.9 %collective-permute-start.16 = (bf16[16,32,128]{2,1,0:T(8,128)(2,1)S(1)}, bf16[16,32,128]{2,1,0:T(8,128)(2,1)S(1)}, u32[]{:S(2)}, u32[]{:S(2)}) collective-permute-start(bf16[16,32,128]{2,1,0:T(8,128)(2,1)S(1)} %pad_maximum_fusion.9), channel_id=1, source_target_pairs={{0,3},{1,2},{2,1},{3,0},{4,5},{5,4},{6,7},{7,6},{8,11},{9,10},{10,... | collective-permute-start | bytes 393224 | tf_op jit(solution)/shard_map/ppermute | solution.py:156
  59.9 7.2 %collective-permute-start.17 = (bf16[32,32,128]{2,1,0:T(8,128)(2,1)S(1)}, bf16[32,32,128]{2,1,0:T(8,128)(2,1)S(1)}, u32[]{:S(2)}, u32[]{:S(2)}) collective-permute-start(bf16[32,32,128]{2,1,0:T(8,128)(2,1)S(1)} %pad_maximum_fusion.6), channel_id=1, source_target_pairs={{0,8},{1,9},{2,10},{3,11},{4,28},{5,29},{6,30},{7,31},{8,0},{9,1},... | collective-permute-start | bytes 786440 | tf_op jit(solution)/shard_map/ppermute | solution.py:156
  63.5 14.9 %collective-permute-start.11 = (bf16[64,48,128]{2,1,0:T(8,128)(2,1)S(1)}, bf16[64,48,128]{2,1,0:T(8,128)(2,1)}, u32[]{:S(2)}, u32[]{:S(2)}) collective-permute-start(bf16[64,48,128]{2,1,0:T(8,128)(2,1)S(1)} %pad_maximum_fusion.1.refs_2_), channel_id=1, source_target_pairs={{0,3},{1,2},{2,1},{3,0},{4,5},{5,4},{6,7},{7,6},{8,11},{9,10},{10,... | collective-permute-start | bytes 2359304 | tf_op jit(solution)/shard_map/ppermute | solution.py:156
  63.6 25.8 %copy-start = (bf16[64,48,128]{2,1,0:T(8,128)(2,1)}, bf16[64,48,128]{2,1,0:T(8,128)(2,1)S(1)}, u32[]{:S(2)}) copy-start(bf16[64,48,128]{2,1,0:T(8,128)(2,1)S(1)} %pad_maximum_fusion.refs_0_) | copy-start | bytes 2359300
  63.7 14.8 %collective-permute-start.5 = (bf16[64,48,128]{2,1,0:T(8,128)(2,1)S(1)}, bf16[64,48,128]{2,1,0:T(8,128)(2,1)}, u32[]{:S(2)}, u32[]{:S(2)}) collective-permute-start(bf16[64,48,128]{2,1,0:T(8,128)(2,1)S(1)} %pad_maximum_fusion.refs_0_), channel_id=1, source_target_pairs={{0,96},{1,97},{2,98},{3,99},{4,36},{5,37},{6,38},{7,39},{8,104},{9... | collective-permute-start | bytes 2359304 | tf_op jit(solution)/shard_map/ppermute | solution.py:156
  67.2 11.2 %collective-permute-start.18 = (bf16[64,32,128]{2,1,0:T(8,128)(2,1)S(1)}, bf16[64,32,128]{2,1,0:T(8,128)(2,1)S(1)}, u32[]{:S(2)}, u32[]{:S(2)}) collective-permute-start(bf16[64,32,128]{2,1,0:T(8,128)(2,1)S(1)} %pad_maximum_fusion.2.refs_4_), channel_id=1, source_target_pairs={{0,24},{1,25},{2,26},{3,27},{4,12},{5,13},{6,14},{7,15},{8,16},{9,... | collective-permute-start | bytes 1572872 | tf_op jit(solution)/shard_map/ppermute | solution.py:156
  68.1 0.7 copy-start.7
  78.4 11.1 %copy-start.2 = (bf16[64,32,128]{2,1,0:T(8,128)(2,1)}, bf16[64,32,128]{2,1,0:T(8,128)(2,1)S(1)}, u32[]{:S(2)}) copy-start(bf16[64,32,128]{2,1,0:T(8,128)(2,1)S(1)} %collective-permute-done.18.refs_5_) | copy-start | bytes 1572868
  78.4 0.6 copy-start.20
  79.1 10.4 %copy-start.16 = (s32[1,240]{1,0:T(1,128)S(1)}, s32[1,240]{1,0:T(1,128)}, u32[]{:S(2)}) copy-start(s32[1,240]{1,0:T(1,128)} %send_ref.1) | copy-start | bytes 2884
  79.1 10.4 %copy-start.18 = (s32[24]{0:T(128)S(1)}, s32[24]{0:T(128)}, u32[]{:S(2)}) copy-start(s32[24]{0:T(128)} %copy-done.17) | copy-start | bytes 292
  81.3 10.4 %collective-permute-start.19 = (bf16[24,128,128]{2,1,0:T(8,128)(2,1)S(1)}, bf16[24,128,128]{2,1,0:T(8,128)(2,1)S(1)}, u32[]{:S(2)}, u32[]{:S(2)}) collective-permute-start(bf16[24,128,128]{2,1,0:T(8,128)(2,1)S(1)} %near1.1), channel_id=1, source_target_pairs={{0,4},{1,5},{2,6},{3,7},{4,0},{5,1},{6,2},{7,3},{8,12},{9,13},{10,... | collective-permute-start | bytes 2359304 | tf_op jit(solution)/shard_map/ppermute | solution.py:171
  94.2 1.6 copy-start.8
  94.2 1.6 copy-start.12
  95.8 35.0 %all-to-all-start.1 = ((bf16[64,128,128]{2,1,0:T(8,128)(2,1)}), bf16[64,128,128]{2,1,0:T(8,128)(2,1)S(1)}, u32[]{:S(2)}, u32[]{:S(2)}) async-start(bf16[64,128,128]{2,1,0:T(8,128)(2,1)} %broadcast_select_fusion), calls=%async_computation.1 | async-start | bytes 4194304 | tf_op jit(solution)/shard_map/all_to_all | solution.py:474
  101.3 1.1 copy-start.1
  102.5 1.0 copy-start.3
  110.4 1.4 copy-start.4
  111.8 27.2 %collective-permute-start.20 = (bf16[64,128,128]{2,1,0:T(8,128)(2,1)}, bf16[64,128,128]{2,1,0:T(8,128)(2,1)}, u32[]{:S(2)}, u32[]{:S(2)}) collective-permute-start(bf16[64,128,128]{2,1,0:T(8,128)(2,1)} %get-tuple-element.53), channel_id=1, source_target_pairs={{0,4},{1,5},{2,6},{3,7},{4,0},{5,1},{6,2},{7,3},{8,12},{9,13},{10,... | collective-permute-start | bytes 6291464 | tf_op jit(solution)/shard_map/ppermute | solution.py:171
  132.4 0.7 copy-start.11
  133.1 5.8 %copy-start.9 = (s32[560]{0:T(1024)S(1)}, s32[560]{0:T(1024)}, u32[]{:S(2)}) copy-start(s32[560]{0:T(1024)} %from_hbm.7) | copy-start | bytes 6724
  134.2 20.7 %all-to-all-start.2 = ((bf16[32,128,128]{2,1,0:T(8,128)(2,1)}), bf16[32,128,128]{2,1,0:T(8,128)(2,1)S(1)}, u32[]{:S(2)}, u32[]{:S(2)}) async-start(bf16[32,128,128]{2,1,0:T(8,128)(2,1)} %broadcast_select_fusion.1), calls=%async_computation.2 | async-start | bytes 2097152 | tf_op jit(solution)/shard_map/all_to_all | solution.py:474
  139.0 1.6 copy-start.5
  154.9 7.4 %copy-start.10 = (s32[560]{0:T(1024)S(1)}, s32[560]{0:T(1024)}, u32[]{:S(2)}) copy-start(s32[560]{0:T(1024)} %from_hbm.7) | copy-start | bytes 6724
  157.6 14.7 %all-to-all-start.3 = ((bf16[16,128,128]{2,1,0:T(8,128)(2,1)}), bf16[16,128,128]{2,1,0:T(8,128)(2,1)S(1)}, u32[]{:S(2)}, u32[]{:S(2)}) async-start(bf16[16,128,128]{2,1,0:T(8,128)(2,1)} %broadcast_select_fusion.2), calls=%async_computation.3 | async-start | bytes 1048576 | tf_op jit(solution)/shard_map/all_to_all | solution.py:474
  162.3 5.9 %copy-start.13 = (f32[2,128,128]{2,1,0:T(8,128)S(1)}, f32[2,128,128]{2,1,0:T(8,128)}, u32[]{:S(2)}) copy-start(f32[2,128,128]{2,1,0:T(8,128)} %copy-done.12) | copy-start | bytes 393220

commit v7 on v6

--- a/solution.py
+++ b/solution.py
@@ -42,9 +42,18 @@
     return lax.dot_general(a, b, (((1,), (1,)), ((), ())), preferred_element_type=jnp.float32)
 
 
-def pack_kernel(target_ref, send_ref, noise_ref, out_ref):
+def pack_kernel(
+    target_hbm, send_hbm, noise_hbm, out_ref, target_ref, send_ref, noise_ref, arrived
+):
     rows = noise_ref.shape[0]
     owners, per_owner, width = out_ref.shape
+    *lists, noise = start(
+        (target_hbm, target_ref, arrived.at[0]),
+        (send_hbm, send_ref, arrived.at[1]),
+        (noise_hbm, noise_ref, arrived.at[2]),
+    )
+    for copy in lists:
+        copy.wait()
     target = target_ref[...]
     owner = target // rows
     slot = target % rows
@@ -56,6 +65,7 @@
     rank = jnp.sum(jnp.where(mine, earlier, 0.0), axis=0, keepdims=True)
     position = owner * per_owner + rank.astype(jnp.int32)
     select = hot(position == lax.broadcasted_iota(jnp.int32, (rows, rows), 0))
+    noise.wait()
     both = jnp.concatenate(halves(noise_ref[...]), axis=1)
     out = jnp.dot(select, both, preferred_element_type=jnp.float32)
     level_rows = TS * BS
@@ -400,11 +410,17 @@
     outgoing = pl.pallas_call(
         pack_kernel,
         out_shape=b16(owners, per_owner, 2 * rhs + BS),
-        in_specs=[whole()] * 3,
+        in_specs=[in_hbm()] * 3,
         out_specs=whole(),
+        scratch_shapes=[
+            pltpu.VMEM((1, rows), jnp.int32),
+            pltpu.VMEM(send_lists.shape, jnp.int32),
+            pltpu.VMEM((rows, rhs), jnp.float32),
+            pltpu.SemaphoreType.DMA((3,)),
+        ],
         compiler_params=VMEM,
         name="pack",
-    )(elimination_row.reshape(1, rows), send_lists, noise_parts)
+    )(*map(streamed, (elimination_row.reshape(1, rows), send_lists, noise_parts)))
     arrived = lax.all_to_all(outgoing, AXES, 0, 0, tiled=True)
     send_row = send_lists[0]
     stream = streamed(panels)
@@ -434,7 +450,7 @@
     leaf = lax.axis_index("leaf")
     at = jnp.stack([lax.axis_index("panel"), leaf // (2 * SIDE), leaf // 2 % SIDE, leaf % 2])
     near = KP * TS * (LEVELS - 1)
-    mine = panel_from[:near]
+    mine = panel_from
     gathered, theirs = gather_core(sent, mine)
     near_tiles = [
         pl.pallas_call(

time: 179 us -> 177 us (0.989)
  blocking collectives: 0 us -> 28.3 us
  waiting for transfers between devices: 66.9 us -> 50.6 us
  starting transfers between devices: 47.9 us -> 36.4 us
  local copies, waits for them, and re-layouts: 10.3 us -> 7.25 us
    all_to_all x0 -> x1, blocking collectives: none -> 28.3 us  [per_device(): arrived = lax.all_to_all(outgoing, AXES, 0, 0, tiled=True)]
    all_to_all x1 -> x0, waiting for transfers between devices: 16.3 us -> none  [per_device(): arrived = lax.all_to_all(outgoing, AXES, 0, 0, tiled=True)]
    all_to_all x1 -> x0, starting transfers between devices: 11.5 us -> none  [per_device(): arrived = lax.all_to_all(outgoing, AXES, 0, 0, tiled=True)]
    unnamed x42 -> x36, local copies, waits for them, and re-layouts: 9.58 us -> 7.22 us
  transfers between devices with their start and end apart: 25 -> 24, of which waited for: 15 -> 14; matrix products, arithmetic and copies ran while one was open for 2% -> 1% of each run, Pallas kernels for 17% -> 17%
where the time goes in v7:
time: 177 us; the launch traced here: 176 us
  waiting for transfers between devices  50.6 us (29%)
  Pallas kernels  47 us (27%)
  starting transfers between devices  36.4 us (21%)
  blocking collectives  28.3 us (16%)
  local copies, waits for them, and re-layouts  7.25 us (4%)
  other arithmetic  4.98 us (3%)
    all_to_all x1, blocking collectives, per_device(): arrived = lax.all_to_all(outgoing, AXES, 0, 0, tiled=True)  28.3 us
    ppermute x18, waiting for transfers between devices, gather_core(): lax.ppermute(part, AXES, step_pairs(order[step // 2], step % 2))  27.7 us
    all_to_all x3, waiting for transfers between devices, per_device(): lax.all_to_all(buffer, AXES, 0, 0, axis_index_groups=groups, tiled=True)  22.8 us
    pallas_call x3, Pallas kernels, leaf_pass(): pl.pallas_call(kernel, grid_spec=pltpu.PrefetchScalarGridSpec(num_scalar_...  19.1 us
    all_to_all x3, starting transfers between devices, per_device(): lax.all_to_all(buffer, AXES, 0, 0, axis_index_groups=groups, tiled=True)  14.9 us
    ppermute x18, starting transfers between devices, gather_core(): lax.ppermute(part, AXES, step_pairs(order[step // 2], step % 2))  12.9 us
    ppermute x3, starting transfers between devices, swap_core(): return lax.ppermute(x, AXES, [(i, i ^ SIDE) for i in range(2 * SIDE ** 3)])  8.65 us
    unnamed x36, local copies, waits for them, and re-layouts  7.22 us
  transfers between devices with their start and end apart: 24, of which 14 were waited for; matrix products, arithmetic and copies ran while one was open for 1% of the time, Pallas kernels for 17%

profile of v7, /device:TPU:1, one launch (start us, length us, event | category | flops | bytes accessed | tf_op | source)
XLA Modules:
  0.0 175.7 jit_solution(16996379600641368096)
XLA Ops:
  0.6 3.1 %pack.1 = bf16[128,8,384]{2,1,0:T(8,128)(2,1)S(1)} custom-call(s32[1,1024]{1,0:T(1,128)} %bitcast.29, s32[1,240]{1,0:T(1,128)} %send_hbm.1, f32[1024,128]{1,0:T(8,128)} %noise_hbm.1), custom_call_target="tpu_custom_call" | custom-call | tf_op jit(solution)/shard_map/pack/pallas_call | solution.py:410
  3.8 28.3 %all_to_all.20.arrived_ref = bf16[128,8,384]{2,1,0:T(8,128)(2,1)S(1)} all-to-all(bf16[128,8,384]{2,1,0:T(8,128)(2,1)S(1)} %pack.1), channel_id=1, replica_groups=mesh['leaf'=32,'panel'=4] {'leaf','panel'}, dimensions={0} | all-to-all | bytes 1572864 | tf_op jit(solution)/shard_map/all_to_all | solution.py:424
  32.0 1.4 first.1
  33.5 0.9 collective-permute-start.13
  34.4 0.3 collective-permute-start.6
  34.7 1.1 collective-permute-start
  35.8 1.5 collective-permute-done.13
  37.4 1.0 collective-permute-done.6
  38.4 0.2 collective-permute-done
  38.6 0.2 collective-permute-start.1
  38.8 2.5 %collective-permute-done.7 = bf16[4,48,128]{2,1,0:T(8,128)(2,1)S(1)} collective-permute-done((bf16[4,48,128]{2,1,0:T(8,128)(2,1)S(1)}, bf16[4,48,128]{2,1,0:T(8,128)(2,1)S(1)}, u32[]{:S(2)}, u32[]{:S(2)}) %collective-permute-start.7) | collective-permute-done | bytes 49184 | tf_op jit(solution)/shard_map/ppermute | solution.py:166
  41.3 1.9 %collective-permute-start.8 = (bf16[8,48,128]{2,1,0:T(8,128)(2,1)S(1)}, bf16[8,48,128]{2,1,0:T(8,128)(2,1)S(1)}, u32[]{:S(2)}, u32[]{:S(2)}) collective-permute-start(bf16[8,48,128]{2,1,0:T(8,128)(2,1)S(1)} %pad_maximum_fusion.11), channel_id=1, source_target_pairs={{0,32},{1,33},{2,34},{3,35},{4,100},{5,101},{6,102},{7,103},{8,40}... | collective-permute-start | bytes 294920 | tf_op jit(solution)/shard_map/ppermute | solution.py:166
  43.3 0.8 collective-permute-start.2
  44.1 2.0 %collective-permute-done.8 = bf16[8,48,128]{2,1,0:T(8,128)(2,1)S(1)} collective-permute-done((bf16[8,48,128]{2,1,0:T(8,128)(2,1)S(1)}, bf16[8,48,128]{2,1,0:T(8,128)(2,1)S(1)}, u32[]{:S(2)}, u32[]{:S(2)}) %collective-permute-start.8) | collective-permute-done | bytes 98336 | tf_op jit(solution)/shard_map/ppermute | solution.py:166
  46.1 0.1 collective-permute-start.9
  46.2 1.8 %collective-permute-done.2 = bf16[8,48,128]{2,1,0:T(8,128)(2,1)S(1)} collective-permute-done((bf16[8,48,128]{2,1,0:T(8,128)(2,1)S(1)}, bf16[8,48,128]{2,1,0:T(8,128)(2,1)S(1)}, u32[]{:S(2)}, u32[]{:S(2)}) %collective-permute-start.2) | collective-permute-done | bytes 98336 | tf_op jit(solution)/shard_map/ppermute | solution.py:166
  48.1 0.1 collective-permute-start.3
  48.2 1.1 collective-permute-start.15
  49.3 1.4 collective-permute-done.9
  50.7 1.4 collective-permute-start.10
  52.1 0.5 collective-permute-done.3
  52.7 1.1 collective-permute-start.4
  53.9 0.1 collective-permute-start.16
  54.0 3.8 %collective-permute-done.16 = bf16[16,32,128]{2,1,0:T(8,128)(2,1)S(1)} collective-permute-done((bf16[16,32,128]{2,1,0:T(8,128)(2,1)S(1)}, bf16[16,32,128]{2,1,0:T(8,128)(2,1)S(1)}, u32[]{:S(2)}, u32[]{:S(2)}) %collective-permute-start.16) | collective-permute-done | bytes 131104 | tf_op jit(solution)/shard_map/ppermute | solution.py:166
  57.8 3.4 %collective-permute-start.17 = (bf16[32,32,128]{2,1,0:T(8,128)(2,1)S(1)}, bf16[32,32,128]{2,1,0:T(8,128)(2,1)S(1)}, u32[]{:S(2)}, u32[]{:S(2)}) collective-permute-start(bf16[32,32,128]{2,1,0:T(8,128)(2,1)S(1)} %pad_maximum_fusion.6), channel_id=1, source_target_pairs={{0,8},{1,9},{2,10},{3,11},{4,28},{5,29},{6,30},{7,31},{8,0},{9,1},... | collective-permute-start | bytes 786440 | tf_op jit(solution)/shard_map/ppermute | solution.py:166
  61.3 0.1 collective-permute-start.11
  61.4 0.1 pad_maximum_fusion.refs_0_
  61.5 0.1 collective-permute-start.5
  61.6 3.4 %collective-permute-done.17 = bf16[32,32,128]{2,1,0:T(8,128)(2,1)S(1)} collective-permute-done((bf16[32,32,128]{2,1,0:T(8,128)(2,1)S(1)}, bf16[32,32,128]{2,1,0:T(8,128)(2,1)S(1)}, u32[]{:S(2)}, u32[]{:S(2)}) %collective-permute-start.17) | collective-permute-done | bytes 262176 | tf_op jit(solution)/shard_map/ppermute | solution.py:166
  65.0 0.1 collective-permute-start.18
  65.2 0.1 pad_add_fusion.at_ref
  65.3 0.7 order.1
  66.0 0.7 copy-done.6
  66.7 9.5 %collective-permute-done.18.refs_5_ = bf16[64,32,128]{2,1,0:T(8,128)(2,1)S(1)} collective-permute-done((bf16[64,32,128]{2,1,0:T(8,128)(2,1)S(1)}, bf16[64,32,128]{2,1,0:T(8,128)(2,1)S(1)}, u32[]{:S(2)}, u32[]{:S(2)}) %collective-permute-start.18) | collective-permute-done | bytes 524320 | tf_op jit(solution)/shard_map/ppermute | solution.py:166
  76.3 0.7 copy-done.15
  76.9 2.3 %near1.1 = bf16[24,128,128]{2,1,0:T(8,128)(2,1)S(1)} custom-call(s32[4]{0:T(128)S(1)} %pad_add_fusion.at_ref, s32[2,1024]{1,0:T(2,128)S(1)} %get-tuple-element.33.picks_ref, s32[560]{0:T(1024)S(1)} %copy-done.15, bf16[64,48,128]{2,1,0:T(8,128)(2,1)S(1)} %pad_maximum_fusion.refs_0_, bf16[64,48,128]{2,1,0:T(8,128)(2,1)} %collective-permute-done.5.refs_1_, ...), custom_call_target="tpu_custom_call" | custom-call | tf_op jit(solution)/shard_map/near1/pallas_call | solution.py:456
  79.2 8.2 %collective-permute-start.19 = (bf16[24,128,128]{2,1,0:T(8,128)(2,1)S(1)}, bf16[24,128,128]{2,1,0:T(8,128)(2,1)S(1)}, u32[]{:S(2)}, u32[]{:S(2)}) collective-permute-start(bf16[24,128,128]{2,1,0:T(8,128)(2,1)S(1)} %near1.1), channel_id=1, source_target_pairs={{0,4},{1,5},{2,6},{3,7},{4,0},{5,1},{6,2},{7,3},{8,12},{9,13},{10,... | collective-permute-start | bytes 2359304 | tf_op jit(solution)/shard_map/ppermute | solution.py:181
  87.4 2.2 %near0.1.own_ref = bf16[24,128,128]{2,1,0:T(8,128)(2,1)S(1)} custom-call(s32[4]{0:T(128)S(1)} %pad_add_fusion.at_ref, s32[2,1024]{1,0:T(2,128)S(1)} %get-tuple-element.33.picks_ref, s32[560]{0:T(1024)S(1)} %copy-done.8, bf16[64,48,128]{2,1,0:T(8,128)(2,1)S(1)} %pad_maximum_fusion.refs_0_, bf16[64,48,128]{2,1,0:T(8,128)(2,1)} %collective-permute-done.5.refs_1_, ...), custom_call_target="tpu_custom_call" | custom-call | tf_op jit(solution)/shard_map/near0/pallas_call | solution.py:456
  89.6 2.4 %level0.1 = (f32[4,128,128]{2,1,0:T(8,128)S(1)}, f32[2,128,128]{2,1,0:T(8,128)S(1)}, bf16[2,128,128]{2,1,0:T(8,128)(2,1)S(1)}) custom-call(s32[560]{0:T(1024)} %from_hbm.7, bf16[560,128,128]{2,1,0:T(8,128)(2,1)} %panels_hbm.7, f32[6,128,128]{2,1,0:T(8,128)} %copy-done.6, f32[40,128,128]{2,1,0:T(8,128)} %diag_hbm.9, s32[4]{0:T(128)S(1)} %pad_add_fusion.at_ref, ...), custom_call_target="tpu_custom_call" | custom-call | tf_op jit(solution)/shard_map/level0/pallas_call | solution.py:528
  92.1 1.5 broadcast_select_fusion
  93.6 5.5 %all-to-all-start.1 = ((bf16[64,128,128]{2,1,0:T(8,128)(2,1)}), bf16[64,128,128]{2,1,0:T(8,128)(2,1)S(1)}, u32[]{:S(2)}, u32[]{:S(2)}) async-start(bf16[64,128,128]{2,1,0:T(8,128)(2,1)} %broadcast_select_fusion), calls=%async_computation.1 | async-start | bytes 4194304 | tf_op jit(solution)/shard_map/all_to_all | solution.py:490
  99.2 1.1 copy-done.1
  100.3 1.0 copy-done.3
  101.4 6.9 %spread.1 = (bf16[64,128,128]{2,1,0:T(8,128)(2,1)S(1)}, bf16[64,128,128]{2,1,0:T(8,128)(2,1)}) custom-call(s32[4]{0:T(128)S(1)} %pad_add_fusion.at_ref, s32[2,1024]{1,0:T(2,128)S(1)} %get-tuple-element.33.picks_ref, bf16[64,48,128]{2,1,0:T(8,128)(2,1)S(1)} %copy-done.1, bf16[64,48,128]{2,1,0:T(8,128)(2,1)} %collective-permute-done.5.refs_1_, ...), custom_call_target="tpu_custom_call" | custom-call | tf_op jit(solution)/shard_map/spread/pallas_call | solution.py:481
  108.3 1.4 copy-done.4
  109.7 0.5 collective-permute-start.20
  110.1 0.1 compare_bitcast_fusion.1
  110.2 18.4 %all-to-all-done.1.received_ref = bf16[64,128,128]{2,1,0:T(8,128)(2,1)S(1)} async-done(((bf16[64,128,128]{2,1,0:T(8,128)(2,1)}), bf16[64,128,128]{2,1,0:T(8,128)(2,1)S(1)}, u32[]{:S(2)}, u32[]{:S(2)}) %all-to-all-start.1) | async-done | bytes 2097184 | tf_op jit(solution)/shard_map/all_to_all | solution.py:490
  128.7 1.7 level1.1
  130.3 0.6 copy-done.11
  131.0 1.1 broadcast_select_fusion.1
  132.1 4.6 %all-to-all-start.2 = ((bf16[32,128,128]{2,1,0:T(8,128)(2,1)}), bf16[32,128,128]{2,1,0:T(8,128)(2,1)S(1)}, u32[]{:S(2)}, u32[]{:S(2)}) async-start(bf16[32,128,128]{2,1,0:T(8,128)(2,1)} %broadcast_select_fusion.1), calls=%async_computation.2 | async-start | bytes 2097152 | tf_op jit(solution)/shard_map/all_to_all | solution.py:490
  136.7 0.1 compare_bitcast_fusion
  136.8 1.6 copy-done.5
  138.4 7.3 %leaf.3.right_ref = f32[32,128,128]{2,1,0:T(8,128)} custom-call(s32[560]{0:T(1024)S(1)} %copy-done.9, s32[4]{0:T(128)S(1)} %pad_add_fusion.at_ref, bf16[64,128,128]{2,1,0:T(8,128)(2,1)S(1)} %copy-done.5, bf16[64,128,128]{2,1,0:T(8,128)(2,1)} %collective-permute-done.20.other_ref, bf16[560,128,128]{2,1,0:T(8,128)(2,1)} %panels_hbm.7, f32[32,128,128]{2,1,0:T(8,128)} %bitcast.26), custom_call_target="tpu_custom_call" | custom-call | tf_op jit(solution)/shard_map/leaf/pallas_call | solution.py:388
  145.7 5.9 %leaf.4.right_ref = f32[32,128,128]{2,1,0:T(8,128)} custom-call(s32[560]{0:T(1024)S(1)} %copy-done.9, bf16[64,128,128]{2,1,0:T(8,128)(2,1)S(1)} %all-to-all-done.1.received_ref, bf16[560,128,128]{2,1,0:T(8,128)(2,1)} %panels_hbm.7, f32[32,128,128]{2,1,0:T(8,128)} %leaf.3.right_ref), custom_call_target="tpu_custom_call" | custom-call | tf_op jit(solution)/shard_map/leaf/pallas_call | solution.py:388
  151.6 1.2 all-to-all-done.2.received_ref
  152.8 1.8 %level2.1 = (f32[2,128,128]{2,1,0:T(8,128)}, f32[2,128,128]{2,1,0:T(8,128)S(1)}, bf16[2,128,128]{2,1,0:T(8,128)(2,1)S(1)}) custom-call(s32[560]{0:T(1024)} %from_hbm.7, bf16[560,128,128]{2,1,0:T(8,128)(2,1)} %panels_hbm.7, f32[2,128,128]{2,1,0:T(8,128)} %copy-done.11, f32[40,128,128]{2,1,0:T(8,128)} %diag_hbm.9, ...), custom_call_target="tpu_custom_call" | custom-call | tf_op jit(solution)/shard_map/level2/pallas_call | solution.py:528
  154.6 0.9 broadcast_select_fusion.2
  155.5 4.7 %all-to-all-start.3 = ((bf16[16,128,128]{2,1,0:T(8,128)(2,1)}), bf16[16,128,128]{2,1,0:T(8,128)(2,1)S(1)}, u32[]{:S(2)}, u32[]{:S(2)}) async-start(bf16[16,128,128]{2,1,0:T(8,128)(2,1)} %broadcast_select_fusion.2), calls=%async_computation.3 | async-start | bytes 1048576 | tf_op jit(solution)/shard_map/all_to_all | solution.py:490
  160.2 5.9 %leaf.5.right_hbm = f32[32,128,128]{2,1,0:T(8,128)} custom-call(s32[560]{0:T(1024)S(1)} %copy-done.10, bf16[32,128,128]{2,1,0:T(8,128)(2,1)S(1)} %all-to-all-done.2.received_ref, bf16[560,128,128]{2,1,0:T(8,128)(2,1)} %panels_hbm.7, f32[32,128,128]{2,1,0:T(8,128)} %leaf.4.right_ref), custom_call_target="tpu_custom_call" | custom-call | tf_op jit(solution)/shard_map/leaf/pallas_call | solution.py:388
  166.1 0.8 pad_maximum_fusion.3
  167.0 3.2 %all-to-all-done.3.received_ref = bf16[16,128,128]{2,1,0:T(8,128)(2,1)S(1)} async-done(((bf16[16,128,128]{2,1,0:T(8,128)(2,1)}), bf16[16,128,128]{2,1,0:T(8,128)(2,1)S(1)}, u32[]{:S(2)}, u32[]{:S(2)}) %all-to-all-start.3) | async-done | bytes 524320 | tf_op jit(solution)/shard_map/all_to_all | solution.py:490
  170.2 5.3 %last.1 = f32[32,128,128]{2,1,0:T(8,128)} custom-call(s32[560]{0:T(1024)} %from_hbm.7, bf16[16,128,128]{2,1,0:T(8,128)(2,1)S(1)} %all-to-all-done.3.received_ref, bf16[560,128,128]{2,1,0:T(8,128)(2,1)} %panels_hbm.7, f32[32,128,128]{2,1,0:T(8,128)} %leaf.5.right_hbm, f32[40,128,128]{2,1,0:T(8,128)} %diag_hbm.9), custom_call_target="tpu_custom_call" | custom-call | tf_op jit(solution)/shard_map/last/pallas_call | solution.py:550
  (62 shorter events, 0.5 us)
Async XLA Ops:
  32.0 2.4 %copy-start.8 = (s32[560]{0:T(1024)S(1)}, s32[560]{0:T(1024)}, u32[]{:S(2)}) copy-start(s32[560]{0:T(1024)} %from_hbm.7) | copy-start | bytes 6724
  33.5 3.9 %collective-permute-start.13 = (bf16[2,32,128]{2,1,0:T(8,128)(2,1)S(1)}, bf16[2,32,128]{2,1,0:T(8,128)(2,1)S(1)}, u32[]{:S(2)}, u32[]{:S(2)}) collective-permute-start(bf16[2,32,128]{2,1,0:T(8,128)(2,1)S(1)} %slice.41), channel_id=1, source_target_pairs={{0,32},{1,33},{2,34},{3,35},{4,100},{5,101},{6,102},{7,103},{8,40}... | collective-permute-start | bytes 49160 | tf_op jit(solution)/shard_map/ppermute | solution.py:166
  34.4 1.5 collective-permute-start.12
  34.4 3.9 %collective-permute-start.6 = (bf16[2,48,128]{2,1,0:T(8,128)(2,1)S(1)}, bf16[2,48,128]{2,1,0:T(8,128)(2,1)S(1)}, u32[]{:S(2)}, u32[]{:S(2)}) collective-permute-start(bf16[2,48,128]{2,1,0:T(8,128)(2,1)S(1)} %get-tuple-element.66), channel_id=1, source_target_pairs={{0,8},{1,9},{2,10},{3,11},{4,28},{5,29},{6,30},{7,31},{8,0},{9,1},... | collective-permute-start | bytes 73736 | tf_op jit(solution)/shard_map/ppermute | solution.py:166
  34.7 3.9 %collective-permute-start = (bf16[2,48,128]{2,1,0:T(8,128)(2,1)S(1)}, bf16[2,48,128]{2,1,0:T(8,128)(2,1)S(1)}, u32[]{:S(2)}, u32[]{:S(2)}) collective-permute-start(bf16[2,48,128]{2,1,0:T(8,128)(2,1)S(1)} %get-tuple-element.67), channel_id=1, source_target_pairs={{0,1},{1,0},{2,3},{3,2},{4,7},{5,6},{6,5},{7,4},{8,9},{9,8},{10,11... | collective-permute-start | bytes 73736 | tf_op jit(solution)/shard_map/ppermute | solution.py:166
  35.8 25.5 %copy-start.14 = (s32[560]{0:T(1024)}, s32[560]{0:T(1024)S(1)}, u32[]{:S(2)}) copy-start(s32[560]{0:T(1024)S(1)} %collective-permute-done.12.from_ref) | copy-start | bytes 6724
  37.4 10.8 %collective-permute-start.14 = (bf16[4,32,128]{2,1,0:T(8,128)(2,1)S(1)}, bf16[4,32,128]{2,1,0:T(8,128)(2,1)S(1)}, u32[]{:S(2)}, u32[]{:S(2)}) collective-permute-start(bf16[4,32,128]{2,1,0:T(8,128)(2,1)S(1)} %pad_maximum_fusion.15), channel_id=1, source_target_pairs={{0,96},{1,97},{2,98},{3,99},{4,36},{5,37},{6,38},{7,39},{8,104},{9... | collective-permute-start | bytes 98312 | tf_op jit(solution)/shard_map/ppermute | solution.py:166
  38.4 2.9 %collective-permute-start.7 = (bf16[4,48,128]{2,1,0:T(8,128)(2,1)S(1)}, bf16[4,48,128]{2,1,0:T(8,128)(2,1)S(1)}, u32[]{:S(2)}, u32[]{:S(2)}) collective-permute-start(bf16[4,48,128]{2,1,0:T(8,128)(2,1)S(1)} %pad_maximum_fusion.14), channel_id=1, source_target_pairs={{0,24},{1,25},{2,26},{3,27},{4,12},{5,13},{6,14},{7,15},{8,16},{9,... | collective-permute-start | bytes 147464 | tf_op jit(solution)/shard_map/ppermute | solution.py:166
  38.6 4.7 %collective-permute-start.1 = (bf16[4,48,128]{2,1,0:T(8,128)(2,1)S(1)}, bf16[4,48,128]{2,1,0:T(8,128)(2,1)S(1)}, u32[]{:S(2)}, u32[]{:S(2)}) collective-permute-start(bf16[4,48,128]{2,1,0:T(8,128)(2,1)S(1)} %pad_maximum_fusion.13), channel_id=1, source_target_pairs={{0,3},{1,2},{2,1},{3,0},{4,5},{5,4},{6,7},{7,6},{8,11},{9,10},{10,... | collective-permute-start | bytes 147464 | tf_op jit(solution)/shard_map/ppermute | solution.py:166
  41.3 4.8 %collective-permute-start.8 = (bf16[8,48,128]{2,1,0:T(8,128)(2,1)S(1)}, bf16[8,48,128]{2,1,0:T(8,128)(2,1)S(1)}, u32[]{:S(2)}, u32[]{:S(2)}) collective-permute-start(bf16[8,48,128]{2,1,0:T(8,128)(2,1)S(1)} %pad_maximum_fusion.11), channel_id=1, source_target_pairs={{0,32},{1,33},{2,34},{3,35},{4,100},{5,101},{6,102},{7,103},{8,40}... | collective-permute-start | bytes 294920 | tf_op jit(solution)/shard_map/ppermute | solution.py:166
  43.3 4.8 %collective-permute-start.2 = (bf16[8,48,128]{2,1,0:T(8,128)(2,1)S(1)}, bf16[8,48,128]{2,1,0:T(8,128)(2,1)S(1)}, u32[]{:S(2)}, u32[]{:S(2)}) collective-permute-start(bf16[8,48,128]{2,1,0:T(8,128)(2,1)S(1)} %pad_maximum_fusion.10), channel_id=1, source_target_pairs={{0,8},{1,9},{2,10},{3,11},{4,28},{5,29},{6,30},{7,31},{8,0},{9,1},... | collective-permute-start | bytes 294920 | tf_op jit(solution)/shard_map/ppermute | solution.py:166
  46.1 4.6 %collective-permute-start.9 = (bf16[16,48,128]{2,1,0:T(8,128)(2,1)S(1)}, bf16[16,48,128]{2,1,0:T(8,128)(2,1)S(1)}, u32[]{:S(2)}, u32[]{:S(2)}) collective-permute-start(bf16[16,48,128]{2,1,0:T(8,128)(2,1)S(1)} %pad_maximum_fusion.8), channel_id=1, source_target_pairs={{0,96},{1,97},{2,98},{3,99},{4,36},{5,37},{6,38},{7,39},{8,104},{9... | collective-permute-start | bytes 589832 | tf_op jit(solution)/shard_map/ppermute | solution.py:166
  48.1 4.6 %collective-permute-start.3 = (bf16[16,48,128]{2,1,0:T(8,128)(2,1)S(1)}, bf16[16,48,128]{2,1,0:T(8,128)(2,1)S(1)}, u32[]{:S(2)}, u32[]{:S(2)}) collective-permute-start(bf16[16,48,128]{2,1,0:T(8,128)(2,1)S(1)} %pad_maximum_fusion.7), channel_id=1, source_target_pairs={{0,24},{1,25},{2,26},{3,27},{4,12},{5,13},{6,14},{7,15},{8,16},{9,... | collective-permute-start | bytes 589832 | tf_op jit(solution)/shard_map/ppermute | solution.py:166
  48.2 5.7 %collective-permute-start.15 = (bf16[8,32,128]{2,1,0:T(8,128)(2,1)S(1)}, bf16[8,32,128]{2,1,0:T(8,128)(2,1)S(1)}, u32[]{:S(2)}, u32[]{:S(2)}) collective-permute-start(bf16[8,32,128]{2,1,0:T(8,128)(2,1)S(1)} %pad_maximum_fusion.12), channel_id=1, source_target_pairs={{0,1},{1,0},{2,3},{3,2},{4,7},{5,6},{6,5},{7,4},{8,9},{9,8},{10,11... | collective-permute-start | bytes 196616 | tf_op jit(solution)/shard_map/ppermute | solution.py:166
  50.7 10.5 %collective-permute-start.10 = (bf16[32,48,128]{2,1,0:T(8,128)(2,1)S(1)}, bf16[32,48,128]{2,1,0:T(8,128)(2,1)S(1)}, u32[]{:S(2)}, u32[]{:S(2)}) collective-permute-start(bf16[32,48,128]{2,1,0:T(8,128)(2,1)S(1)} %pad_maximum_fusion.5), channel_id=1, source_target_pairs={{0,1},{1,0},{2,3},{3,2},{4,7},{5,6},{6,5},{7,4},{8,9},{9,8},{10,11... | collective-permute-start | bytes 1179656 | tf_op jit(solution)/shard_map/ppermute | solution.py:166
  52.7 8.7 %collective-permute-start.4 = (bf16[32,48,128]{2,1,0:T(8,128)(2,1)S(1)}, bf16[32,48,128]{2,1,0:T(8,128)(2,1)S(1)}, u32[]{:S(2)}, u32[]{:S(2)}) collective-permute-start(bf16[32,48,128]{2,1,0:T(8,128)(2,1)S(1)} %pad_maximum_fusion.4), channel_id=1, source_target_pairs={{0,32},{1,33},{2,34},{3,35},{4,100},{5,101},{6,102},{7,103},{8,40}... | collective-permute-start | bytes 1179656 | tf_op jit(solution)/shard_map/ppermute | solution.py:166
  53.9 3.9 %collective-permute-start.16 = (bf16[16,32,128]{2,1,0:T(8,128)(2,1)S(1)}, bf16[16,32,128]{2,1,0:T(8,128)(2,1)S(1)}, u32[]{:S(2)}, u32[]{:S(2)}) collective-permute-start(bf16[16,32,128]{2,1,0:T(8,128)(2,1)S(1)} %pad_maximum_fusion.9), channel_id=1, source_target_pairs={{0,3},{1,2},{2,1},{3,0},{4,5},{5,4},{6,7},{7,6},{8,11},{9,10},{10,... | collective-permute-start | bytes 393224 | tf_op jit(solution)/shard_map/ppermute | solution.py:166
  57.8 7.2 %collective-permute-start.17 = (bf16[32,32,128]{2,1,0:T(8,128)(2,1)S(1)}, bf16[32,32,128]{2,1,0:T(8,128)(2,1)S(1)}, u32[]{:S(2)}, u32[]{:S(2)}) collective-permute-start(bf16[32,32,128]{2,1,0:T(8,128)(2,1)S(1)} %pad_maximum_fusion.6), channel_id=1, source_target_pairs={{0,8},{1,9},{2,10},{3,11},{4,28},{5,29},{6,30},{7,31},{8,0},{9,1},... | collective-permute-start | bytes 786440 | tf_op jit(solution)/shard_map/ppermute | solution.py:166
  61.3 14.9 %collective-permute-start.11 = (bf16[64,48,128]{2,1,0:T(8,128)(2,1)S(1)}, bf16[64,48,128]{2,1,0:T(8,128)(2,1)}, u32[]{:S(2)}, u32[]{:S(2)}) collective-permute-start(bf16[64,48,128]{2,1,0:T(8,128)(2,1)S(1)} %pad_maximum_fusion.1.refs_2_), channel_id=1, source_target_pairs={{0,3},{1,2},{2,1},{3,0},{4,5},{5,4},{6,7},{7,6},{8,11},{9,10},{10,... | collective-permute-start | bytes 2359304 | tf_op jit(solution)/shard_map/ppermute | solution.py:166
  61.5 25.9 %copy-start = (bf16[64,48,128]{2,1,0:T(8,128)(2,1)}, bf16[64,48,128]{2,1,0:T(8,128)(2,1)S(1)}, u32[]{:S(2)}) copy-start(bf16[64,48,128]{2,1,0:T(8,128)(2,1)S(1)} %pad_maximum_fusion.refs_0_) | copy-start | bytes 2359300
  61.5 14.8 %collective-permute-start.5 = (bf16[64,48,128]{2,1,0:T(8,128)(2,1)S(1)}, bf16[64,48,128]{2,1,0:T(8,128)(2,1)}, u32[]{:S(2)}, u32[]{:S(2)}) collective-permute-start(bf16[64,48,128]{2,1,0:T(8,128)(2,1)S(1)} %pad_maximum_fusion.refs_0_), channel_id=1, source_target_pairs={{0,96},{1,97},{2,98},{3,99},{4,36},{5,37},{6,38},{7,39},{8,104},{9... | collective-permute-start | bytes 2359304 | tf_op jit(solution)/shard_map/ppermute | solution.py:166
  65.0 11.2 %collective-permute-start.18 = (bf16[64,32,128]{2,1,0:T(8,128)(2,1)S(1)}, bf16[64,32,128]{2,1,0:T(8,128)(2,1)S(1)}, u32[]{:S(2)}, u32[]{:S(2)}) collective-permute-start(bf16[64,32,128]{2,1,0:T(8,128)(2,1)S(1)} %pad_maximum_fusion.2.refs_4_), channel_id=1, source_target_pairs={{0,24},{1,25},{2,26},{3,27},{4,12},{5,13},{6,14},{7,15},{8,16},{9,... | collective-permute-start | bytes 1572872 | tf_op jit(solution)/shard_map/ppermute | solution.py:166
  66.0 0.7 copy-start.6
  76.3 11.1 %copy-start.2 = (bf16[64,32,128]{2,1,0:T(8,128)(2,1)}, bf16[64,32,128]{2,1,0:T(8,128)(2,1)S(1)}, u32[]{:S(2)}) copy-start(bf16[64,32,128]{2,1,0:T(8,128)(2,1)S(1)} %collective-permute-done.18.refs_5_) | copy-start | bytes 1572868
  76.3 0.7 copy-start.15
  76.9 10.4 %copy-start.16 = (s32[1,240]{1,0:T(1,128)S(1)}, s32[1,240]{1,0:T(1,128)}, u32[]{:S(2)}) copy-start(s32[1,240]{1,0:T(1,128)} %send_hbm.1) | copy-start | bytes 2884
  79.2 10.4 %collective-permute-start.19 = (bf16[24,128,128]{2,1,0:T(8,128)(2,1)S(1)}, bf16[24,128,128]{2,1,0:T(8,128)(2,1)S(1)}, u32[]{:S(2)}, u32[]{:S(2)}) collective-permute-start(bf16[24,128,128]{2,1,0:T(8,128)(2,1)S(1)} %near1.1), channel_id=1, source_target_pairs={{0,4},{1,5},{2,6},{3,7},{4,0},{5,1},{6,2},{7,3},{8,12},{9,13},{10,... | collective-permute-start | bytes 2359304 | tf_op jit(solution)/shard_map/ppermute | solution.py:181
  92.1 1.6 copy-start.7
  92.1 1.6 copy-start.12
  93.6 35.0 %all-to-all-start.1 = ((bf16[64,128,128]{2,1,0:T(8,128)(2,1)}), bf16[64,128,128]{2,1,0:T(8,128)(2,1)S(1)}, u32[]{:S(2)}, u32[]{:S(2)}) async-start(bf16[64,128,128]{2,1,0:T(8,128)(2,1)} %broadcast_select_fusion), calls=%async_computation.1 | async-start | bytes 4194304 | tf_op jit(solution)/shard_map/all_to_all | solution.py:490
  99.2 1.1 copy-start.1
  100.3 1.0 copy-start.3
  101.4 8.8 %copy-start.17 = (s32[1,240]{1,0:T(1,128)S(1)}, s32[1,240]{1,0:T(1,128)}, u32[]{:S(2)}) copy-start(s32[1,240]{1,0:T(1,128)} %send_hbm.1) | copy-start | bytes 2884
  108.3 1.4 copy-start.4
  109.7 27.1 %collective-permute-start.20 = (bf16[64,128,128]{2,1,0:T(8,128)(2,1)}, bf16[64,128,128]{2,1,0:T(8,128)(2,1)}, u32[]{:S(2)}, u32[]{:S(2)}) collective-permute-start(bf16[64,128,128]{2,1,0:T(8,128)(2,1)} %get-tuple-element.53), channel_id=1, source_target_pairs={{0,4},{1,5},{2,6},{3,7},{4,0},{5,1},{6,2},{7,3},{8,12},{9,13},{10,... | collective-permute-start | bytes 6291464 | tf_op jit(solution)/shard_map/ppermute | solution.py:181
  130.3 0.7 copy-start.11
  131.0 5.8 %copy-start.9 = (s32[560]{0:T(1024)S(1)}, s32[560]{0:T(1024)}, u32[]{:S(2)}) copy-start(s32[560]{0:T(1024)} %from_hbm.7) | copy-start | bytes 6724
  132.1 20.7 %all-to-all-start.2 = ((bf16[32,128,128]{2,1,0:T(8,128)(2,1)}), bf16[32,128,128]{2,1,0:T(8,128)(2,1)S(1)}, u32[]{:S(2)}, u32[]{:S(2)}) async-start(bf16[32,128,128]{2,1,0:T(8,128)(2,1)} %broadcast_select_fusion.1), calls=%async_computation.2 | async-start | bytes 2097152 | tf_op jit(solution)/shard_map/all_to_all | solution.py:490
  136.8 1.6 copy-start.5
  152.8 7.4 %copy-start.10 = (s32[560]{0:T(1024)S(1)}, s32[560]{0:T(1024)}, u32[]{:S(2)}) copy-start(s32[560]{0:T(1024)} %from_hbm.7) | copy-start | bytes 6724
  155.5 14.7 %all-to-all-start.3 = ((bf16[16,128,128]{2,1,0:T(8,128)(2,1)}), bf16[16,128,128]{2,1,0:T(8,128)(2,1)S(1)}, u32[]{:S(2)}, u32[]{:S(2)}) async-start(bf16[16,128,128]{2,1,0:T(8,128)(2,1)} %broadcast_select_fusion.2), calls=%async_computation.3 | async-start | bytes 1048576 | tf_op jit(solution)/shard_map/all_to_all | solution.py:490
  160.2 5.9 %copy-start.13 = (f32[2,128,128]{2,1,0:T(8,128)S(1)}, f32[2,128,128]{2,1,0:T(8,128)}, u32[]{:S(2)}) copy-start(f32[2,128,128]{2,1,0:T(8,128)} %copy-done.12) | copy-start | bytes 393220

commit v8 on v7

--- a/solution.py
+++ b/solution.py
@@ -13,12 +13,12 @@
 KP = 4
 LEVELS = 4
 AXES = ("leaf", "panel")
-LEAF_STEP = 8
+LEAF_STEP = 16
 LAST_STEP = 8
 SIDE = 4
 CUTS = (0, 48, 96, 128)
 ORDERS = ("xzy", "zyx", "yxz")
-VMEM = pltpu.CompilerParams(vmem_limit_bytes=16 * 1024 * 1024)
+VMEM = pltpu.CompilerParams(vmem_limit_bytes=24 * 1024 * 1024)
 
 
 def in_hbm():

time: 177 us -> 176 us (level)
  Pallas kernels: 47 us -> 44.7 us
  waiting for transfers between devices: 50.6 us -> 52.9 us
    all_to_all x3, waiting for transfers between devices: 22.8 us -> 25.2 us  [per_device(): lax.all_to_all(buffer, AXES, 0, 0, axis_index_groups=groups, tiled=True)]
    pallas_call x3, Pallas kernels: 19.1 us -> 16.8 us  [leaf_pass(): pl.pallas_call(kernel, grid_spec=pltpu.PrefetchScalarGridSpec(num_scalar_...]
  transfers between devices with their start and end apart: 24 -> 24, of which waited for: 14 -> 14; matrix products, arithmetic and copies ran while one was open for 1% -> 1% of each run, Pallas kernels for 17% -> 16%
where the time goes in v8:
time: 176 us
  waiting for transfers between devices  52.9 us (30%)
  Pallas kernels  44.7 us (25%)
  starting transfers between devices  36.4 us (21%)
  blocking collectives  28.3 us (16%)
  local copies, waits for them, and re-layouts  7.25 us (4%)
  other arithmetic  4.98 us (3%)
    all_to_all x1, blocking collectives, per_device(): arrived = lax.all_to_all(outgoing, AXES, 0, 0, tiled=True)  28.3 us
    ppermute x18, waiting for transfers between devices, gather_core(): lax.ppermute(part, AXES, step_pairs(order[step // 2], step % 2))  27.7 us
    all_to_all x3, waiting for transfers between devices, per_device(): lax.all_to_all(buffer, AXES, 0, 0, axis_index_groups=groups, tiled=True)  25.2 us
    pallas_call x3, Pallas kernels, leaf_pass(): pl.pallas_call(kernel, grid_spec=pltpu.PrefetchScalarGridSpec(num_scalar_...  16.8 us
    all_to_all x3, starting transfers between devices, per_device(): lax.all_to_all(buffer, AXES, 0, 0, axis_index_groups=groups, tiled=True)  14.9 us
    ppermute x18, starting transfers between devices, gather_core(): lax.ppermute(part, AXES, step_pairs(order[step // 2], step % 2))  12.9 us
    ppermute x3, starting transfers between devices, swap_core(): return lax.ppermute(x, AXES, [(i, i ^ SIDE) for i in range(2 * SIDE ** 3)])  8.65 us
    unnamed x36, local copies, waits for them, and re-layouts  7.22 us
  transfers between devices with their start and end apart: 24, of which 14 were waited for; matrix products, arithmetic and copies ran while one was open for 1% of the time, Pallas kernels for 16%

profile of v8, /device:TPU:1, one launch (start us, length us, event | category | flops | bytes accessed | tf_op | source)
XLA Modules:
  0.0 175.7 jit_solution(2013213618276831369)
XLA Ops:
  0.6 3.1 %pack.1 = bf16[128,8,384]{2,1,0:T(8,128)(2,1)S(1)} custom-call(s32[1,1024]{1,0:T(1,128)} %bitcast.29, s32[1,240]{1,0:T(1,128)} %send_hbm.1, f32[1024,128]{1,0:T(8,128)} %noise_hbm.1), custom_call_target="tpu_custom_call" | custom-call | tf_op jit(solution)/shard_map/pack/pallas_call | solution.py:410
  3.8 28.3 %all_to_all.20.arrived_ref = bf16[128,8,384]{2,1,0:T(8,128)(2,1)S(1)} all-to-all(bf16[128,8,384]{2,1,0:T(8,128)(2,1)S(1)} %pack.1), channel_id=1, replica_groups=mesh['leaf'=32,'panel'=4] {'leaf','panel'}, dimensions={0} | all-to-all | bytes 1572864 | tf_op jit(solution)/shard_map/all_to_all | solution.py:424
  32.0 1.4 first.1
  33.5 0.9 collective-permute-start.13
  34.4 0.3 collective-permute-start.6
  34.7 1.1 collective-permute-start
  35.8 1.5 collective-permute-done.13
  37.4 1.0 collective-permute-done.6
  38.4 0.2 collective-permute-done
  38.6 0.2 collective-permute-start.1
  38.8 2.5 %collective-permute-done.7 = bf16[4,48,128]{2,1,0:T(8,128)(2,1)S(1)} collective-permute-done((bf16[4,48,128]{2,1,0:T(8,128)(2,1)S(1)}, bf16[4,48,128]{2,1,0:T(8,128)(2,1)S(1)}, u32[]{:S(2)}, u32[]{:S(2)}) %collective-permute-start.7) | collective-permute-done | bytes 49184 | tf_op jit(solution)/shard_map/ppermute | solution.py:166
  41.3 1.9 %collective-permute-start.8 = (bf16[8,48,128]{2,1,0:T(8,128)(2,1)S(1)}, bf16[8,48,128]{2,1,0:T(8,128)(2,1)S(1)}, u32[]{:S(2)}, u32[]{:S(2)}) collective-permute-start(bf16[8,48,128]{2,1,0:T(8,128)(2,1)S(1)} %pad_maximum_fusion.11), channel_id=1, source_target_pairs={{0,32},{1,33},{2,34},{3,35},{4,100},{5,101},{6,102},{7,103},{8,40}... | collective-permute-start | bytes 294920 | tf_op jit(solution)/shard_map/ppermute | solution.py:166
  43.3 0.8 collective-permute-start.2
  44.1 2.0 %collective-permute-done.8 = bf16[8,48,128]{2,1,0:T(8,128)(2,1)S(1)} collective-permute-done((bf16[8,48,128]{2,1,0:T(8,128)(2,1)S(1)}, bf16[8,48,128]{2,1,0:T(8,128)(2,1)S(1)}, u32[]{:S(2)}, u32[]{:S(2)}) %collective-permute-start.8) | collective-permute-done | bytes 98336 | tf_op jit(solution)/shard_map/ppermute | solution.py:166
  46.1 0.1 collective-permute-start.9
  46.2 1.8 %collective-permute-done.2 = bf16[8,48,128]{2,1,0:T(8,128)(2,1)S(1)} collective-permute-done((bf16[8,48,128]{2,1,0:T(8,128)(2,1)S(1)}, bf16[8,48,128]{2,1,0:T(8,128)(2,1)S(1)}, u32[]{:S(2)}, u32[]{:S(2)}) %collective-permute-start.2) | collective-permute-done | bytes 98336 | tf_op jit(solution)/shard_map/ppermute | solution.py:166
  48.1 0.1 collective-permute-start.3
  48.2 1.1 collective-permute-start.15
  49.3 1.4 collective-permute-done.9
  50.7 1.4 collective-permute-start.10
  52.1 0.5 collective-permute-done.3
  52.7 1.1 collective-permute-start.4
  53.9 0.1 collective-permute-start.16
  54.0 3.8 %collective-permute-done.16 = bf16[16,32,128]{2,1,0:T(8,128)(2,1)S(1)} collective-permute-done((bf16[16,32,128]{2,1,0:T(8,128)(2,1)S(1)}, bf16[16,32,128]{2,1,0:T(8,128)(2,1)S(1)}, u32[]{:S(2)}, u32[]{:S(2)}) %collective-permute-start.16) | collective-permute-done | bytes 131104 | tf_op jit(solution)/shard_map/ppermute | solution.py:166
  57.8 3.4 %collective-permute-start.17 = (bf16[32,32,128]{2,1,0:T(8,128)(2,1)S(1)}, bf16[32,32,128]{2,1,0:T(8,128)(2,1)S(1)}, u32[]{:S(2)}, u32[]{:S(2)}) collective-permute-start(bf16[32,32,128]{2,1,0:T(8,128)(2,1)S(1)} %pad_maximum_fusion.6), channel_id=1, source_target_pairs={{0,8},{1,9},{2,10},{3,11},{4,28},{5,29},{6,30},{7,31},{8,0},{9,1},... | collective-permute-start | bytes 786440 | tf_op jit(solution)/shard_map/ppermute | solution.py:166
  61.3 0.1 collective-permute-start.11
  61.4 0.1 pad_maximum_fusion.refs_0_
  61.5 0.1 collective-permute-start.5
  61.6 3.4 %collective-permute-done.17 = bf16[32,32,128]{2,1,0:T(8,128)(2,1)S(1)} collective-permute-done((bf16[32,32,128]{2,1,0:T(8,128)(2,1)S(1)}, bf16[32,32,128]{2,1,0:T(8,128)(2,1)S(1)}, u32[]{:S(2)}, u32[]{:S(2)}) %collective-permute-start.17) | collective-permute-done | bytes 262176 | tf_op jit(solution)/shard_map/ppermute | solution.py:166
  65.0 0.1 collective-permute-start.18
  65.2 0.1 pad_add_fusion.at_ref
  65.3 0.7 order.1
  66.0 0.7 copy-done.6
  66.7 9.5 %collective-permute-done.18.refs_5_ = bf16[64,32,128]{2,1,0:T(8,128)(2,1)S(1)} collective-permute-done((bf16[64,32,128]{2,1,0:T(8,128)(2,1)S(1)}, bf16[64,32,128]{2,1,0:T(8,128)(2,1)S(1)}, u32[]{:S(2)}, u32[]{:S(2)}) %collective-permute-start.18) | collective-permute-done | bytes 524320 | tf_op jit(solution)/shard_map/ppermute | solution.py:166
  76.3 0.7 copy-done.15
  76.9 2.3 %near1.1 = bf16[24,128,128]{2,1,0:T(8,128)(2,1)S(1)} custom-call(s32[4]{0:T(128)S(1)} %pad_add_fusion.at_ref, s32[2,1024]{1,0:T(2,128)S(1)} %get-tuple-element.33.picks_ref, s32[560]{0:T(1024)S(1)} %copy-done.15, bf16[64,48,128]{2,1,0:T(8,128)(2,1)S(1)} %pad_maximum_fusion.refs_0_, bf16[64,48,128]{2,1,0:T(8,128)(2,1)} %collective-permute-done.5.refs_1_, ...), custom_call_target="tpu_custom_call" | custom-call | tf_op jit(solution)/shard_map/near1/pallas_call | solution.py:456
  79.2 8.2 %collective-permute-start.19 = (bf16[24,128,128]{2,1,0:T(8,128)(2,1)S(1)}, bf16[24,128,128]{2,1,0:T(8,128)(2,1)S(1)}, u32[]{:S(2)}, u32[]{:S(2)}) collective-permute-start(bf16[24,128,128]{2,1,0:T(8,128)(2,1)S(1)} %near1.1), channel_id=1, source_target_pairs={{0,4},{1,5},{2,6},{3,7},{4,0},{5,1},{6,2},{7,3},{8,12},{9,13},{10,... | collective-permute-start | bytes 2359304 | tf_op jit(solution)/shard_map/ppermute | solution.py:181
  87.4 2.2 %near0.1.own_ref = bf16[24,128,128]{2,1,0:T(8,128)(2,1)S(1)} custom-call(s32[4]{0:T(128)S(1)} %pad_add_fusion.at_ref, s32[2,1024]{1,0:T(2,128)S(1)} %get-tuple-element.33.picks_ref, s32[560]{0:T(1024)S(1)} %copy-done.8, bf16[64,48,128]{2,1,0:T(8,128)(2,1)S(1)} %pad_maximum_fusion.refs_0_, bf16[64,48,128]{2,1,0:T(8,128)(2,1)} %collective-permute-done.5.refs_1_, ...), custom_call_target="tpu_custom_call" | custom-call | tf_op jit(solution)/shard_map/near0/pallas_call | solution.py:456
  89.6 2.4 %level0.1 = (f32[4,128,128]{2,1,0:T(8,128)S(1)}, f32[2,128,128]{2,1,0:T(8,128)S(1)}, bf16[2,128,128]{2,1,0:T(8,128)(2,1)S(1)}) custom-call(s32[560]{0:T(1024)} %from_hbm.7, bf16[560,128,128]{2,1,0:T(8,128)(2,1)} %panels_hbm.7, f32[6,128,128]{2,1,0:T(8,128)} %copy-done.6, f32[40,128,128]{2,1,0:T(8,128)} %diag_hbm.9, s32[4]{0:T(128)S(1)} %pad_add_fusion.at_ref, ...), custom_call_target="tpu_custom_call" | custom-call | tf_op jit(solution)/shard_map/level0/pallas_call | solution.py:528
  92.1 1.5 broadcast_select_fusion
  93.6 5.5 %all-to-all-start.1 = ((bf16[64,128,128]{2,1,0:T(8,128)(2,1)}), bf16[64,128,128]{2,1,0:T(8,128)(2,1)S(1)}, u32[]{:S(2)}, u32[]{:S(2)}) async-start(bf16[64,128,128]{2,1,0:T(8,128)(2,1)} %broadcast_select_fusion), calls=%async_computation.1 | async-start | bytes 4194304 | tf_op jit(solution)/shard_map/all_to_all | solution.py:490
  99.2 1.1 copy-done.1
  100.3 1.0 copy-done.3
  101.4 6.9 %spread.1 = (bf16[64,128,128]{2,1,0:T(8,128)(2,1)S(1)}, bf16[64,128,128]{2,1,0:T(8,128)(2,1)}) custom-call(s32[4]{0:T(128)S(1)} %pad_add_fusion.at_ref, s32[2,1024]{1,0:T(2,128)S(1)} %get-tuple-element.33.picks_ref, bf16[64,48,128]{2,1,0:T(8,128)(2,1)S(1)} %copy-done.1, bf16[64,48,128]{2,1,0:T(8,128)(2,1)} %collective-permute-done.5.refs_1_, ...), custom_call_target="tpu_custom_call" | custom-call | tf_op jit(solution)/shard_map/spread/pallas_call | solution.py:481
  108.3 1.4 copy-done.4
  109.7 0.5 collective-permute-start.20
  110.1 0.1 compare_bitcast_fusion.1
  110.2 18.4 %all-to-all-done.1.received_ref = bf16[64,128,128]{2,1,0:T(8,128)(2,1)S(1)} async-done(((bf16[64,128,128]{2,1,0:T(8,128)(2,1)}), bf16[64,128,128]{2,1,0:T(8,128)(2,1)S(1)}, u32[]{:S(2)}, u32[]{:S(2)}) %all-to-all-start.1) | async-done | bytes 2097184 | tf_op jit(solution)/shard_map/all_to_all | solution.py:490
  128.7 1.7 level1.1
  130.3 0.6 copy-done.11
  131.0 1.1 broadcast_select_fusion.1
  132.1 4.6 %all-to-all-start.2 = ((bf16[32,128,128]{2,1,0:T(8,128)(2,1)}), bf16[32,128,128]{2,1,0:T(8,128)(2,1)S(1)}, u32[]{:S(2)}, u32[]{:S(2)}) async-start(bf16[32,128,128]{2,1,0:T(8,128)(2,1)} %broadcast_select_fusion.1), calls=%async_computation.2 | async-start | bytes 2097152 | tf_op jit(solution)/shard_map/all_to_all | solution.py:490
  136.7 0.1 compare_bitcast_fusion
  136.8 1.6 copy-done.5
  138.4 6.6 %leaf.3.right_ref = f32[32,128,128]{2,1,0:T(8,128)} custom-call(s32[560]{0:T(1024)S(1)} %copy-done.9, s32[4]{0:T(128)S(1)} %pad_add_fusion.at_ref, bf16[64,128,128]{2,1,0:T(8,128)(2,1)S(1)} %copy-done.5, bf16[64,128,128]{2,1,0:T(8,128)(2,1)} %collective-permute-done.20.other_ref, bf16[560,128,128]{2,1,0:T(8,128)(2,1)} %panels_hbm.7, f32[32,128,128]{2,1,0:T(8,128)} %bitcast.26), custom_call_target="tpu_custom_call" | custom-call | tf_op jit(solution)/shard_map/leaf/pallas_call | solution.py:388
  145.1 5.1 %leaf.4.right_ref = f32[32,128,128]{2,1,0:T(8,128)} custom-call(s32[560]{0:T(1024)S(1)} %copy-done.9, bf16[64,128,128]{2,1,0:T(8,128)(2,1)S(1)} %all-to-all-done.1.received_ref, bf16[560,128,128]{2,1,0:T(8,128)(2,1)} %panels_hbm.7, f32[32,128,128]{2,1,0:T(8,128)} %leaf.3.right_ref), custom_call_target="tpu_custom_call" | custom-call | tf_op jit(solution)/shard_map/leaf/pallas_call | solution.py:388
  150.1 2.7 %all-to-all-done.2.received_ref = bf16[32,128,128]{2,1,0:T(8,128)(2,1)S(1)} async-done(((bf16[32,128,128]{2,1,0:T(8,128)(2,1)}), bf16[32,128,128]{2,1,0:T(8,128)(2,1)S(1)}, u32[]{:S(2)}, u32[]{:S(2)}) %all-to-all-start.2) | async-done | bytes 1048608 | tf_op jit(solution)/shard_map/all_to_all | solution.py:490
  152.8 1.8 %level2.1 = (f32[2,128,128]{2,1,0:T(8,128)}, f32[2,128,128]{2,1,0:T(8,128)S(1)}, bf16[2,128,128]{2,1,0:T(8,128)(2,1)S(1)}) custom-call(s32[560]{0:T(1024)} %from_hbm.7, bf16[560,128,128]{2,1,0:T(8,128)(2,1)} %panels_hbm.7, f32[2,128,128]{2,1,0:T(8,128)} %copy-done.11, f32[40,128,128]{2,1,0:T(8,128)} %diag_hbm.9, ...), custom_call_target="tpu_custom_call" | custom-call | tf_op jit(solution)/shard_map/level2/pallas_call | solution.py:528
  154.6 0.9 broadcast_select_fusion.2
  155.5 4.7 %all-to-all-start.3 = ((bf16[16,128,128]{2,1,0:T(8,128)(2,1)}), bf16[16,128,128]{2,1,0:T(8,128)(2,1)S(1)}, u32[]{:S(2)}, u32[]{:S(2)}) async-start(bf16[16,128,128]{2,1,0:T(8,128)(2,1)} %broadcast_select_fusion.2), calls=%async_computation.3 | async-start | bytes 1048576 | tf_op jit(solution)/shard_map/all_to_all | solution.py:490
  160.2 5.1 %leaf.5.right_hbm = f32[32,128,128]{2,1,0:T(8,128)} custom-call(s32[560]{0:T(1024)S(1)} %copy-done.10, bf16[32,128,128]{2,1,0:T(8,128)(2,1)S(1)} %all-to-all-done.2.received_ref, bf16[560,128,128]{2,1,0:T(8,128)(2,1)} %panels_hbm.7, f32[32,128,128]{2,1,0:T(8,128)} %leaf.4.right_ref), custom_call_target="tpu_custom_call" | custom-call | tf_op jit(solution)/shard_map/leaf/pallas_call | solution.py:388
  165.3 0.8 pad_maximum_fusion.3
  166.1 4.1 %all-to-all-done.3.received_ref = bf16[16,128,128]{2,1,0:T(8,128)(2,1)S(1)} async-done(((bf16[16,128,128]{2,1,0:T(8,128)(2,1)}), bf16[16,128,128]{2,1,0:T(8,128)(2,1)S(1)}, u32[]{:S(2)}, u32[]{:S(2)}) %all-to-all-start.3) | async-done | bytes 524320 | tf_op jit(solution)/shard_map/all_to_all | solution.py:490
  170.2 5.3 %last.1 = f32[32,128,128]{2,1,0:T(8,128)} custom-call(s32[560]{0:T(1024)} %from_hbm.7, bf16[16,128,128]{2,1,0:T(8,128)(2,1)S(1)} %all-to-all-done.3.received_ref, bf16[560,128,128]{2,1,0:T(8,128)(2,1)} %panels_hbm.7, f32[32,128,128]{2,1,0:T(8,128)} %leaf.5.right_hbm, f32[40,128,128]{2,1,0:T(8,128)} %diag_hbm.9), custom_call_target="tpu_custom_call" | custom-call | tf_op jit(solution)/shard_map/last/pallas_call | solution.py:550
  (62 shorter events, 0.5 us)
Async XLA Ops:
  32.0 2.4 %copy-start.8 = (s32[560]{0:T(1024)S(1)}, s32[560]{0:T(1024)}, u32[]{:S(2)}) copy-start(s32[560]{0:T(1024)} %from_hbm.7) | copy-start | bytes 6724
  33.5 3.9 %collective-permute-start.13 = (bf16[2,32,128]{2,1,0:T(8,128)(2,1)S(1)}, bf16[2,32,128]{2,1,0:T(8,128)(2,1)S(1)}, u32[]{:S(2)}, u32[]{:S(2)}) collective-permute-start(bf16[2,32,128]{2,1,0:T(8,128)(2,1)S(1)} %slice.41), channel_id=1, source_target_pairs={{0,32},{1,33},{2,34},{3,35},{4,100},{5,101},{6,102},{7,103},{8,40}... | collective-permute-start | bytes 49160 | tf_op jit(solution)/shard_map/ppermute | solution.py:166
  34.4 1.5 collective-permute-start.12
  34.4 3.9 %collective-permute-start.6 = (bf16[2,48,128]{2,1,0:T(8,128)(2,1)S(1)}, bf16[2,48,128]{2,1,0:T(8,128)(2,1)S(1)}, u32[]{:S(2)}, u32[]{:S(2)}) collective-permute-start(bf16[2,48,128]{2,1,0:T(8,128)(2,1)S(1)} %get-tuple-element.66), channel_id=1, source_target_pairs={{0,8},{1,9},{2,10},{3,11},{4,28},{5,29},{6,30},{7,31},{8,0},{9,1},... | collective-permute-start | bytes 73736 | tf_op jit(solution)/shard_map/ppermute | solution.py:166
  34.7 3.9 %collective-permute-start = (bf16[2,48,128]{2,1,0:T(8,128)(2,1)S(1)}, bf16[2,48,128]{2,1,0:T(8,128)(2,1)S(1)}, u32[]{:S(2)}, u32[]{:S(2)}) collective-permute-start(bf16[2,48,128]{2,1,0:T(8,128)(2,1)S(1)} %get-tuple-element.67), channel_id=1, source_target_pairs={{0,1},{1,0},{2,3},{3,2},{4,7},{5,6},{6,5},{7,4},{8,9},{9,8},{10,11... | collective-permute-start | bytes 73736 | tf_op jit(solution)/shard_map/ppermute | solution.py:166
  35.8 25.5 %copy-start.14 = (s32[560]{0:T(1024)}, s32[560]{0:T(1024)S(1)}, u32[]{:S(2)}) copy-start(s32[560]{0:T(1024)S(1)} %collective-permute-done.12.from_ref) | copy-start | bytes 6724
  37.4 10.8 %collective-permute-start.14 = (bf16[4,32,128]{2,1,0:T(8,128)(2,1)S(1)}, bf16[4,32,128]{2,1,0:T(8,128)(2,1)S(1)}, u32[]{:S(2)}, u32[]{:S(2)}) collective-permute-start(bf16[4,32,128]{2,1,0:T(8,128)(2,1)S(1)} %pad_maximum_fusion.15), channel_id=1, source_target_pairs={{0,96},{1,97},{2,98},{3,99},{4,36},{5,37},{6,38},{7,39},{8,104},{9... | collective-permute-start | bytes 98312 | tf_op jit(solution)/shard_map/ppermute | solution.py:166
  38.4 2.9 %collective-permute-start.7 = (bf16[4,48,128]{2,1,0:T(8,128)(2,1)S(1)}, bf16[4,48,128]{2,1,0:T(8,128)(2,1)S(1)}, u32[]{:S(2)}, u32[]{:S(2)}) collective-permute-start(bf16[4,48,128]{2,1,0:T(8,128)(2,1)S(1)} %pad_maximum_fusion.14), channel_id=1, source_target_pairs={{0,24},{1,25},{2,26},{3,27},{4,12},{5,13},{6,14},{7,15},{8,16},{9,... | collective-permute-start | bytes 147464 | tf_op jit(solution)/shard_map/ppermute | solution.py:166
  38.6 4.7 %collective-permute-start.1 = (bf16[4,48,128]{2,1,0:T(8,128)(2,1)S(1)}, bf16[4,48,128]{2,1,0:T(8,128)(2,1)S(1)}, u32[]{:S(2)}, u32[]{:S(2)}) collective-permute-start(bf16[4,48,128]{2,1,0:T(8,128)(2,1)S(1)} %pad_maximum_fusion.13), channel_id=1, source_target_pairs={{0,3},{1,2},{2,1},{3,0},{4,5},{5,4},{6,7},{7,6},{8,11},{9,10},{10,... | collective-permute-start | bytes 147464 | tf_op jit(solution)/shard_map/ppermute | solution.py:166
  41.3 4.8 %collective-permute-start.8 = (bf16[8,48,128]{2,1,0:T(8,128)(2,1)S(1)}, bf16[8,48,128]{2,1,0:T(8,128)(2,1)S(1)}, u32[]{:S(2)}, u32[]{:S(2)}) collective-permute-start(bf16[8,48,128]{2,1,0:T(8,128)(2,1)S(1)} %pad_maximum_fusion.11), channel_id=1, source_target_pairs={{0,32},{1,33},{2,34},{3,35},{4,100},{5,101},{6,102},{7,103},{8,40}... | collective-permute-start | bytes 294920 | tf_op jit(solution)/shard_map/ppermute | solution.py:166
  43.3 4.8 %collective-permute-start.2 = (bf16[8,48,128]{2,1,0:T(8,128)(2,1)S(1)}, bf16[8,48,128]{2,1,0:T(8,128)(2,1)S(1)}, u32[]{:S(2)}, u32[]{:S(2)}) collective-permute-start(bf16[8,48,128]{2,1,0:T(8,128)(2,1)S(1)} %pad_maximum_fusion.10), channel_id=1, source_target_pairs={{0,8},{1,9},{2,10},{3,11},{4,28},{5,29},{6,30},{7,31},{8,0},{9,1},... | collective-permute-start | bytes 294920 | tf_op jit(solution)/shard_map/ppermute | solution.py:166
  46.1 4.6 %collective-permute-start.9 = (bf16[16,48,128]{2,1,0:T(8,128)(2,1)S(1)}, bf16[16,48,128]{2,1,0:T(8,128)(2,1)S(1)}, u32[]{:S(2)}, u32[]{:S(2)}) collective-permute-start(bf16[16,48,128]{2,1,0:T(8,128)(2,1)S(1)} %pad_maximum_fusion.8), channel_id=1, source_target_pairs={{0,96},{1,97},{2,98},{3,99},{4,36},{5,37},{6,38},{7,39},{8,104},{9... | collective-permute-start | bytes 589832 | tf_op jit(solution)/shard_map/ppermute | solution.py:166
  48.1 4.6 %collective-permute-start.3 = (bf16[16,48,128]{2,1,0:T(8,128)(2,1)S(1)}, bf16[16,48,128]{2,1,0:T(8,128)(2,1)S(1)}, u32[]{:S(2)}, u32[]{:S(2)}) collective-permute-start(bf16[16,48,128]{2,1,0:T(8,128)(2,1)S(1)} %pad_maximum_fusion.7), channel_id=1, source_target_pairs={{0,24},{1,25},{2,26},{3,27},{4,12},{5,13},{6,14},{7,15},{8,16},{9,... | collective-permute-start | bytes 589832 | tf_op jit(solution)/shard_map/ppermute | solution.py:166
  48.2 5.7 %collective-permute-start.15 = (bf16[8,32,128]{2,1,0:T(8,128)(2,1)S(1)}, bf16[8,32,128]{2,1,0:T(8,128)(2,1)S(1)}, u32[]{:S(2)}, u32[]{:S(2)}) collective-permute-start(bf16[8,32,128]{2,1,0:T(8,128)(2,1)S(1)} %pad_maximum_fusion.12), channel_id=1, source_target_pairs={{0,1},{1,0},{2,3},{3,2},{4,7},{5,6},{6,5},{7,4},{8,9},{9,8},{10,11... | collective-permute-start | bytes 196616 | tf_op jit(solution)/shard_map/ppermute | solution.py:166
  50.7 10.5 %collective-permute-start.10 = (bf16[32,48,128]{2,1,0:T(8,128)(2,1)S(1)}, bf16[32,48,128]{2,1,0:T(8,128)(2,1)S(1)}, u32[]{:S(2)}, u32[]{:S(2)}) collective-permute-start(bf16[32,48,128]{2,1,0:T(8,128)(2,1)S(1)} %pad_maximum_fusion.5), channel_id=1, source_target_pairs={{0,1},{1,0},{2,3},{3,2},{4,7},{5,6},{6,5},{7,4},{8,9},{9,8},{10,11... | collective-permute-start | bytes 1179656 | tf_op jit(solution)/shard_map/ppermute | solution.py:166
  52.7 8.7 %collective-permute-start.4 = (bf16[32,48,128]{2,1,0:T(8,128)(2,1)S(1)}, bf16[32,48,128]{2,1,0:T(8,128)(2,1)S(1)}, u32[]{:S(2)}, u32[]{:S(2)}) collective-permute-start(bf16[32,48,128]{2,1,0:T(8,128)(2,1)S(1)} %pad_maximum_fusion.4), channel_id=1, source_target_pairs={{0,32},{1,33},{2,34},{3,35},{4,100},{5,101},{6,102},{7,103},{8,40}... | collective-permute-start | bytes 1179656 | tf_op jit(solution)/shard_map/ppermute | solution.py:166
  53.9 3.9 %collective-permute-start.16 = (bf16[16,32,128]{2,1,0:T(8,128)(2,1)S(1)}, bf16[16,32,128]{2,1,0:T(8,128)(2,1)S(1)}, u32[]{:S(2)}, u32[]{:S(2)}) collective-permute-start(bf16[16,32,128]{2,1,0:T(8,128)(2,1)S(1)} %pad_maximum_fusion.9), channel_id=1, source_target_pairs={{0,3},{1,2},{2,1},{3,0},{4,5},{5,4},{6,7},{7,6},{8,11},{9,10},{10,... | collective-permute-start | bytes 393224 | tf_op jit(solution)/shard_map/ppermute | solution.py:166
  57.8 7.2 %collective-permute-start.17 = (bf16[32,32,128]{2,1,0:T(8,128)(2,1)S(1)}, bf16[32,32,128]{2,1,0:T(8,128)(2,1)S(1)}, u32[]{:S(2)}, u32[]{:S(2)}) collective-permute-start(bf16[32,32,128]{2,1,0:T(8,128)(2,1)S(1)} %pad_maximum_fusion.6), channel_id=1, source_target_pairs={{0,8},{1,9},{2,10},{3,11},{4,28},{5,29},{6,30},{7,31},{8,0},{9,1},... | collective-permute-start | bytes 786440 | tf_op jit(solution)/shard_map/ppermute | solution.py:166
  61.3 14.9 %collective-permute-start.11 = (bf16[64,48,128]{2,1,0:T(8,128)(2,1)S(1)}, bf16[64,48,128]{2,1,0:T(8,128)(2,1)}, u32[]{:S(2)}, u32[]{:S(2)}) collective-permute-start(bf16[64,48,128]{2,1,0:T(8,128)(2,1)S(1)} %pad_maximum_fusion.1.refs_2_), channel_id=1, source_target_pairs={{0,3},{1,2},{2,1},{3,0},{4,5},{5,4},{6,7},{7,6},{8,11},{9,10},{10,... | collective-permute-start | bytes 2359304 | tf_op jit(solution)/shard_map/ppermute | solution.py:166
  61.5 25.9 %copy-start = (bf16[64,48,128]{2,1,0:T(8,128)(2,1)}, bf16[64,48,128]{2,1,0:T(8,128)(2,1)S(1)}, u32[]{:S(2)}) copy-start(bf16[64,48,128]{2,1,0:T(8,128)(2,1)S(1)} %pad_maximum_fusion.refs_0_) | copy-start | bytes 2359300
  61.5 14.8 %collective-permute-start.5 = (bf16[64,48,128]{2,1,0:T(8,128)(2,1)S(1)}, bf16[64,48,128]{2,1,0:T(8,128)(2,1)}, u32[]{:S(2)}, u32[]{:S(2)}) collective-permute-start(bf16[64,48,128]{2,1,0:T(8,128)(2,1)S(1)} %pad_maximum_fusion.refs_0_), channel_id=1, source_target_pairs={{0,96},{1,97},{2,98},{3,99},{4,36},{5,37},{6,38},{7,39},{8,104},{9... | collective-permute-start | bytes 2359304 | tf_op jit(solution)/shard_map/ppermute | solution.py:166
  65.0 11.2 %collective-permute-start.18 = (bf16[64,32,128]{2,1,0:T(8,128)(2,1)S(1)}, bf16[64,32,128]{2,1,0:T(8,128)(2,1)S(1)}, u32[]{:S(2)}, u32[]{:S(2)}) collective-permute-start(bf16[64,32,128]{2,1,0:T(8,128)(2,1)S(1)} %pad_maximum_fusion.2.refs_4_), channel_id=1, source_target_pairs={{0,24},{1,25},{2,26},{3,27},{4,12},{5,13},{6,14},{7,15},{8,16},{9,... | collective-permute-start | bytes 1572872 | tf_op jit(solution)/shard_map/ppermute | solution.py:166
  66.0 0.7 copy-start.6
  76.3 11.1 %copy-start.2 = (bf16[64,32,128]{2,1,0:T(8,128)(2,1)}, bf16[64,32,128]{2,1,0:T(8,128)(2,1)S(1)}, u32[]{:S(2)}) copy-start(bf16[64,32,128]{2,1,0:T(8,128)(2,1)S(1)} %collective-permute-done.18.refs_5_) | copy-start | bytes 1572868
  76.3 0.7 copy-start.15
  76.9 10.4 %copy-start.16 = (s32[1,240]{1,0:T(1,128)S(1)}, s32[1,240]{1,0:T(1,128)}, u32[]{:S(2)}) copy-start(s32[1,240]{1,0:T(1,128)} %send_hbm.1) | copy-start | bytes 2884
  79.2 10.4 %collective-permute-start.19 = (bf16[24,128,128]{2,1,0:T(8,128)(2,1)S(1)}, bf16[24,128,128]{2,1,0:T(8,128)(2,1)S(1)}, u32[]{:S(2)}, u32[]{:S(2)}) collective-permute-start(bf16[24,128,128]{2,1,0:T(8,128)(2,1)S(1)} %near1.1), channel_id=1, source_target_pairs={{0,4},{1,5},{2,6},{3,7},{4,0},{5,1},{6,2},{7,3},{8,12},{9,13},{10,... | collective-permute-start | bytes 2359304 | tf_op jit(solution)/shard_map/ppermute | solution.py:181
  92.1 1.6 copy-start.7
  92.1 1.6 copy-start.12
  93.6 35.0 %all-to-all-start.1 = ((bf16[64,128,128]{2,1,0:T(8,128)(2,1)}), bf16[64,128,128]{2,1,0:T(8,128)(2,1)S(1)}, u32[]{:S(2)}, u32[]{:S(2)}) async-start(bf16[64,128,128]{2,1,0:T(8,128)(2,1)} %broadcast_select_fusion), calls=%async_computation.1 | async-start | bytes 4194304 | tf_op jit(solution)/shard_map/all_to_all | solution.py:490
  99.2 1.1 copy-start.1
  100.3 1.0 copy-start.3
  101.4 8.8 %copy-start.17 = (s32[1,240]{1,0:T(1,128)S(1)}, s32[1,240]{1,0:T(1,128)}, u32[]{:S(2)}) copy-start(s32[1,240]{1,0:T(1,128)} %send_hbm.1) | copy-start | bytes 2884
  108.3 1.4 copy-start.4
  109.7 27.1 %collective-permute-start.20 = (bf16[64,128,128]{2,1,0:T(8,128)(2,1)}, bf16[64,128,128]{2,1,0:T(8,128)(2,1)}, u32[]{:S(2)}, u32[]{:S(2)}) collective-permute-start(bf16[64,128,128]{2,1,0:T(8,128)(2,1)} %get-tuple-element.53), channel_id=1, source_target_pairs={{0,4},{1,5},{2,6},{3,7},{4,0},{5,1},{6,2},{7,3},{8,12},{9,13},{10,... | collective-permute-start | bytes 6291464 | tf_op jit(solution)/shard_map/ppermute | solution.py:181
  130.3 0.7 copy-start.11
  131.0 5.8 %copy-start.9 = (s32[560]{0:T(1024)S(1)}, s32[560]{0:T(1024)}, u32[]{:S(2)}) copy-start(s32[560]{0:T(1024)} %from_hbm.7) | copy-start | bytes 6724
  132.1 20.7 %all-to-all-start.2 = ((bf16[32,128,128]{2,1,0:T(8,128)(2,1)}), bf16[32,128,128]{2,1,0:T(8,128)(2,1)S(1)}, u32[]{:S(2)}, u32[]{:S(2)}) async-start(bf16[32,128,128]{2,1,0:T(8,128)(2,1)} %broadcast_select_fusion.1), calls=%async_computation.2 | async-start | bytes 2097152 | tf_op jit(solution)/shard_map/all_to_all | solution.py:490
  136.8 1.6 copy-start.5
  152.8 7.4 %copy-start.10 = (s32[560]{0:T(1024)S(1)}, s32[560]{0:T(1024)}, u32[]{:S(2)}) copy-start(s32[560]{0:T(1024)} %from_hbm.7) | copy-start | bytes 6724
  155.5 14.7 %all-to-all-start.3 = ((bf16[16,128,128]{2,1,0:T(8,128)(2,1)}), bf16[16,128,128]{2,1,0:T(8,128)(2,1)S(1)}, u32[]{:S(2)}, u32[]{:S(2)}) async-start(bf16[16,128,128]{2,1,0:T(8,128)(2,1)} %broadcast_select_fusion.2), calls=%async_computation.3 | async-start | bytes 1048576 | tf_op jit(solution)/shard_map/all_to_all | solution.py:490
  160.2 5.1 %copy-start.13 = (f32[2,128,128]{2,1,0:T(8,128)S(1)}, f32[2,128,128]{2,1,0:T(8,128)}, u32[]{:S(2)}) copy-start(f32[2,128,128]{2,1,0:T(8,128)} %copy-done.12) | copy-start | bytes 393220
